TPU v7x, 32 devices: a whole 2x2x4 slice. The times are simulated.
32 devices in a mesh: grp: 2 (over y), ccd: 4 (over z), row: 2 (over x), amp: 2 (over core).
Axes of the slice: x: 2, y: 2, z: 4, core: 2. Of those that a mesh axis runs over, the one named last changes fastest.
Arguments:
- science: float32 [8, 512, 1024], P(('grp', 'ccd'), 'row', 'amp'), parts along dimension 0, may hold values from -6 to 6
- template: bfloat16 [8, 2, 2, 8, 32, 512], P(('grp', 'ccd'), 'row', 'amp'), parts along dimension 0, may hold values from -6 to 6
- owners: int32 [8, 2, 2, 8, 1], P(('grp', 'ccd'), 'row', 'amp'), parts along dimension 0, may hold values from 0 to 3; in each aligned block of 8 rows (0 to 7, 8 to 15, ..., all dimensions but the last counted through in order) at most 2 rows name the same one
- patch_strip: int32 [8, 2, 2, 8], P(('grp', 'ccd'), 'row', 'amp'), parts along dimension 0, may hold values from 0 to 7
- shifts: int32 [8, 2, 2, 2, 8], P(('grp', 'ccd'), 'row', 'amp'), parts along dimension 0, may hold values from -3 to 3
- fractions: float32 [8, 2, 2, 2, 8], P(('grp', 'ccd'), 'row', 'amp'), parts along dimension 0, may hold values from 0.05 to 0.95
- coefs: float32 [8, 3, 9], P(('grp', 'ccd')), parts along dimension 0, may hold values from -3 to 3
Outputs:
- difference: float32 [8, 512, 1024], P(('grp', 'ccd'), 'row', 'amp'), parts along dimension 0
- stack: float32 [8, 2, 2, 8, 32, 512], P(('grp', 'ccd'), 'row', 'amp'), parts along dimension 0
There are 2 independent parts, one for each index of `grp`. A program takes and returns all parts, laid end to end along the dimension named above; each array names one. Nothing has to cross between parts.
Inputs may be any that keep to these rules, and one draw needn't show every extreme that they name: Among the 8 strips of one device's block no owner is named more than 2 times, and some block names one owner exactly 2 times in every draw; owners lie in the same row band and column half as the block.
All inputs are finite; a program needn't handle non-finite values.
Results may differ from a plain program's by a relative error of at most 0.0057.
Values may be sent and summed in bfloat16 or wider, within the bound.
No kernel may reach another device: no remote copies, remote signals or barrier semaphores. Data moves between devices by JAX's collectives and lax.ppermute only.
A program may use at most 64 MiB of HBM per device.

v0:
```python
import functools

import jax
import jax.numpy as jnp
import ml_dtypes
import numpy as np
from jax import lax
from jax.experimental import pallas as pl
from jax.experimental.pallas import tpu as pltpu
from jax.sharding import PartitionSpec as P

RADIUS = 9
LANES = 128
HALF_TILE = 64
MARGIN = 16
TAPS = 6
KINDS = 3

F32 = jnp.float32
BF16 = jnp.bfloat16
SMEM = pl.BlockSpec(memory_space=pltpu.SMEM)
VMEM = pl.BlockSpec(memory_space=pltpu.VMEM)


def kernel_table():
    support = np.arange(-RADIUS, RADIUS + 1).astype(np.float32)
    narrow = np.exp(-support * support / np.float32(4.5))
    slope = support * np.exp(-support * support / np.float32(12.5))
    broad = np.exp(-support * support / np.float32(40.5))
    table = np.stack([narrow / narrow.sum(), slope / np.abs(slope).sum(), broad / broad.sum()])
    return table.astype(ml_dtypes.bfloat16)


def column_bands():
    table = kernel_table()
    source = np.arange(2 * LANES)[:, None]
    target = np.arange(LANES)[None, :]
    place = source - HALF_TILE - target + RADIUS
    inside = (place >= 0) & (place <= 2 * RADIUS)
    return np.stack(
        [np.where(inside, row[np.clip(place, 0, 2 * RADIUS)], 0) for row in table]
    ).astype(ml_dtypes.bfloat16)


def row_bands(count):
    table = kernel_table()
    source = np.arange(count + 2 * MARGIN)[None, :]
    target = np.arange(count)[:, None]
    place = source - MARGIN - target + RADIUS
    inside = (place >= 0) & (place <= 2 * RADIUS)
    return np.concatenate(
        [np.where(inside, row[np.clip(place, 0, 2 * RADIUS)], 0) for row in table]
    ).astype(ml_dtypes.bfloat16)


def lanczos_taps(fraction):
    offsets = jnp.arange(-2, 4).astype(F32)
    spread = offsets[None, :] - fraction[:, None]
    return (jnp.sinc(spread) * jnp.sinc(spread / 3.0)).astype(BF16)


def lane_index(rows):
    return lax.broadcasted_iota(jnp.int32, (rows, LANES), 1)


def partner_of(me, group, xor):
    return me ^ group if xor else group


def matches(code_ref, group, me, strips, capacity):
    found, count = [jnp.int32(0)] * capacity, jnp.int32(0)
    for q in range(strips):
        code = code_ref[group * strips + q] if group is not None else code_ref[q]
        hit = lax.div(code, jnp.int32(strips)) == me
        strip = lax.rem(code, jnp.int32(strips))
        found = [jnp.where(hit & (count == j), strip, f) for j, f in enumerate(found)]
        count = count + hit.astype(jnp.int32)
    return found, count


def slots_of(code_ref, me, strips, capacity, xor):
    owners = [lax.div(code_ref[q], jnp.int32(strips)) for q in range(strips)]
    slots = []
    for q in range(strips):
        rank = jnp.int32(0)
        for p in range(q):
            rank = rank + (owners[p] == owners[q]).astype(jnp.int32)
        slots.append(partner_of(me, owners[q], xor) * capacity + rank)
    return slots


def pick_kernel(n, capacity, strips, xor, *refs):
    codes, template, outs = refs[:-2] if xor else refs[:1], None, None
    if xor:
        codes, template, outs = refs[:n], refs[n], refs[n + 1 :]
    else:
        codes, template, outs = [refs[0]] * n, refs[1], refs[2:]
    me = lax.axis_index("ccd")
    for g in range(n):
        found, _ = matches(codes[g], None if xor else g, me, strips, capacity)
        for j in range(capacity):
            if xor:
                outs[g][j] = template[found[j]]
            else:
                outs[0][g * capacity + j] = template[found[j]]


def prepare_kernel(strips, strip_rows, tiles, amp_count, coefs, taps, shifts, bands, de, forward, mid, edge):
    amp = lax.axis_index("amp")
    width = tiles * LANES
    for first in range(KINDS):
        for tile in range(tiles):
            column = lane_index(1) + (amp * width + tile * LANES)
            px = (column.astype(F32) + 0.5) / (width * amp_count) * 2.0 - 1.0
            for half in range(2):
                rows = pl.ds(half * LANES, LANES)
                d = jnp.zeros((LANES, LANES), F32)
                e = jnp.zeros((LANES, LANES), F32)
                for second in range(KINDS):
                    basis = first * KINDS + second
                    band = bands[second, rows, :].astype(F32)
                    d = d + band * (coefs[basis] + coefs[9 + basis] * px)
                    e = e + band * coefs[18 + basis]
                at = pl.ds(half * KINDS * LANES + first * LANES, LANES)
                de[tile, at, 0:LANES] = d.astype(BF16)
                de[tile, at, LANES : 2 * LANES] = e.astype(BF16)

    def operator(out, chosen, transposed):
        size = out.shape[1]
        lane = lax.broadcasted_iota(jnp.int32, (strip_rows, size), 1)
        row = lax.broadcasted_iota(jnp.int32, (strip_rows, size), 0)
        for place, q in enumerate(chosen):
            low = place * strip_rows
            within = (lane >= low) & (lane < low + strip_rows)
            step = lane - low - row
            offset = (-step if transposed else step) - shifts[q]
            offset = jnp.where(within, offset, jnp.int32(1 << 20))
            value = jnp.zeros((strip_rows, size), F32)
            for t in range(TAPS):
                value = jnp.where(offset == t - 2, taps[q * TAPS + t], value)
            out[pl.ds(low, strip_rows), :] = value.astype(BF16)

    operator(forward, range(strips), False)
    operator(mid, range(1, strips - 1), True)
    operator(edge, (0, strips - 1), True)


def warp_kernel(n, capacity, strips, strip_rows, tiles, xor, paired, *refs):
    code, shifts, taps, forward = refs[:4]
    if xor:
        received, rest = refs[4 : 4 + n], refs[4 + n :]
    else:
        received, rest = refs[4:5], refs[5:]
    if paired:
        image, send_row, send_amp, send_diag, pool, fetched, rows_done = rest
    else:
        image, pool, fetched, rows_done = rest
    me = lax.axis_index("ccd")
    if xor:
        for g in range(n):
            pool[pl.ds(g * capacity, capacity)] = received[g][...]
    else:
        pool[...] = received[0][...]
    for q, slot in enumerate(slots_of(code, me, strips, capacity, xor)):
        fetched[pl.ds(q * strip_rows, strip_rows), :] = pool[slot]
    rows_done[...] = jnp.dot(forward[...], fetched[...], preferred_element_type=F32).astype(BF16).astype(F32)
    lane = lane_index(strip_rows)
    for q in range(strips):
        rows = pl.ds(q * strip_rows, strip_rows)
        source = [rows_done[rows, pl.ds(b * LANES, LANES)] for b in range(tiles)]
        total = [jnp.zeros((strip_rows, LANES), F32)] * (tiles + 1)
        for t in range(TAPS):
            amount = HALF_TILE - (shifts[strips + q] + (t - 2))
            tap = taps[(strips + q) * TAPS + t]
            spill = lane < amount
            before = None
            for b in range(tiles + 1):
                here = pltpu.roll(source[b], amount, 1) * tap if b < tiles else None
                if before is None:
                    value = jnp.where(spill, 0.0, here)
                elif here is None:
                    value = jnp.where(spill, before, 0.0)
                else:
                    value = jnp.where(spill, before, here)
                total[b] = total[b] + value
                before = here
        total[0] = jnp.where(lane < HALF_TILE, 0.0, total[0])
        total[tiles] = jnp.where(lane < HALF_TILE, total[tiles], 0.0)
        for b in range(tiles + 1):
            image[rows, pl.ds(b * LANES, LANES)] = total[b].astype(BF16)
    if paired:
        band = strips * strip_rows
        row_first = lax.axis_index("row") == 0
        amp_first = lax.axis_index("amp") == 0
        edge_rows = jnp.where(row_first, image[band - MARGIN : band, :], image[0:MARGIN, :])
        send_row[...] = edge_rows
        send_amp[...] = jnp.where(amp_first, image[:, tiles * LANES :], image[:, 0:LANES])
        send_diag[...] = jnp.where(amp_first, edge_rows[:, tiles * LANES :], edge_rows[:, 0:LANES])


def joined(ref, rows, left, right, tiles, amp_count):
    amp = lax.axis_index("amp")
    zero = jnp.zeros((), BF16)
    first = ref[rows, 0:LANES] + jnp.where(amp > 0, left, zero)
    last = ref[rows, tiles * LANES :] + jnp.where(amp < amp_count - 1, right, zero)
    return [first] + [ref[rows, b * LANES : (b + 1) * LANES] for b in range(1, tiles)] + [last]


def row_convolved(bands, parts, across, at, count):
    for low in range(0, len(parts), 2):
        window = jnp.concatenate(parts[low : low + 2], axis=1)
        result = jnp.dot(bands, window, preferred_element_type=F32)
        for b in range(low, min(low + 2, len(parts))):
            for kind in range(KINDS):
                piece = result[kind * count : (kind + 1) * count, (b - low) * LANES : (b - low + 1) * LANES]
                across[at : at + count, (b * KINDS + kind) * LANES : (b * KINDS + kind + 1) * LANES] = piece.astype(BF16)


def columns_returned(lowered, columns, at, strips, q, strip_rows, tiles, shifts, taps):
    lane = lane_index(strip_rows)
    rows = slice(at, at + strip_rows)
    source = [lowered[rows, b * LANES : (b + 1) * LANES] for b in range(tiles)]
    total = [jnp.zeros((strip_rows, LANES), F32)] * tiles
    for t in range(TAPS):
        amount = shifts[strips + q] + (t - 2)
        tap = taps[(strips + q) * TAPS + t]
        turn = jnp.where(amount < 0, amount + LANES, amount)
        low, high = lane < amount, lane >= LANES + amount
        moved = [pltpu.roll(s, turn, 1) * tap for s in source]
        for b in range(tiles):
            value = jnp.where(low, moved[b - 1] if b > 0 else 0.0, moved[b])
            value = jnp.where(high, moved[b + 1] if b < tiles - 1 else 0.0, value)
            total[b] = total[b] + value
    for b in range(tiles):
        columns[rows, b * LANES : (b + 1) * LANES] = total[b].astype(BF16)


def subtracted(science, across, de, store, count, tiles, place):
    for b in range(tiles):
        acc = jnp.dot(
            across[:, b * KINDS * LANES : (b + 2) * KINDS * LANES], de[b], preferred_element_type=F32
        )
        store(b, science(b) - (acc[:, 0:LANES] + place * acc[:, LANES:]))


def row_place(first, count, band, row_count):
    row = lax.broadcasted_iota(jnp.int32, (count, LANES), 0) + (lax.axis_index("row") * band + first)
    return (row.astype(F32) + 0.5) / (band * row_count) * 2.0 - 1.0


def mid_kernel(strips, strip_rows, tiles, row_count, amp_count, image, left, right, science, de, bands, operator,
               shifts, taps, diff, contribution, across, lowered, columns):
    band = strips * strip_rows
    count = band - 2 * strip_rows
    rows = slice(strip_rows - MARGIN, band - strip_rows + MARGIN)
    parts = joined(image, rows, left[rows, :], right[rows, :], tiles, amp_count)
    row_convolved(bands[...], parts, across, 0, count)

    def store(b, value):
        diff[:, b * LANES : (b + 1) * LANES] = value
        lowered[:, b * LANES : (b + 1) * LANES] = value.astype(BF16).astype(F32)

    subtracted(
        lambda b: science[strip_rows : strip_rows + count, b * LANES : (b + 1) * LANES],
        across, de, store, count, tiles, row_place(strip_rows, count, band, row_count),
    )
    for q in range(1, strips - 1):
        columns_returned(lowered, columns, (q - 1) * strip_rows, strips, q, strip_rows, tiles, shifts, taps)
    contribution[...] = jnp.dot(operator[...], columns[...], preferred_element_type=F32).astype(BF16)


def edge_kernel(n, capacity, strips, strip_rows, tiles, row_count, amp_count, xor, image, left, right, top, bottom,
                top_left, top_right, bottom_left, bottom_right, science, de, bands, operator, shifts, taps, code,
                diff_mid, contribution_mid, diff, *rest):
    outs = rest[: n if xor else 1]
    across, lowered, columns, pool = rest[len(outs) :]
    band = strips * strip_rows
    inner = strip_rows + MARGIN
    row = lax.axis_index("row")
    zero = jnp.zeros((), BF16)
    everything = slice(0, MARGIN)
    above = [jnp.where(row > 0, part, zero)
             for part in joined(top, everything, top_left[...], top_right[...], tiles, amp_count)]
    below = [jnp.where(row < row_count - 1, part, zero)
             for part in joined(bottom, everything, bottom_left[...], bottom_right[...], tiles, amp_count)]
    first, last = slice(0, inner), slice(band - inner, band)
    upper = joined(image, first, left[first, :], right[first, :], tiles, amp_count)
    lower = joined(image, last, left[last, :], right[last, :], tiles, amp_count)
    row_convolved(bands[...], [jnp.concatenate(p, axis=0) for p in zip(above, upper)], across, 0, strip_rows)
    row_convolved(bands[...], [jnp.concatenate(p, axis=0) for p in zip(lower, below)], across, strip_rows, strip_rows)

    def store(b, value):
        at = slice(b * LANES, (b + 1) * LANES)
        diff[0:strip_rows, at] = value[0:strip_rows]
        diff[band - strip_rows : band, at] = value[strip_rows:]
        lowered[:, at] = value.astype(BF16).astype(F32)

    def edge_science(b):
        at = slice(b * LANES, (b + 1) * LANES)
        return jnp.concatenate([science[0:strip_rows, at], science[band - strip_rows : band, at]], axis=0)

    place = jnp.concatenate([row_place(0, strip_rows, band, row_count),
                             row_place(band - strip_rows, strip_rows, band, row_count)], axis=0)
    subtracted(edge_science, across, de, store, 2 * strip_rows, tiles, place)
    diff[strip_rows : band - strip_rows, :] = diff_mid[...]
    columns_returned(lowered, columns, 0, strips, 0, strip_rows, tiles, shifts, taps)
    columns_returned(lowered, columns, strip_rows, strips, strips - 1, strip_rows, tiles, shifts, taps)
    ends = jnp.dot(operator[...], columns[...], preferred_element_type=F32).astype(BF16)
    me = lax.axis_index("ccd")
    target = pool if xor else outs[0]
    if n * capacity != strips:
        target[...] = jnp.zeros(target.shape, BF16)
    for q, slot in enumerate(slots_of(code, me, strips, capacity, xor)):
        if q == 0:
            target[slot] = ends[0:strip_rows]
        elif q == strips - 1:
            target[slot] = ends[strip_rows:]
        else:
            target[slot] = contribution_mid[(q - 1) * strip_rows : q * strip_rows, :]
    if xor:
        for g in range(n):
            outs[g][...] = pool[pl.ds(g * capacity, capacity)]


def sum_kernel(n, capacity, strips, xor, *refs):
    if xor:
        codes, returned, stack = refs[:n], refs[n : 2 * n], refs[2 * n]
    else:
        codes, returned, stack = [refs[0]] * n, [refs[1]] * n, refs[2]
    me = lax.axis_index("ccd")
    stack[...] = jnp.zeros(stack.shape, F32)
    for g in range(n):
        found, count = matches(codes[g], None if xor else g, me, strips, capacity)
        for j in range(capacity):

            @pl.when(count > j)
            def _(g=g, j=j, strip=found[j]):
                at = j if xor else g * capacity + j
                stack[strip] += returned[g][at].astype(F32)


def body(science, template, owners, patch_strip, shifts, fractions, coefs):
    n = lax.axis_size("ccd")
    row_count = lax.axis_size("row")
    amp_count = lax.axis_size("amp")
    band, width = science.shape[1:]
    strips, strip_rows = template.shape[3:5]
    capacity = max(2, strips // n)
    tiles = width // LANES
    padded = width + LANES
    xor = n in (2, 4)
    paired = row_count == 2 and amp_count == 2
    swap = [(0, 1), (1, 0)]
    strip_shape = (capacity, strip_rows, width)

    def call(kernel, out_shape, operands, spaces, scratch=(), megabytes=8, flops=0):
        return pl.pallas_call(
            kernel,
            out_shape=[jax.ShapeDtypeStruct(s, d) for s, d in out_shape],
            in_specs=list(spaces),
            out_specs=[VMEM] * len(out_shape),
            scratch_shapes=[pltpu.VMEM(s, d) for s, d in scratch],
            compiler_params=pltpu.CompilerParams(vmem_limit_bytes=megabytes << 20),
            cost_estimate=pl.CostEstimate(flops=flops, bytes_accessed=1 << 20, transcendentals=0),
        )(*operands)

    def exchange(parts):
        if not xor:
            return [lax.all_to_all(parts[0], "ccd", split_axis=0, concat_axis=0, tiled=True)]
        return [parts[0]] + [
            lax.ppermute(parts[g], "ccd", [(i, i ^ g) for i in range(n)]) for g in range(1, n)
        ]

    code = owners.reshape(strips) * strips + patch_strip.reshape(strips)
    if xor:
        codes = [code] + [lax.ppermute(code, "ccd", [(i, i ^ g) for i in range(n)]) for g in range(1, n)]
        picked_shapes = [(strip_shape, BF16)] * n
    else:
        codes = [lax.all_gather(code, "ccd", axis=0, tiled=True)]
        picked_shapes = [((n * capacity, strip_rows, width), BF16)]
    shift_list = shifts.reshape(2 * strips)
    taps = lanczos_taps(fractions.reshape(2 * strips)).astype(F32).reshape(2 * strips * TAPS)
    science = science.reshape(band, width)
    template_strips = template.reshape(strips, strip_rows, width)

    picked = call(
        functools.partial(pick_kernel, n, capacity, strips, xor),
        picked_shapes,
        [*codes, template_strips],
        [SMEM] * len(codes) + [VMEM],
    )
    mid_rows = band - 2 * strip_rows
    de, forward, mid_operator, edge_operator = call(
        functools.partial(prepare_kernel, strips, strip_rows, tiles, amp_count),
        [
            ((tiles, 2 * KINDS * LANES, 2 * LANES), BF16),
            ((band, band), BF16),
            ((mid_rows, mid_rows), BF16),
            ((2 * strip_rows, 2 * strip_rows), BF16),
        ],
        [coefs.reshape(27), taps, shift_list, jnp.asarray(column_bands())],
        [SMEM, SMEM, SMEM, VMEM],
    )
    received = exchange(picked)
    image_shape = ((band, padded), BF16)
    halo_shapes = [((MARGIN, padded), BF16), ((band, LANES), BF16), ((MARGIN, LANES), BF16)]
    warped = call(
        functools.partial(warp_kernel, n, capacity, strips, strip_rows, tiles, xor, paired),
        [image_shape] + (halo_shapes if paired else []),
        [code, shift_list, taps, forward, *received],
        [SMEM, SMEM, SMEM, VMEM] + [VMEM] * len(received),
        [((n * capacity, strip_rows, width), BF16), ((band, width), BF16), ((band, width), F32)],
    )
    image = warped[0]
    if paired:
        side = lax.ppermute(warped[2], "amp", swap)
        ends = lax.ppermute(warped[1], "row", swap)
        corner = lax.ppermute(warped[3], ("row", "amp"), [(0, 3), (3, 0), (1, 2), (2, 1)])
        left = right = side
        top = bottom = ends
        top_left = top_right = bottom_left = bottom_right = corner
    else:
        first, last = image[:MARGIN], image[band - MARGIN :]

        def moved(value, down, along):
            pairs = []
            for r in range(row_count):
                for a in range(amp_count):
                    if 0 <= r + down < row_count and 0 <= a + along < amp_count:
                        pairs.append((r * amp_count + a, (r + down) * amp_count + a + along))
            return lax.ppermute(value, ("row", "amp"), pairs)

        left = moved(image[:, padded - LANES :], 0, 1)
        right = moved(image[:, :LANES], 0, -1)
        top, bottom = moved(last, 1, 0), moved(first, -1, 0)
        top_left = moved(last[:, padded - LANES :], 1, 1)
        top_right = moved(last[:, :LANES], 1, -1)
        bottom_left = moved(first[:, padded - LANES :], -1, 1)
        bottom_right = moved(first[:, :LANES], -1, -1)

    diff_mid, contribution_mid = call(
        functools.partial(mid_kernel, strips, strip_rows, tiles, row_count, amp_count),
        [((mid_rows, width), F32), ((mid_rows, width), BF16)],
        [image, left, right, science, de, jnp.asarray(row_bands(mid_rows)), mid_operator, shift_list, taps],
        [VMEM] * 7 + [SMEM] * 2,
        [((mid_rows, (tiles + 1) * KINDS * LANES), BF16), ((mid_rows, width), F32), ((mid_rows, width), BF16)],
        megabytes=12,
    )
    outgoing_shapes = picked_shapes
    difference, *outgoing = call(
        functools.partial(edge_kernel, n, capacity, strips, strip_rows, tiles, row_count, amp_count, xor),
        [((band, width), F32)] + outgoing_shapes,
        [image, left, right, top, bottom, top_left, top_right, bottom_left, bottom_right, science, de,
         jnp.asarray(row_bands(strip_rows)), edge_operator, shift_list, taps, code, diff_mid, contribution_mid],
        [VMEM] * 13 + [SMEM] * 3 + [VMEM] * 2,
        [((2 * strip_rows, (tiles + 1) * KINDS * LANES), BF16), ((2 * strip_rows, width), F32),
         ((2 * strip_rows, width), BF16), ((n * capacity, strip_rows, width), BF16)],
        megabytes=12,
    )
    returned = exchange(outgoing)
    (stack,) = call(
        functools.partial(sum_kernel, n, capacity, strips, xor),
        [((strips, strip_rows, width), F32)],
        [*codes, *returned],
        [SMEM] * len(codes) + [VMEM] * len(returned),
    )
    return difference[None], stack.reshape(template.shape)


def solution(mesh):
    return jax.shard_map(
        body,
        mesh=mesh,
        in_specs=(
            P(("grp", "ccd"), "row", "amp"),
            P(("grp", "ccd"), "row", "amp", None, None, None),
            P(("grp", "ccd"), "row", "amp", None, None),
            P(("grp", "ccd"), "row", "amp", None),
            P(("grp", "ccd"), "row", "amp", None, None),
            P(("grp", "ccd"), "row", "amp", None, None),
            P(("grp", "ccd"), None, None),
        ),
        out_specs=(
            P(("grp", "ccd"), "row", "amp"),
            P(("grp", "ccd"), "row", "amp", None, None, None),
        ),
        check_vma=False,
    )
```

profile of v0, /device:TPU:0, one launch (start us, length us, event | category | flops | bytes accessed | tf_op | source)
XLA Modules:
  0.0 41.1 jit_solution(12810539874121415391)
XLA Ops:
  0.6 0.7 %bitcast_add_fusion.refs_0_.code = s32[8]{0:T(128)S(1)} fusion(s32[1,1,1,8]{3,2,1,0:T(1,128)} %param.14, s32[1,1,1,8,1]{3,4,2,1,0:T(1,128)} %param.13), kind=kLoop, calls=%fused_computation.59 | loop fusion | flops 16 | bytes 96 | tf_op jit(solution)/shard_map/add | solution.py:374
  1.3 5.0 %collective-permute-start.2 = (s32[8]{0:T(128)S(1)}, s32[8]{0:T(128)S(1)}, u32[]{:S(2)}, u32[]{:S(2)}) collective-permute-start(s32[8]{0:T(128)S(1)} %bitcast_add_fusion.refs_0_.code), channel_id=1, source_target_pairs={{0,12},{4,8},{8,4},{12,0},{1,13},{5,9},{9,5},{13,1},{2,14},{6,10},... | collective-permute-start | bytes 104 | tf_op jit(solution)/shard_map/ppermute | solution.py:376
  6.4 0.6 %collective-permute-start = (s32[8]{0:T(128)S(1)}, s32[8]{0:T(128)S(1)}, u32[]{:S(2)}, u32[]{:S(2)}) collective-permute-start(s32[8]{0:T(128)S(1)} %bitcast_add_fusion.refs_0_.code), channel_id=1, source_target_pairs={{0,4},{4,0},{8,12},{12,8},{1,5},{5,1},{9,13},{13,9},{2,6},{6,2},{1... | collective-permute-start | bytes 104 | tf_op jit(solution)/shard_map/ppermute | solution.py:376
  6.9 0.8 %sub.22 = f32[16]{0:T(128)S(1)} reshape(f32[1,1,1,2,8]{4,3,2,1,0:T(2,128)} %param.16) | data formatting | bytes 128 | tf_op jit(solution)/shard_map/sub | solution.py:58
  7.7 0.2 collective-permute-done.2.refs_3_
  7.9 2.9 %collective-permute-done.1.refs_2_ = s32[8]{0:T(128)S(1)} collective-permute-done((s32[8]{0:T(128)S(1)}, s32[8]{0:T(128)S(1)}, u32[]{:S(2)}, u32[]{:S(2)}) %collective-permute-start.1) | collective-permute-done | bytes 64 | tf_op jit(solution)/shard_map/ppermute | solution.py:376
  10.8 0.9 %copy-done.3 = bf16[1,1,1,8,32,512]{5,4,3,2,1,0:T(8,128)(2,1)S(1)} copy-done((bf16[1,1,1,8,32,512]{5,4,3,2,1,0:T(8,128)(2,1)S(1)}, bf16[1,1,1,8,32,512]{5,4,3,2,1,0:T(8,128)(2,1)}, u32[]{:S(2)}) %copy-start.3) | copy-done | bytes 262168
  11.8 0.7 %shard_map.114 = (bf16[2,32,512]{2,1,0:T(8,128)(2,1)S(1)}, bf16[2,32,512]{2,1,0:T(8,128)(2,1)S(1)}, bf16[2,32,512]{2,1,0:T(8,128)(2,1)S(1)}, bf16[2,32,512]{2,1,0:T(8,128)(2,1)S(1)}) custom-call(s32[8]{0:T(128)S(1)} %bitcast_add_fusion.refs_0_.code, s32[8]{0:T(128)S(1)} %collective-permute-done.refs_1_, s32[8]{0:T(128)S(1)} %collective-permute-done.1.refs_2_, ...), custom_call_target="tpu_custom_call" | custom-call | bytes 1048576 | tf_op jit(solution)/shard_map/pallas_call | solution.py:357
  12.5 0.1 collective-permute-start.3
  12.6 2.1 %collective-permute-start.4 = (bf16[2,32,512]{2,1,0:T(8,128)(2,1)S(1)}, bf16[2,32,512]{2,1,0:T(8,128)(2,1)S(1)}, u32[]{:S(2)}, u32[]{:S(2)}) collective-permute-start(bf16[2,32,512]{2,1,0:T(8,128)(2,1)S(1)} %get-tuple-element.25), channel_id=1, source_target_pairs={{0,8},{4,12},{8,0},{12,4},{1,9},{5,13},{9,1},{13,5},{2,10},{6,14},... | collective-permute-start | bytes 196616 | tf_op jit(solution)/shard_map/ppermute | solution.py:371
  14.7 2.3 %collective-permute-start.5 = (bf16[2,32,512]{2,1,0:T(8,128)(2,1)S(1)}, bf16[2,32,512]{2,1,0:T(8,128)(2,1)S(1)}, u32[]{:S(2)}, u32[]{:S(2)}) collective-permute-start(bf16[2,32,512]{2,1,0:T(8,128)(2,1)S(1)} %get-tuple-element.26), channel_id=1, source_target_pairs={{0,12},{4,8},{8,4},{12,0},{1,13},{5,9},{9,5},{13,1},{2,14},{6,10},... | collective-permute-start | bytes 196616 | tf_op jit(solution)/shard_map/ppermute | solution.py:371
  16.9 0.1 fusion.44
  17.0 0.8 %reshape.37.shifts.refs_1_ = s32[16]{0:T(128)S(1)} reshape(s32[1,1,1,2,8]{4,3,2,1,0:T(2,128)} %param.15) | data formatting | bytes 128 | tf_op jit(solution)/shard_map/reshape | solution.py:381
  17.8 0.7 %reduce = f32[3,9]{1,0:T(4,128)S(1)} reduce(f32[1,3,9]{2,0,1:T(1,128)} %param.17, f32[]{:T(128)} %constant.49), dimensions={0}, to_apply=%param.17.reduce_sub_computation | reduce | bytes 220 | tf_op args[6]
  18.5 0.1 reshape.40.coefs
  18.6 0.1 reshape.45.taps.refs_2_
  18.7 0.9 %copy-done.4 = bf16[3,256,128]{2,1,0:T(8,128)(2,1)S(1)} copy-done((bf16[3,256,128]{2,1,0:T(8,128)(2,1)S(1)}, bf16[3,256,128]{2,1,0:T(8,128)(2,1)}, u32[]{:S(2)}) %copy-start.4) | copy-done | bytes 196632
  19.6 1.6 %shard_map.113 = (bf16[4,768,256]{2,1,0:T(8,128)(2,1)S(1)}, bf16[256,256]{1,0:T(8,128)(2,1)S(1)}, bf16[192,192]{1,0:T(8,128)(2,1)S(1)}, bf16[64,64]{1,0:T(8,128)(2,1)S(1)}) custom-call(f32[27]{0:T(128)S(1)} %reshape.40.coefs, f32[96]{0:T(128)S(1)} %reshape.45.taps.refs_2_, s32[16]{0:T(128)S(1)} %reshape.37.shifts.refs_1_, bf16[3,256,128]{2,1,0:T(8,128)(2,1)S(1)} %copy-done.4), custom_call_target="tpu_custom_call" | custom-call | bytes 1048576 | tf_op jit(solution)/shard_map/pallas_call | solution.py:357
  21.3 1.4 %shard_map.115 = (bf16[256,640]{1,0:T(8,128)(2,1)S(1)}, bf16[16,640]{1,0:T(8,128)(2,1)S(1)}, bf16[256,128]{1,0:T(8,128)(2,1)S(1)}, bf16[16,128]{1,0:T(8,128)(2,1)S(1)}) custom-call(s32[8]{0:T(128)S(1)} %bitcast_add_fusion.refs_0_.code, s32[16]{0:T(128)S(1)} %reshape.37.shifts.refs_1_, f32[96]{0:T(128)S(1)} %reshape.45.taps.refs_2_, ...), custom_call_target="tpu_custom_call" | custom-call | bytes 1048576 | tf_op jit(solution)/shard_map/pallas_call | solution.py:357
  22.7 0.1 collective-permute-start.6
  22.7 1.6 %collective-permute-start.7 = (bf16[16,640]{1,0:T(8,128)(2,1)S(1)}, bf16[16,640]{1,0:T(8,128)(2,1)S(1)}, u32[]{:S(2)}, u32[]{:S(2)}) collective-permute-start(bf16[16,640]{1,0:T(8,128)(2,1)S(1)} %get-tuple-element.29), channel_id=1, source_target_pairs={{0,2},{2,0},{1,3},{3,1},{4,6},{6,4},{5,7},{7,5},{8,10},{10,8},{9,1... | collective-permute-start | bytes 61448 | tf_op jit(solution)/shard_map/ppermute | solution.py:417
  24.3 0.3 collective-permute-start.8
  24.6 1.0 %copy-done = f32[1,256,512]{2,1,0:T(8,128)S(1)} copy-done((f32[1,256,512]{2,1,0:T(8,128)S(1)}, f32[1,256,512]{2,1,0:T(8,128)}, u32[]{:S(2)}) %copy-start) | copy-done | bytes 524312
  25.7 1.0 %copy-done.2 = bf16[576,224]{1,0:T(8,128)(2,1)S(1)} copy-done((bf16[576,224]{1,0:T(8,128)(2,1)S(1)}, bf16[576,224]{1,0:T(8,128)(2,1)}, u32[]{:S(2)}) %copy-start.2) | copy-done | bytes 258072
  26.6 1.9 %shard_map.116 = (f32[192,512]{1,0:T(8,128)S(1)}, bf16[192,512]{1,0:T(8,128)(2,1)S(1)}) custom-call(bf16[256,640]{1,0:T(8,128)(2,1)S(1)} %get-tuple-element.27.image, bf16[256,128]{1,0:T(8,128)(2,1)S(1)} %collective-permute-done.6.left.right, bf16[256,128]{1,0:T(8,128)(2,1)S(1)} %collective-permute-done.6.left.right, f32[256,512]{1,0:T(8,128)S(1)} %bitcast.8, ...), custom_call_target="tpu_custom_call" | custom-call | bytes 1048576 | tf_op jit(solution)/shard_map/pallas_call | solution.py:357
  28.6 2.1 %shard_map.117 = (f32[256,512]{1,0:T(8,128)}, bf16[2,32,512]{2,1,0:T(8,128)(2,1)S(1)}, bf16[2,32,512]{2,1,0:T(8,128)(2,1)S(1)}, bf16[2,32,512]{2,1,0:T(8,128)(2,1)S(1)}, bf16[2,32,512]{2,1,0:T(8,128)(2,1)S(1)}) custom-call(bf16[256,640]{1,0:T(8,128)(2,1)S(1)} %get-tuple-element.27.image, bf16[256,128]{1,0:T(8,128)(2,1)S(1)} %collective-permute-done.6.left.right, ...), custom_call_target="tpu_custom_call" | custom-call | bytes 1048576 | tf_op jit(solution)/shard_map/pallas_call | solution.py:357
  30.7 0.3 collective-permute-start.9
  31.0 2.0 %collective-permute-start.10 = (bf16[2,32,512]{2,1,0:T(8,128)(2,1)S(1)}, bf16[2,32,512]{2,1,0:T(8,128)(2,1)S(1)}, u32[]{:S(2)}, u32[]{:S(2)}) collective-permute-start(bf16[2,32,512]{2,1,0:T(8,128)(2,1)S(1)} %get-tuple-element.39), channel_id=1, source_target_pairs={{0,8},{4,12},{8,0},{12,4},{1,9},{5,13},{9,1},{13,5},{2,10},{6,14},... | collective-permute-start | bytes 196616 | tf_op jit(solution)/shard_map/ppermute | solution.py:371
  33.0 2.1 %collective-permute-start.11 = (bf16[2,32,512]{2,1,0:T(8,128)(2,1)S(1)}, bf16[2,32,512]{2,1,0:T(8,128)(2,1)S(1)}, u32[]{:S(2)}, u32[]{:S(2)}) collective-permute-start(bf16[2,32,512]{2,1,0:T(8,128)(2,1)S(1)} %get-tuple-element.40), channel_id=1, source_target_pairs={{0,12},{4,8},{8,4},{12,0},{1,13},{5,9},{9,5},{13,1},{2,14},{6,10},... | collective-permute-start | bytes 196616 | tf_op jit(solution)/shard_map/ppermute | solution.py:371
  35.1 0.9 %collective-permute-done.9.refs_5_ = bf16[2,32,512]{2,1,0:T(8,128)(2,1)S(1)} collective-permute-done((bf16[2,32,512]{2,1,0:T(8,128)(2,1)S(1)}, bf16[2,32,512]{2,1,0:T(8,128)(2,1)S(1)}, u32[]{:S(2)}, u32[]{:S(2)}) %collective-permute-start.9) | collective-permute-done | bytes 65568 | tf_op jit(solution)/shard_map/ppermute | solution.py:371
  36.0 3.5 %collective-permute-done.10.refs_6_ = bf16[2,32,512]{2,1,0:T(8,128)(2,1)S(1)} collective-permute-done((bf16[2,32,512]{2,1,0:T(8,128)(2,1)S(1)}, bf16[2,32,512]{2,1,0:T(8,128)(2,1)S(1)}, u32[]{:S(2)}, u32[]{:S(2)}) %collective-permute-start.10) | collective-permute-done | bytes 65568 | tf_op jit(solution)/shard_map/ppermute | solution.py:371
  39.5 1.6 %shard_map.118 = f32[8,32,512]{2,1,0:T(8,128)} custom-call(s32[8]{0:T(128)S(1)} %bitcast_add_fusion.refs_0_.code, s32[8]{0:T(128)S(1)} %collective-permute-done.refs_1_, s32[8]{0:T(128)S(1)} %collective-permute-done.1.refs_2_, s32[8]{0:T(128)S(1)} %collective-permute-done.2.refs_3_, bf16[2,32,512]{2,1,0:T(8,128)(2,1)S(1)} %get-tuple-element.37.refs_4_, ...), custom_call_target="tpu_custom_call" | custom-call | bytes 1048576 | tf_op jit(solution)/shard_map/pallas_call | solution.py:357
  (18 shorter events, 0.0 us)
Async XLA Ops:
  1.3 6.6 %collective-permute-start.2 = (s32[8]{0:T(128)S(1)}, s32[8]{0:T(128)S(1)}, u32[]{:S(2)}, u32[]{:S(2)}) collective-permute-start(s32[8]{0:T(128)S(1)} %bitcast_add_fusion.refs_0_.code), channel_id=1, source_target_pairs={{0,12},{4,8},{8,4},{12,0},{1,13},{5,9},{9,5},{13,1},{2,14},{6,10},... | collective-permute-start | bytes 104 | tf_op jit(solution)/shard_map/ppermute | solution.py:376
  6.4 4.4 %collective-permute-start.1 = (s32[8]{0:T(128)S(1)}, s32[8]{0:T(128)S(1)}, u32[]{:S(2)}, u32[]{:S(2)}) collective-permute-start(s32[8]{0:T(128)S(1)} %bitcast_add_fusion.refs_0_.code), channel_id=1, source_target_pairs={{0,8},{4,12},{8,0},{12,4},{1,9},{5,13},{9,1},{13,5},{2,10},{6,14},... | collective-permute-start | bytes 104 | tf_op jit(solution)/shard_map/ppermute | solution.py:376
  6.4 4.4 %collective-permute-start = (s32[8]{0:T(128)S(1)}, s32[8]{0:T(128)S(1)}, u32[]{:S(2)}, u32[]{:S(2)}) collective-permute-start(s32[8]{0:T(128)S(1)} %bitcast_add_fusion.refs_0_.code), channel_id=1, source_target_pairs={{0,4},{4,0},{8,12},{12,8},{1,5},{5,1},{9,13},{13,9},{2,6},{6,2},{1... | collective-permute-start | bytes 104 | tf_op jit(solution)/shard_map/ppermute | solution.py:376
  10.8 1.0 %copy-start.3 = (bf16[1,1,1,8,32,512]{5,4,3,2,1,0:T(8,128)(2,1)S(1)}, bf16[1,1,1,8,32,512]{5,4,3,2,1,0:T(8,128)(2,1)}, u32[]{:S(2)}) copy-start(bf16[1,1,1,8,32,512]{5,4,3,2,1,0:T(8,128)(2,1)} %param.12) | copy-start | bytes 786436
  12.5 8.7 %collective-permute-start.3 = (bf16[2,32,512]{2,1,0:T(8,128)(2,1)S(1)}, bf16[2,32,512]{2,1,0:T(8,128)(2,1)S(1)}, u32[]{:S(2)}, u32[]{:S(2)}) collective-permute-start(bf16[2,32,512]{2,1,0:T(8,128)(2,1)S(1)} %get-tuple-element.24), channel_id=1, source_target_pairs={{0,4},{4,0},{8,12},{12,8},{1,5},{5,1},{9,13},{13,9},{2,6},{6,2},{1... | collective-permute-start | bytes 196616 | tf_op jit(solution)/shard_map/ppermute | solution.py:371
  12.6 8.7 %collective-permute-start.4 = (bf16[2,32,512]{2,1,0:T(8,128)(2,1)S(1)}, bf16[2,32,512]{2,1,0:T(8,128)(2,1)S(1)}, u32[]{:S(2)}, u32[]{:S(2)}) collective-permute-start(bf16[2,32,512]{2,1,0:T(8,128)(2,1)S(1)} %get-tuple-element.25), channel_id=1, source_target_pairs={{0,8},{4,12},{8,0},{12,4},{1,9},{5,13},{9,1},{13,5},{2,10},{6,14},... | collective-permute-start | bytes 196616 | tf_op jit(solution)/shard_map/ppermute | solution.py:371
  14.7 6.6 %collective-permute-start.5 = (bf16[2,32,512]{2,1,0:T(8,128)(2,1)S(1)}, bf16[2,32,512]{2,1,0:T(8,128)(2,1)S(1)}, u32[]{:S(2)}, u32[]{:S(2)}) collective-permute-start(bf16[2,32,512]{2,1,0:T(8,128)(2,1)S(1)} %get-tuple-element.26), channel_id=1, source_target_pairs={{0,12},{4,8},{8,4},{12,0},{1,13},{5,9},{9,5},{13,1},{2,14},{6,10},... | collective-permute-start | bytes 196616 | tf_op jit(solution)/shard_map/ppermute | solution.py:371
  18.7 0.9 %copy-start.4 = (bf16[3,256,128]{2,1,0:T(8,128)(2,1)S(1)}, bf16[3,256,128]{2,1,0:T(8,128)(2,1)}, u32[]{:S(2)}) copy-start(bf16[3,256,128]{2,1,0:T(8,128)(2,1)} %constant.39.clone.bands) | copy-start | bytes 589828
  19.6 8.9 %copy-start.1 = (f32[1,256,512]{2,1,0:T(8,128)S(1)}, f32[1,256,512]{2,1,0:T(8,128)}, u32[]{:S(2)}) copy-start(f32[1,256,512]{2,1,0:T(8,128)} %param.11) | copy-start | bytes 1572868
  21.3 7.3 %copy-start.5 = (bf16[96,64]{1,0:T(8,128)(2,1)S(1)}, bf16[96,64]{1,0:T(8,128)(2,1)}, u32[]{:S(2)}) copy-start(bf16[96,64]{1,0:T(8,128)(2,1)} %constant.41.clone.bands) | copy-start | bytes 36868
  22.7 1.9 %collective-permute-start.6 = (bf16[256,128]{1,0:T(8,128)(2,1)S(1)}, bf16[256,128]{1,0:T(8,128)(2,1)S(1)}, u32[]{:S(2)}, u32[]{:S(2)}) collective-permute-start(bf16[256,128]{1,0:T(8,128)(2,1)S(1)} %get-tuple-element.28), channel_id=1, source_target_pairs={{0,1},{1,0},{2,3},{3,2},{4,5},{5,4},{6,7},{7,6},{8,9},{9,8},{10,11... | collective-permute-start | bytes 196616 | tf_op jit(solution)/shard_map/ppermute | solution.py:416
  22.7 5.8 %collective-permute-start.7 = (bf16[16,640]{1,0:T(8,128)(2,1)S(1)}, bf16[16,640]{1,0:T(8,128)(2,1)S(1)}, u32[]{:S(2)}, u32[]{:S(2)}) collective-permute-start(bf16[16,640]{1,0:T(8,128)(2,1)S(1)} %get-tuple-element.29), channel_id=1, source_target_pairs={{0,2},{2,0},{1,3},{3,1},{4,6},{6,4},{5,7},{7,5},{8,10},{10,8},{9,1... | collective-permute-start | bytes 61448 | tf_op jit(solution)/shard_map/ppermute | solution.py:417
  24.3 4.2 %collective-permute-start.8 = (bf16[16,128]{1,0:T(8,128)(2,1)S(1)}, bf16[16,128]{1,0:T(8,128)(2,1)S(1)}, u32[]{:S(2)}, u32[]{:S(2)}) collective-permute-start(bf16[16,128]{1,0:T(8,128)(2,1)S(1)} %get-tuple-element.30), channel_id=1, source_target_pairs={{0,3},{3,0},{1,2},{2,1},{4,7},{7,4},{5,6},{6,5},{8,11},{11,8},{9,1... | collective-permute-start | bytes 12296 | tf_op jit(solution)/shard_map/ppermute | solution.py:418
  24.6 1.0 %copy-start = (f32[1,256,512]{2,1,0:T(8,128)S(1)}, f32[1,256,512]{2,1,0:T(8,128)}, u32[]{:S(2)}) copy-start(f32[1,256,512]{2,1,0:T(8,128)} %param.11) | copy-start | bytes 1572868
  25.7 1.0 %copy-start.2 = (bf16[576,224]{1,0:T(8,128)(2,1)S(1)}, bf16[576,224]{1,0:T(8,128)(2,1)}, u32[]{:S(2)}) copy-start(bf16[576,224]{1,0:T(8,128)(2,1)} %constant.40.clone.bands) | copy-start | bytes 774148
  30.7 5.3 %collective-permute-start.9 = (bf16[2,32,512]{2,1,0:T(8,128)(2,1)S(1)}, bf16[2,32,512]{2,1,0:T(8,128)(2,1)S(1)}, u32[]{:S(2)}, u32[]{:S(2)}) collective-permute-start(bf16[2,32,512]{2,1,0:T(8,128)(2,1)S(1)} %get-tuple-element.38), channel_id=1, source_target_pairs={{0,4},{4,0},{8,12},{12,8},{1,5},{5,1},{9,13},{13,9},{2,6},{6,2},{1... | collective-permute-start | bytes 196616 | tf_op jit(solution)/shard_map/ppermute | solution.py:371
  31.0 8.5 %collective-permute-start.10 = (bf16[2,32,512]{2,1,0:T(8,128)(2,1)S(1)}, bf16[2,32,512]{2,1,0:T(8,128)(2,1)S(1)}, u32[]{:S(2)}, u32[]{:S(2)}) collective-permute-start(bf16[2,32,512]{2,1,0:T(8,128)(2,1)S(1)} %get-tuple-element.39), channel_id=1, source_target_pairs={{0,8},{4,12},{8,0},{12,4},{1,9},{5,13},{9,1},{13,5},{2,10},{6,14},... | collective-permute-start | bytes 196616 | tf_op jit(solution)/shard_map/ppermute | solution.py:371
  33.0 6.5 %collective-permute-start.11 = (bf16[2,32,512]{2,1,0:T(8,128)(2,1)S(1)}, bf16[2,32,512]{2,1,0:T(8,128)(2,1)S(1)}, u32[]{:S(2)}, u32[]{:S(2)}) collective-permute-start(bf16[2,32,512]{2,1,0:T(8,128)(2,1)S(1)} %get-tuple-element.40), channel_id=1, source_target_pairs={{0,12},{4,8},{8,4},{12,0},{1,13},{5,9},{9,5},{13,1},{2,14},{6,10},... | collective-permute-start | bytes 196616 | tf_op jit(solution)/shard_map/ppermute | solution.py:371
where the time goes:
time: 41.4 us; the launch traced here: 41.1 us
  starting transfers between devices  16.4 us (40%)
  Pallas kernels  9.34 us (23%)
  waiting for transfers between devices  7.54 us (18%)
  local copies, waits for them, and re-layouts  5.58 us (13%)
  other arithmetic  1.47 us (4%)
  between operations  0.77 us (2%)
    pallas_call x6, Pallas kernels, call(): pl.pallas_call(kernel, out_shape=[jax.ShapeDtypeStruct(s, d) for s, d in...  9.34 us
    ppermute x6, starting transfers between devices, exchange(): lax.ppermute(parts[g], 'ccd', [(i, i ^ g) for i in range(n)])  8.83 us
    ppermute x3, starting transfers between devices, body(): lax.ppermute(code, 'ccd', [(i, i ^ g) for i in range(n)])  5.62 us
    ppermute x6, waiting for transfers between devices, exchange(): lax.ppermute(parts[g], 'ccd', [(i, i ^ g) for i in range(n)])  4.42 us
    unnamed x12, local copies, waits for them, and re-layouts  3.89 us
    ppermute x3, waiting for transfers between devices, body(): lax.ppermute(code, 'ccd', [(i, i ^ g) for i in range(n)])  3.11 us
    ppermute x1, starting transfers between devices, body(): ends = lax.ppermute(warped[1], 'row', swap)  1.56 us
  transfers between devices with their start and end apart: 12, of which 4 were waited for; matrix products, arithmetic and copies ran while one was open for 6% of the time, Pallas kernels for 9%

commit v1 on v0

--- a/solution.py
+++ b/solution.py
@@ -20,6 +20,7 @@
 BF16 = jnp.bfloat16
 SMEM = pl.BlockSpec(memory_space=pltpu.SMEM)
 VMEM = pl.BlockSpec(memory_space=pltpu.VMEM)
+HBM = pl.BlockSpec(memory_space=pltpu.HBM)
 
 
 def kernel_table():
@@ -53,10 +54,19 @@
     ).astype(ml_dtypes.bfloat16)
 
 
+def sinc(value):
+    turn = jnp.pi * value
+    return jnp.where(value == 0.0, 1.0, jnp.sin(turn) / jnp.where(value == 0.0, 1.0, turn))
+
+
 def lanczos_taps(fraction):
-    offsets = jnp.arange(-2, 4).astype(F32)
-    spread = offsets[None, :] - fraction[:, None]
-    return (jnp.sinc(spread) * jnp.sinc(spread / 3.0)).astype(BF16)
+    place = lax.broadcasted_iota(jnp.int32, (8, fraction.shape[1]), 0) - 2
+    spread = place.astype(F32) - fraction
+    return (sinc(spread) * sinc(spread / 3.0)).astype(BF16).astype(F32)
+
+
+def in_hbm(value):
+    return pltpu.with_memory_space_constraint(value, pltpu.HBM)
 
 
 def lane_index(rows):
@@ -105,25 +115,24 @@
                 outs[0][g * capacity + j] = template[found[j]]
 
 
-def prepare_kernel(strips, strip_rows, tiles, amp_count, coefs, taps, shifts, bands, de, forward, mid, edge):
-    amp = lax.axis_index("amp")
-    width = tiles * LANES
-    for first in range(KINDS):
-        for tile in range(tiles):
-            column = lane_index(1) + (amp * width + tile * LANES)
-            px = (column.astype(F32) + 0.5) / (width * amp_count) * 2.0 - 1.0
-            for half in range(2):
-                rows = pl.ds(half * LANES, LANES)
-                d = jnp.zeros((LANES, LANES), F32)
-                e = jnp.zeros((LANES, LANES), F32)
-                for second in range(KINDS):
-                    basis = first * KINDS + second
-                    band = bands[second, rows, :].astype(F32)
-                    d = d + band * (coefs[basis] + coefs[9 + basis] * px)
-                    e = e + band * coefs[18 + basis]
-                at = pl.ds(half * KINDS * LANES + first * LANES, LANES)
-                de[tile, at, 0:LANES] = d.astype(BF16)
-                de[tile, at, LANES : 2 * LANES] = e.astype(BF16)
+def load_kernel(source, target, sem):
+    copy = pltpu.make_async_copy(source, target, sem)
+    copy.start()
+    copy.wait()
+
+
+def prepare_kernel(strips, strip_rows, tiles, amp_count, coefs_in, shifts_in, fractions_in, bands_in, science_in,
+                   row_band_in, after, de, forward, mid, edge, spread, gather, science, row_band,
+                   coefs, shifts, fractions, bands, sems):
+    del after
+    pairs = [(fractions_in, fractions), (shifts_in, shifts), (coefs_in, coefs),
+             (bands_in, bands), (row_band_in, row_band), (science_in, science)]
+    copies = [pltpu.make_async_copy(source, target, sems.at[i]) for i, (source, target) in enumerate(pairs)]
+    for copy in copies:
+        copy.start()
+    for copy in copies[:2]:
+        copy.wait()
+    taps = [lanczos_taps(fractions[d : d + 1, :]) for d in range(2)]
 
     def operator(out, chosen, transposed):
         size = out.shape[1]
@@ -133,24 +142,63 @@
             low = place * strip_rows
             within = (lane >= low) & (lane < low + strip_rows)
             step = lane - low - row
-            offset = (-step if transposed else step) - shifts[q]
+            offset = (-step if transposed else step) - shifts[0, q]
             offset = jnp.where(within, offset, jnp.int32(1 << 20))
             value = jnp.zeros((strip_rows, size), F32)
             for t in range(TAPS):
-                value = jnp.where(offset == t - 2, taps[q * TAPS + t], value)
+                tap = jnp.broadcast_to(taps[0][t : t + 1, q : q + 1], (strip_rows, size))
+                value = jnp.where(offset == t - 2, tap, value)
             out[pl.ds(low, strip_rows), :] = value.astype(BF16)
 
     operator(forward, range(strips), False)
     operator(mid, range(1, strips - 1), True)
     operator(edge, (0, strips - 1), True)
 
+    rows = 160
+    away = lane_index(rows) - lax.broadcasted_iota(jnp.int32, (rows, LANES), 0)
+    for out, low, centre, sign in ((spread, 48, HALF_TILE, 1), (gather, 112, LANES, -1)):
+        size = out.shape[1]
+        for q in range(strips):
+            step = -sign * (away + (centre - low)) - shifts[1, q]
+            value = jnp.zeros((rows, LANES), F32)
+            for t in range(TAPS):
+                tap = jnp.broadcast_to(taps[1][t : t + 1, q : q + 1], (rows, LANES))
+                value = jnp.where(step == t - 2, tap, value)
+            out[q, 0:low, :] = jnp.zeros((low, LANES), BF16)
+            out[q, low : low + rows, :] = value.astype(BF16)
+            out[q, low + rows : size, :] = jnp.zeros((size - low - rows, LANES), BF16)
+    for copy in copies[2:4]:
+        copy.wait()
+    amp = lax.axis_index("amp")
+    width = tiles * LANES
+    for first in range(KINDS):
+        for half in range(2):
+            rows = pl.ds(half * LANES, LANES)
+            at = pl.ds((half * KINDS + first) * LANES, LANES)
+            band = [bands[second, rows, :].astype(F32) for second in range(KINDS)]
+            e = sum(band[b] * coefs[2, 0, first * KINDS + b] for b in range(KINDS)).astype(BF16)
+            for tile in range(tiles):
+                column = lane_index(1) + (amp * width + tile * LANES)
+                px = (column.astype(F32) + 0.5) / (width * amp_count) * 2.0 - 1.0
+                weight = [coefs[0, 0, first * KINDS + b] + coefs[1, 0, first * KINDS + b] * px for b in range(KINDS)]
+                de[tile, at, 0:LANES] = sum(band[b] * weight[b] for b in range(KINDS)).astype(BF16)
+                de[tile, at, LANES : 2 * LANES] = e
+    for copy in copies[4:]:
+        copy.wait()
+
+
+def clear_ends(ref, tiles):
+    zero = jnp.zeros((ref.shape[0], LANES), BF16)
+    ref[:, 0:LANES] = zero
+    ref[:, (tiles + 1) * LANES : (tiles + 2) * LANES] = zero
+
 
 def warp_kernel(n, capacity, strips, strip_rows, tiles, xor, paired, *refs):
-    code, shifts, taps, forward = refs[:4]
+    code, forward, spread = refs[:3]
     if xor:
-        received, rest = refs[4 : 4 + n], refs[4 + n :]
-    else:
-        received, rest = refs[4:5], refs[5:]
+        received, rest = refs[3 : 3 + n], refs[3 + n :]
+    else:
+        received, rest = refs[3:4], refs[4:]
     if paired:
         image, send_row, send_amp, send_diag, pool, fetched, rows_done = rest
     else:
@@ -163,31 +211,23 @@
         pool[...] = received[0][...]
     for q, slot in enumerate(slots_of(code, me, strips, capacity, xor)):
         fetched[pl.ds(q * strip_rows, strip_rows), :] = pool[slot]
-    rows_done[...] = jnp.dot(forward[...], fetched[...], preferred_element_type=F32).astype(BF16).astype(F32)
+    width = tiles * LANES
+    clear_ends(rows_done, tiles)
+    rows_done[:, LANES : LANES + width] = jnp.dot(
+        forward[...], fetched[...], preferred_element_type=F32
+    ).astype(BF16)
     lane = lane_index(strip_rows)
     for q in range(strips):
-        rows = pl.ds(q * strip_rows, strip_rows)
-        source = [rows_done[rows, pl.ds(b * LANES, LANES)] for b in range(tiles)]
-        total = [jnp.zeros((strip_rows, LANES), F32)] * (tiles + 1)
-        for t in range(TAPS):
-            amount = HALF_TILE - (shifts[strips + q] + (t - 2))
-            tap = taps[(strips + q) * TAPS + t]
-            spill = lane < amount
-            before = None
-            for b in range(tiles + 1):
-                here = pltpu.roll(source[b], amount, 1) * tap if b < tiles else None
-                if before is None:
-                    value = jnp.where(spill, 0.0, here)
-                elif here is None:
-                    value = jnp.where(spill, before, 0.0)
-                else:
-                    value = jnp.where(spill, before, here)
-                total[b] = total[b] + value
-                before = here
-        total[0] = jnp.where(lane < HALF_TILE, 0.0, total[0])
-        total[tiles] = jnp.where(lane < HALF_TILE, total[tiles], 0.0)
+        rows = slice(q * strip_rows, (q + 1) * strip_rows)
+        windows = [rows_done[rows, b * LANES : (b + 2) * LANES] for b in range(tiles + 1)]
+        result = jnp.dot(jnp.concatenate(windows, axis=0), spread[q], preferred_element_type=F32)
         for b in range(tiles + 1):
-            image[rows, pl.ds(b * LANES, LANES)] = total[b].astype(BF16)
+            value = result[b * strip_rows : (b + 1) * strip_rows]
+            if b == 0:
+                value = jnp.where(lane < HALF_TILE, 0.0, value)
+            if b == tiles:
+                value = jnp.where(lane < HALF_TILE, value, 0.0)
+            image[rows, b * LANES : (b + 1) * LANES] = value.astype(BF16)
     if paired:
         band = strips * strip_rows
         row_first = lax.axis_index("row") == 0
@@ -216,23 +256,12 @@
                 across[at : at + count, (b * KINDS + kind) * LANES : (b * KINDS + kind + 1) * LANES] = piece.astype(BF16)
 
 
-def columns_returned(lowered, columns, at, strips, q, strip_rows, tiles, shifts, taps):
-    lane = lane_index(strip_rows)
+def columns_returned(lowered, columns, at, gather, strip_rows, tiles):
     rows = slice(at, at + strip_rows)
-    source = [lowered[rows, b * LANES : (b + 1) * LANES] for b in range(tiles)]
-    total = [jnp.zeros((strip_rows, LANES), F32)] * tiles
-    for t in range(TAPS):
-        amount = shifts[strips + q] + (t - 2)
-        tap = taps[(strips + q) * TAPS + t]
-        turn = jnp.where(amount < 0, amount + LANES, amount)
-        low, high = lane < amount, lane >= LANES + amount
-        moved = [pltpu.roll(s, turn, 1) * tap for s in source]
-        for b in range(tiles):
-            value = jnp.where(low, moved[b - 1] if b > 0 else 0.0, moved[b])
-            value = jnp.where(high, moved[b + 1] if b < tiles - 1 else 0.0, value)
-            total[b] = total[b] + value
+    windows = [lowered[rows, b * LANES : (b + 3) * LANES] for b in range(tiles)]
+    result = jnp.dot(jnp.concatenate(windows, axis=0), gather, preferred_element_type=F32)
     for b in range(tiles):
-        columns[rows, b * LANES : (b + 1) * LANES] = total[b].astype(BF16)
+        columns[rows, b * LANES : (b + 1) * LANES] = result[b * strip_rows : (b + 1) * strip_rows].astype(BF16)
 
 
 def subtracted(science, across, de, store, count, tiles, place):
@@ -249,29 +278,30 @@
 
 
 def mid_kernel(strips, strip_rows, tiles, row_count, amp_count, image, left, right, science, de, bands, operator,
-               shifts, taps, diff, contribution, across, lowered, columns):
+               gather, diff, contribution, across, lowered, columns):
     band = strips * strip_rows
     count = band - 2 * strip_rows
     rows = slice(strip_rows - MARGIN, band - strip_rows + MARGIN)
     parts = joined(image, rows, left[rows, :], right[rows, :], tiles, amp_count)
     row_convolved(bands[...], parts, across, 0, count)
+    clear_ends(lowered, tiles)
 
     def store(b, value):
         diff[:, b * LANES : (b + 1) * LANES] = value
-        lowered[:, b * LANES : (b + 1) * LANES] = value.astype(BF16).astype(F32)
+        lowered[:, (b + 1) * LANES : (b + 2) * LANES] = value.astype(BF16)
 
     subtracted(
         lambda b: science[strip_rows : strip_rows + count, b * LANES : (b + 1) * LANES],
         across, de, store, count, tiles, row_place(strip_rows, count, band, row_count),
     )
     for q in range(1, strips - 1):
-        columns_returned(lowered, columns, (q - 1) * strip_rows, strips, q, strip_rows, tiles, shifts, taps)
+        columns_returned(lowered, columns, (q - 1) * strip_rows, gather[q], strip_rows, tiles)
     contribution[...] = jnp.dot(operator[...], columns[...], preferred_element_type=F32).astype(BF16)
 
 
 def edge_kernel(n, capacity, strips, strip_rows, tiles, row_count, amp_count, xor, image, left, right, top, bottom,
-                top_left, top_right, bottom_left, bottom_right, science, de, bands, operator, shifts, taps, code,
-                diff_mid, contribution_mid, diff, *rest):
+                top_left, top_right, bottom_left, bottom_right, science, de, bands, operator, gather, code,
+                contribution_mid, diff, *rest):
     outs = rest[: n if xor else 1]
     across, lowered, columns, pool = rest[len(outs) :]
     band = strips * strip_rows
@@ -291,9 +321,10 @@
 
     def store(b, value):
         at = slice(b * LANES, (b + 1) * LANES)
-        diff[0:strip_rows, at] = value[0:strip_rows]
-        diff[band - strip_rows : band, at] = value[strip_rows:]
-        lowered[:, at] = value.astype(BF16).astype(F32)
+        diff[:, at] = value
+        lowered[:, (b + 1) * LANES : (b + 2) * LANES] = value.astype(BF16)
+
+    clear_ends(lowered, tiles)
 
     def edge_science(b):
         at = slice(b * LANES, (b + 1) * LANES)
@@ -302,9 +333,8 @@
     place = jnp.concatenate([row_place(0, strip_rows, band, row_count),
                              row_place(band - strip_rows, strip_rows, band, row_count)], axis=0)
     subtracted(edge_science, across, de, store, 2 * strip_rows, tiles, place)
-    diff[strip_rows : band - strip_rows, :] = diff_mid[...]
-    columns_returned(lowered, columns, 0, strips, 0, strip_rows, tiles, shifts, taps)
-    columns_returned(lowered, columns, strip_rows, strips, strips - 1, strip_rows, tiles, shifts, taps)
+    columns_returned(lowered, columns, 0, gather[0], strip_rows, tiles)
+    columns_returned(lowered, columns, strip_rows, gather[strips - 1], strip_rows, tiles)
     ends = jnp.dot(operator[...], columns[...], preferred_element_type=F32).astype(BF16)
     me = lax.axis_index("ccd")
     target = pool if xor else outs[0]
@@ -359,7 +389,7 @@
             out_shape=[jax.ShapeDtypeStruct(s, d) for s, d in out_shape],
             in_specs=list(spaces),
             out_specs=[VMEM] * len(out_shape),
-            scratch_shapes=[pltpu.VMEM(s, d) for s, d in scratch],
+            scratch_shapes=[pltpu.VMEM(*s) if isinstance(s, tuple) else s for s in scratch],
             compiler_params=pltpu.CompilerParams(vmem_limit_bytes=megabytes << 20),
             cost_estimate=pl.CostEstimate(flops=flops, bytes_accessed=1 << 20, transcendentals=0),
         )(*operands)
@@ -378,11 +408,13 @@
     else:
         codes = [lax.all_gather(code, "ccd", axis=0, tiled=True)]
         picked_shapes = [((n * capacity, strip_rows, width), BF16)]
-    shift_list = shifts.reshape(2 * strips)
-    taps = lanczos_taps(fractions.reshape(2 * strips)).astype(F32).reshape(2 * strips * TAPS)
-    science = science.reshape(band, width)
-    template_strips = template.reshape(strips, strip_rows, width)
-
+    (template_strips,) = call(
+        load_kernel,
+        [((strips, strip_rows, width), BF16)],
+        [in_hbm(template.reshape(strips, strip_rows, width))],
+        [HBM],
+        [pltpu.SemaphoreType.DMA],
+    )
     picked = call(
         functools.partial(pick_kernel, n, capacity, strips, xor),
         picked_shapes,
@@ -390,16 +422,25 @@
         [SMEM] * len(codes) + [VMEM],
     )
     mid_rows = band - 2 * strip_rows
-    de, forward, mid_operator, edge_operator = call(
+    mid_bands = jnp.asarray(row_bands(mid_rows))
+    de, forward, mid_operator, edge_operator, spread, gather, science, mid_bands = call(
         functools.partial(prepare_kernel, strips, strip_rows, tiles, amp_count),
         [
             ((tiles, 2 * KINDS * LANES, 2 * LANES), BF16),
             ((band, band), BF16),
             ((mid_rows, mid_rows), BF16),
             ((2 * strip_rows, 2 * strip_rows), BF16),
+            ((strips, 2 * LANES, LANES), BF16),
+            ((strips, 3 * LANES, LANES), BF16),
+            ((band, width), F32),
+            (mid_bands.shape, BF16),
         ],
-        [coefs.reshape(27), taps, shift_list, jnp.asarray(column_bands())],
-        [SMEM, SMEM, SMEM, VMEM],
+        [in_hbm(value) for value in (
+            coefs.transpose(1, 0, 2), shifts.reshape(2, strips), fractions.reshape(2, strips),
+            jnp.asarray(column_bands()), science.reshape(band, width), mid_bands)] + [picked[0]],
+        [HBM] * 6 + [VMEM],
+        [pltpu.SMEM((3, 1, 9), F32), pltpu.SMEM((2, strips), jnp.int32),
+         ((2, strips), F32), ((KINDS, 2 * LANES, LANES), BF16), pltpu.SemaphoreType.DMA((6,))],
     )
     received = exchange(picked)
     image_shape = ((band, padded), BF16)
@@ -407,9 +448,10 @@
     warped = call(
         functools.partial(warp_kernel, n, capacity, strips, strip_rows, tiles, xor, paired),
         [image_shape] + (halo_shapes if paired else []),
-        [code, shift_list, taps, forward, *received],
-        [SMEM, SMEM, SMEM, VMEM] + [VMEM] * len(received),
-        [((n * capacity, strip_rows, width), BF16), ((band, width), BF16), ((band, width), F32)],
+        [code, forward, spread, *received],
+        [SMEM, VMEM, VMEM] + [VMEM] * len(received),
+        [((n * capacity, strip_rows, width), BF16), ((band, width), BF16),
+         ((band, padded + LANES), BF16)],
     )
     image = warped[0]
     if paired:
@@ -441,19 +483,20 @@
     diff_mid, contribution_mid = call(
         functools.partial(mid_kernel, strips, strip_rows, tiles, row_count, amp_count),
         [((mid_rows, width), F32), ((mid_rows, width), BF16)],
-        [image, left, right, science, de, jnp.asarray(row_bands(mid_rows)), mid_operator, shift_list, taps],
-        [VMEM] * 7 + [SMEM] * 2,
-        [((mid_rows, (tiles + 1) * KINDS * LANES), BF16), ((mid_rows, width), F32), ((mid_rows, width), BF16)],
+        [image, left, right, science, de, mid_bands, mid_operator, gather],
+        [VMEM] * 8,
+        [((mid_rows, (tiles + 1) * KINDS * LANES), BF16), ((mid_rows, padded + LANES), BF16),
+         ((mid_rows, width), BF16)],
         megabytes=12,
     )
     outgoing_shapes = picked_shapes
-    difference, *outgoing = call(
+    diff_edge, *outgoing = call(
         functools.partial(edge_kernel, n, capacity, strips, strip_rows, tiles, row_count, amp_count, xor),
-        [((band, width), F32)] + outgoing_shapes,
+        [((2 * strip_rows, width), F32)] + outgoing_shapes,
         [image, left, right, top, bottom, top_left, top_right, bottom_left, bottom_right, science, de,
-         jnp.asarray(row_bands(strip_rows)), edge_operator, shift_list, taps, code, diff_mid, contribution_mid],
-        [VMEM] * 13 + [SMEM] * 3 + [VMEM] * 2,
-        [((2 * strip_rows, (tiles + 1) * KINDS * LANES), BF16), ((2 * strip_rows, width), F32),
+         jnp.asarray(row_bands(strip_rows)), edge_operator, gather, code, contribution_mid],
+        [VMEM] * 14 + [SMEM, VMEM],
+        [((2 * strip_rows, (tiles + 1) * KINDS * LANES), BF16), ((2 * strip_rows, padded + LANES), BF16),
          ((2 * strip_rows, width), BF16), ((n * capacity, strip_rows, width), BF16)],
         megabytes=12,
     )
@@ -464,6 +507,7 @@
         [*codes, *returned],
         [SMEM] * len(codes) + [VMEM] * len(returned),
     )
+    difference = jnp.concatenate([diff_edge[:strip_rows], diff_mid, diff_edge[strip_rows:]])
     return difference[None], stack.reshape(template.shape)
 
 

time: 41.4 us -> 38 us (0.918)
  local copies, waits for them, and re-layouts: 5.58 us -> 0.01 us
  waiting for transfers between devices: 7.54 us -> 9.62 us
    unnamed x12 -> x2, local copies, waits for them, and re-layouts: 3.89 us -> 0.01 us
    ppermute x1, waiting for transfers between devices: 0.01 us -> 1.38 us  [body(): lax.ppermute(warped[3], ('row', 'amp'), [(0, 3), (3, 0), (1, 2), (2, 1)])]
    reshape x3 -> x0, local copies, waits for them, and re-layouts: 0.93 us -> none  [the longest x1 0.76 us: body(): shift_list = shifts.reshape(2 * strips)]
    ppermute x6, waiting for transfers between devices: 4.42 us -> 5.33 us  [exchange(): lax.ppermute(parts[g], 'ccd', [(i, i ^ g) for i in range(n)])]
    broadcast_in_dim x0 -> x1, other arithmetic: none -> 0.83 us  [body(): return (difference[None], stack.reshape(template.shape))]
    sub x1 -> x0, local copies, waits for them, and re-layouts: 0.76 us -> none  [lanczos_taps(): spread = offsets[None, :] - fraction[:, None]]
    unnamed x1 -> x0, other arithmetic: 0.7 us -> none
    pallas_call x6 -> x7, Pallas kernels: 9.34 us -> 9.48 us  [call(): pl.pallas_call(kernel, out_shape=[jax.ShapeDtypeStruct(s, d) for s, d in...]
  transfers between devices with their start and end apart: 12 -> 12, of which waited for: 4 -> 4; matrix products, arithmetic and copies ran while one was open for 6% -> 2% of each run, Pallas kernels for 9% -> 12%
where the time goes in v1:
time: 38 us; the launch traced here: 37.8 us
  starting transfers between devices  16.4 us (43%)
  waiting for transfers between devices  9.62 us (25%)
  Pallas kernels  9.48 us (25%)
  other arithmetic  1.51 us (4%)
  between operations  0.73 us (2%)
    pallas_call x7, Pallas kernels, call(): pl.pallas_call(kernel, out_shape=[jax.ShapeDtypeStruct(s, d) for s, d in...  9.48 us
    ppermute x6, starting transfers between devices, exchange(): lax.ppermute(parts[g], 'ccd', [(i, i ^ g) for i in range(n)])  8.9 us
    ppermute x3, starting transfers between devices, body(): lax.ppermute(code, 'ccd', [(i, i ^ g) for i in range(n)])  5.62 us
    ppermute x6, waiting for transfers between devices, exchange(): lax.ppermute(parts[g], 'ccd', [(i, i ^ g) for i in range(n)])  5.33 us
    ppermute x3, waiting for transfers between devices, body(): lax.ppermute(code, 'ccd', [(i, i ^ g) for i in range(n)])  2.9 us
    ppermute x1, starting transfers between devices, body(): ends = lax.ppermute(warped[1], 'row', swap)  1.55 us
    ppermute x1, waiting for transfers between devices, body(): lax.ppermute(warped[3], ('row', 'amp'), [(0, 3), (3, 0), (1, 2), (2, 1)])  1.38 us
    broadcast_in_dim x1, other arithmetic, body(): return (difference[None], stack.reshape(template.shape))  0.83 us
  transfers between devices with their start and end apart: 12, of which 4 were waited for; matrix products, arithmetic and copies ran while one was open for 2% of the time, Pallas kernels for 12%

profile of v1, /device:TPU:0, one launch (start us, length us, event | category | flops | bytes accessed | tf_op | source)
XLA Modules:
  0.0 37.8 jit_solution(8546277209048326254)
XLA Ops:
  0.6 0.7 %bitcast_add_fusion.refs_0_.code = s32[8]{0:T(128)S(1)} fusion(s32[1,1,1,8]{3,2,1,0:T(1,128)} %param.13, s32[1,1,1,8,1]{3,4,2,1,0:T(1,128)} %param.12), kind=kLoop, calls=%fused_computation.1 | loop fusion | flops 16 | bytes 96 | tf_op jit(solution)/shard_map/add | solution.py:404
  1.3 5.0 %collective-permute-start.2 = (s32[8]{0:T(128)S(1)}, s32[8]{0:T(128)S(1)}, u32[]{:S(2)}, u32[]{:S(2)}) collective-permute-start(s32[8]{0:T(128)S(1)} %bitcast_add_fusion.refs_0_.code), channel_id=1, source_target_pairs={{0,12},{4,8},{8,4},{12,0},{1,13},{5,9},{9,5},{13,1},{2,14},{6,10},... | collective-permute-start | bytes 104 | tf_op jit(solution)/shard_map/ppermute | solution.py:406
  6.4 0.0 collective-permute-start.1
  6.4 0.6 %collective-permute-start = (s32[8]{0:T(128)S(1)}, s32[8]{0:T(128)S(1)}, u32[]{:S(2)}, u32[]{:S(2)}) collective-permute-start(s32[8]{0:T(128)S(1)} %bitcast_add_fusion.refs_0_.code), channel_id=1, source_target_pairs={{0,4},{4,0},{8,12},{12,8},{1,5},{5,1},{9,13},{13,9},{2,6},{6,2},{1... | collective-permute-start | bytes 104 | tf_op jit(solution)/shard_map/ppermute | solution.py:406
  6.9 1.0 %shard_map.113.refs_4_ = bf16[8,32,512]{2,1,0:T(8,128)(2,1)S(1)} custom-call(bf16[8,32,512]{2,1,0:T(8,128)(2,1)} %bitcast.14), custom_call_target="tpu_custom_call" | custom-call | bytes 1048576 | tf_op jit(solution)/shard_map/pallas_call | solution.py:387
  7.9 0.0 collective-permute-done.2.refs_3_
  7.9 2.9 %collective-permute-done.1.refs_2_ = s32[8]{0:T(128)S(1)} collective-permute-done((s32[8]{0:T(128)S(1)}, s32[8]{0:T(128)S(1)}, u32[]{:S(2)}, u32[]{:S(2)}) %collective-permute-start.1) | collective-permute-done | bytes 64 | tf_op jit(solution)/shard_map/ppermute | solution.py:406
  10.8 0.0 collective-permute-done.refs_1_
  10.8 0.7 %shard_map.114 = (bf16[2,32,512]{2,1,0:T(8,128)(2,1)S(1)}, bf16[2,32,512]{2,1,0:T(8,128)(2,1)S(1)}, bf16[2,32,512]{2,1,0:T(8,128)(2,1)S(1)}, bf16[2,32,512]{2,1,0:T(8,128)(2,1)S(1)}) custom-call(s32[8]{0:T(128)S(1)} %bitcast_add_fusion.refs_0_.code, s32[8]{0:T(128)S(1)} %collective-permute-done.refs_1_, s32[8]{0:T(128)S(1)} %collective-permute-done.1.refs_2_, ...), custom_call_target="tpu_custom_call" | custom-call | bytes 1048576 | tf_op jit(solution)/shard_map/pallas_call | solution.py:387
  11.5 0.1 collective-permute-start.3
  11.6 2.1 %collective-permute-start.4 = (bf16[2,32,512]{2,1,0:T(8,128)(2,1)S(1)}, bf16[2,32,512]{2,1,0:T(8,128)(2,1)S(1)}, u32[]{:S(2)}, u32[]{:S(2)}) collective-permute-start(bf16[2,32,512]{2,1,0:T(8,128)(2,1)S(1)} %get-tuple-element.29), channel_id=1, source_target_pairs={{0,8},{4,12},{8,0},{12,4},{1,9},{5,13},{9,1},{13,5},{2,10},{6,14},... | collective-permute-start | bytes 196616 | tf_op jit(solution)/shard_map/ppermute | solution.py:401
  13.7 2.3 %collective-permute-start.5 = (bf16[2,32,512]{2,1,0:T(8,128)(2,1)S(1)}, bf16[2,32,512]{2,1,0:T(8,128)(2,1)S(1)}, u32[]{:S(2)}, u32[]{:S(2)}) collective-permute-start(bf16[2,32,512]{2,1,0:T(8,128)(2,1)S(1)} %get-tuple-element.30), channel_id=1, source_target_pairs={{0,12},{4,8},{8,4},{12,0},{1,13},{5,9},{9,5},{13,1},{2,14},{6,10},... | collective-permute-start | bytes 196616 | tf_op jit(solution)/shard_map/ppermute | solution.py:401
  16.0 2.4 %shard_map.115 = (bf16[4,768,256]{2,1,0:T(8,128)(2,1)S(1)}, bf16[256,256]{1,0:T(8,128)(2,1)S(1)}, bf16[192,192]{1,0:T(8,128)(2,1)S(1)}, bf16[64,64]{1,0:T(8,128)...) custom-call(f32[3,1,9]{2,1,0:T(1,128)} %bitcast.15, ...), custom_call_target="tpu_custom_call" | custom-call | bytes 1048576 | tf_op jit(solution)/shard_map/pallas_call | solution.py:387
  18.4 0.0 collective-permute-done.3.refs_4_
  18.4 0.0 collective-permute-done.4.refs_5_
  18.4 1.5 %collective-permute-done.5.refs_6_ = bf16[2,32,512]{2,1,0:T(8,128)(2,1)S(1)} collective-permute-done((bf16[2,32,512]{2,1,0:T(8,128)(2,1)S(1)}, bf16[2,32,512]{2,1,0:T(8,128)(2,1)S(1)}, u32[]{:S(2)}, u32[]{:S(2)}) %collective-permute-start.5) | collective-permute-done | bytes 65568 | tf_op jit(solution)/shard_map/ppermute | solution.py:401
  19.9 1.1 %shard_map.116 = (bf16[256,640]{1,0:T(8,128)(2,1)S(1)}, bf16[16,640]{1,0:T(8,128)(2,1)S(1)}, bf16[256,128]{1,0:T(8,128)(2,1)S(1)}, bf16[16,128]{1,0:T(8,128)(2,1)S(1)}) custom-call(s32[8]{0:T(128)S(1)} %bitcast_add_fusion.refs_0_.code, bf16[256,256]{1,0:T(8,128)(2,1)S(1)} %get-tuple-element.26.refs_1_, bf16[8,256,128]{2,1,0:T(8,128)(2,1)S(1)} %get-tuple-element.27.refs_2_, ...), custom_call_target="tpu_custom_call" | custom-call | bytes 1048576 | tf_op jit(solution)/shard_map/pallas_call | solution.py:387
  21.0 0.1 collective-permute-start.6
  21.0 1.6 %collective-permute-start.7 = (bf16[16,640]{1,0:T(8,128)(2,1)S(1)}, bf16[16,640]{1,0:T(8,128)(2,1)S(1)}, u32[]{:S(2)}, u32[]{:S(2)}) collective-permute-start(bf16[16,640]{1,0:T(8,128)(2,1)S(1)} %get-tuple-element.33), channel_id=1, source_target_pairs={{0,2},{2,0},{1,3},{3,1},{4,6},{6,4},{5,7},{7,5},{8,10},{10,8},{9,1... | collective-permute-start | bytes 61448 | tf_op jit(solution)/shard_map/ppermute | solution.py:459
  22.6 0.3 collective-permute-start.8
  22.9 0.0 collective-permute-done.6.left.right
  22.9 1.3 %shard_map.117 = (f32[192,512]{1,0:T(8,128)S(1)}, bf16[192,512]{1,0:T(8,128)(2,1)S(1)}) custom-call(bf16[256,640]{1,0:T(8,128)(2,1)S(1)} %get-tuple-element.31.image, bf16[256,128]{1,0:T(8,128)(2,1)S(1)} %collective-permute-done.6.left.right, bf16[256,128]{1,0:T(8,128)(2,1)S(1)} %collective-permute-done.6.left.right, ...), custom_call_target="tpu_custom_call" | custom-call | bytes 1048576 | tf_op jit(solution)/shard_map/pallas_call | solution.py:387
  24.2 1.4 %collective-permute-done.8.top_left.top_right.bottom_left.bottom_right = bf16[16,128]{1,0:T(8,128)(2,1)S(1)} collective-permute-done((bf16[16,128]{1,0:T(8,128)(2,1)S(1)}, bf16[16,128]{1,0:T(8,128)(2,1)S(1)}, u32[]{:S(2)}, u32[]{:S(2)}) %collective-permute-start.8) | collective-permute-done | bytes 4128 | tf_op jit(solution)/shard_map/ppermute | solution.py:460
  25.6 1.4 %shard_map.118 = (f32[64,512]{1,0:T(8,128)S(1)}, bf16[2,32,512]{2,1,0:T(8,128)(2,1)S(1)}, bf16[2,32,512]{2,1,0:T(8,128)(2,1)S(1)}, bf16[2,32,512]{2,1,0:T(8,128)(2,1)S(1)}, bf16[2,32,512]{2,1,0:T(8,128)(2,1)S(1)}) custom-call(bf16[256,640]{1,0:T(8,128)(2,1)S(1)} %get-tuple-element.31.image, bf16[256,128]{1,0:T(8,128)(2,1)S(1)} %collective-permute-done.6.left.right, ...), custom_call_target="tpu_custom_call" | custom-call | bytes 1048576 | tf_op jit(solution)/shard_map/pallas_call | solution.py:387
  27.1 0.8 %collective-permute-start.9 = (bf16[2,32,512]{2,1,0:T(8,128)(2,1)S(1)}, bf16[2,32,512]{2,1,0:T(8,128)(2,1)S(1)}, u32[]{:S(2)}, u32[]{:S(2)}) collective-permute-start(bf16[2,32,512]{2,1,0:T(8,128)(2,1)S(1)} %get-tuple-element.45), channel_id=1, source_target_pairs={{0,4},{4,0},{8,12},{12,8},{1,5},{5,1},{9,13},{13,9},{2,6},{6,2},{1... | collective-permute-start | bytes 196616 | tf_op jit(solution)/shard_map/ppermute | solution.py:401
  27.9 2.0 %collective-permute-start.10 = (bf16[2,32,512]{2,1,0:T(8,128)(2,1)S(1)}, bf16[2,32,512]{2,1,0:T(8,128)(2,1)S(1)}, u32[]{:S(2)}, u32[]{:S(2)}) collective-permute-start(bf16[2,32,512]{2,1,0:T(8,128)(2,1)S(1)} %get-tuple-element.46), channel_id=1, source_target_pairs={{0,8},{4,12},{8,0},{12,4},{1,9},{5,13},{9,1},{13,5},{2,10},{6,14},... | collective-permute-start | bytes 196616 | tf_op jit(solution)/shard_map/ppermute | solution.py:401
  29.9 1.6 %collective-permute-start.11 = (bf16[2,32,512]{2,1,0:T(8,128)(2,1)S(1)}, bf16[2,32,512]{2,1,0:T(8,128)(2,1)S(1)}, u32[]{:S(2)}, u32[]{:S(2)}) collective-permute-start(bf16[2,32,512]{2,1,0:T(8,128)(2,1)S(1)} %get-tuple-element.47), channel_id=1, source_target_pairs={{0,12},{4,8},{8,4},{12,0},{1,13},{5,9},{9,5},{13,1},{2,14},{6,10},... | collective-permute-start | bytes 196616 | tf_op jit(solution)/shard_map/ppermute | solution.py:401
  31.5 0.8 %maximum_bitcast_fusion = f32[1,256,512]{2,1,0:T(8,128)} fusion(f32[32,512]{1,0:T(8,128)S(1)} %get-tuple-element.49, f32[192,512]{1,0:T(8,128)S(1)} %get-tuple-element.43, f32[32,512]{1,0:T(8,128)S(1)} %get-tuple-element.48), kind=kLoop, calls=%fused_computation | loop fusion | flops 262144 | bytes 1048576 | tf_op jit(solution)/shard_map/broadcast_in_dim | solution.py:511
  32.4 0.0 collective-permute-done.9.refs_5_
  32.4 3.8 %collective-permute-done.10.refs_6_ = bf16[2,32,512]{2,1,0:T(8,128)(2,1)S(1)} collective-permute-done((bf16[2,32,512]{2,1,0:T(8,128)(2,1)S(1)}, bf16[2,32,512]{2,1,0:T(8,128)(2,1)S(1)}, u32[]{:S(2)}, u32[]{:S(2)}) %collective-permute-start.10) | collective-permute-done | bytes 65568 | tf_op jit(solution)/shard_map/ppermute | solution.py:401
  36.2 0.0 collective-permute-done.11.refs_7_
  36.2 1.6 %shard_map.119 = f32[8,32,512]{2,1,0:T(8,128)} custom-call(s32[8]{0:T(128)S(1)} %bitcast_add_fusion.refs_0_.code, s32[8]{0:T(128)S(1)} %collective-permute-done.refs_1_, s32[8]{0:T(128)S(1)} %collective-permute-done.1.refs_2_, s32[8]{0:T(128)S(1)} %collective-permute-done.2.refs_3_, bf16[2,32,512]{2,1,0:T(8,128)(2,1)S(1)} %get-tuple-element.44.refs_4_, ...), custom_call_target="tpu_custom_call" | custom-call | bytes 1048576 | tf_op jit(solution)/shard_map/pallas_call | solution.py:387
  (4 shorter events, 0.0 us)
Async XLA Ops:
  1.3 6.6 %collective-permute-start.2 = (s32[8]{0:T(128)S(1)}, s32[8]{0:T(128)S(1)}, u32[]{:S(2)}, u32[]{:S(2)}) collective-permute-start(s32[8]{0:T(128)S(1)} %bitcast_add_fusion.refs_0_.code), channel_id=1, source_target_pairs={{0,12},{4,8},{8,4},{12,0},{1,13},{5,9},{9,5},{13,1},{2,14},{6,10},... | collective-permute-start | bytes 104 | tf_op jit(solution)/shard_map/ppermute | solution.py:406
  6.4 4.4 %collective-permute-start.1 = (s32[8]{0:T(128)S(1)}, s32[8]{0:T(128)S(1)}, u32[]{:S(2)}, u32[]{:S(2)}) collective-permute-start(s32[8]{0:T(128)S(1)} %bitcast_add_fusion.refs_0_.code), channel_id=1, source_target_pairs={{0,8},{4,12},{8,0},{12,4},{1,9},{5,13},{9,1},{13,5},{2,10},{6,14},... | collective-permute-start | bytes 104 | tf_op jit(solution)/shard_map/ppermute | solution.py:406
  6.4 4.4 %collective-permute-start = (s32[8]{0:T(128)S(1)}, s32[8]{0:T(128)S(1)}, u32[]{:S(2)}, u32[]{:S(2)}) collective-permute-start(s32[8]{0:T(128)S(1)} %bitcast_add_fusion.refs_0_.code), channel_id=1, source_target_pairs={{0,4},{4,0},{8,12},{12,8},{1,5},{5,1},{9,13},{13,9},{2,6},{6,2},{1... | collective-permute-start | bytes 104 | tf_op jit(solution)/shard_map/ppermute | solution.py:406
  11.5 6.8 %collective-permute-start.3 = (bf16[2,32,512]{2,1,0:T(8,128)(2,1)S(1)}, bf16[2,32,512]{2,1,0:T(8,128)(2,1)S(1)}, u32[]{:S(2)}, u32[]{:S(2)}) collective-permute-start(bf16[2,32,512]{2,1,0:T(8,128)(2,1)S(1)} %get-tuple-element.28), channel_id=1, source_target_pairs={{0,4},{4,0},{8,12},{12,8},{1,5},{5,1},{9,13},{13,9},{2,6},{6,2},{1... | collective-permute-start | bytes 196616 | tf_op jit(solution)/shard_map/ppermute | solution.py:401
  11.6 6.8 %collective-permute-start.4 = (bf16[2,32,512]{2,1,0:T(8,128)(2,1)S(1)}, bf16[2,32,512]{2,1,0:T(8,128)(2,1)S(1)}, u32[]{:S(2)}, u32[]{:S(2)}) collective-permute-start(bf16[2,32,512]{2,1,0:T(8,128)(2,1)S(1)} %get-tuple-element.29), channel_id=1, source_target_pairs={{0,8},{4,12},{8,0},{12,4},{1,9},{5,13},{9,1},{13,5},{2,10},{6,14},... | collective-permute-start | bytes 196616 | tf_op jit(solution)/shard_map/ppermute | solution.py:401
  13.7 6.2 %collective-permute-start.5 = (bf16[2,32,512]{2,1,0:T(8,128)(2,1)S(1)}, bf16[2,32,512]{2,1,0:T(8,128)(2,1)S(1)}, u32[]{:S(2)}, u32[]{:S(2)}) collective-permute-start(bf16[2,32,512]{2,1,0:T(8,128)(2,1)S(1)} %get-tuple-element.30), channel_id=1, source_target_pairs={{0,12},{4,8},{8,4},{12,0},{1,13},{5,9},{9,5},{13,1},{2,14},{6,10},... | collective-permute-start | bytes 196616 | tf_op jit(solution)/shard_map/ppermute | solution.py:401
  21.0 1.9 %collective-permute-start.6 = (bf16[256,128]{1,0:T(8,128)(2,1)S(1)}, bf16[256,128]{1,0:T(8,128)(2,1)S(1)}, u32[]{:S(2)}, u32[]{:S(2)}) collective-permute-start(bf16[256,128]{1,0:T(8,128)(2,1)S(1)} %get-tuple-element.32), channel_id=1, source_target_pairs={{0,1},{1,0},{2,3},{3,2},{4,5},{5,4},{6,7},{7,6},{8,9},{9,8},{10,11... | collective-permute-start | bytes 196616 | tf_op jit(solution)/shard_map/ppermute | solution.py:458
  21.0 4.6 %collective-permute-start.7 = (bf16[16,640]{1,0:T(8,128)(2,1)S(1)}, bf16[16,640]{1,0:T(8,128)(2,1)S(1)}, u32[]{:S(2)}, u32[]{:S(2)}) collective-permute-start(bf16[16,640]{1,0:T(8,128)(2,1)S(1)} %get-tuple-element.33), channel_id=1, source_target_pairs={{0,2},{2,0},{1,3},{3,1},{4,6},{6,4},{5,7},{7,5},{8,10},{10,8},{9,1... | collective-permute-start | bytes 61448 | tf_op jit(solution)/shard_map/ppermute | solution.py:459
  22.6 3.0 %collective-permute-start.8 = (bf16[16,128]{1,0:T(8,128)(2,1)S(1)}, bf16[16,128]{1,0:T(8,128)(2,1)S(1)}, u32[]{:S(2)}, u32[]{:S(2)}) collective-permute-start(bf16[16,128]{1,0:T(8,128)(2,1)S(1)} %get-tuple-element.34), channel_id=1, source_target_pairs={{0,3},{3,0},{1,2},{2,1},{4,7},{7,4},{5,6},{6,5},{8,11},{11,8},{9,1... | collective-permute-start | bytes 12296 | tf_op jit(solution)/shard_map/ppermute | solution.py:460
  22.9 2.7 %copy-start = (bf16[96,64]{1,0:T(8,128)(2,1)S(1)}, bf16[96,64]{1,0:T(8,128)(2,1)}, u32[]{:S(2)}) copy-start(bf16[96,64]{1,0:T(8,128)(2,1)} %constant.10.clone.bands) | copy-start | bytes 36868
  27.1 5.3 %collective-permute-start.9 = (bf16[2,32,512]{2,1,0:T(8,128)(2,1)S(1)}, bf16[2,32,512]{2,1,0:T(8,128)(2,1)S(1)}, u32[]{:S(2)}, u32[]{:S(2)}) collective-permute-start(bf16[2,32,512]{2,1,0:T(8,128)(2,1)S(1)} %get-tuple-element.45), channel_id=1, source_target_pairs={{0,4},{4,0},{8,12},{12,8},{1,5},{5,1},{9,13},{13,9},{2,6},{6,2},{1... | collective-permute-start | bytes 196616 | tf_op jit(solution)/shard_map/ppermute | solution.py:401
  27.9 8.3 %collective-permute-start.10 = (bf16[2,32,512]{2,1,0:T(8,128)(2,1)S(1)}, bf16[2,32,512]{2,1,0:T(8,128)(2,1)S(1)}, u32[]{:S(2)}, u32[]{:S(2)}) collective-permute-start(bf16[2,32,512]{2,1,0:T(8,128)(2,1)S(1)} %get-tuple-element.46), channel_id=1, source_target_pairs={{0,8},{4,12},{8,0},{12,4},{1,9},{5,13},{9,1},{13,5},{2,10},{6,14},... | collective-permute-start | bytes 196616 | tf_op jit(solution)/shard_map/ppermute | solution.py:401
  29.9 6.3 %collective-permute-start.11 = (bf16[2,32,512]{2,1,0:T(8,128)(2,1)S(1)}, bf16[2,32,512]{2,1,0:T(8,128)(2,1)S(1)}, u32[]{:S(2)}, u32[]{:S(2)}) collective-permute-start(bf16[2,32,512]{2,1,0:T(8,128)(2,1)S(1)} %get-tuple-element.47), channel_id=1, source_target_pairs={{0,12},{4,8},{8,4},{12,0},{1,13},{5,9},{9,5},{13,1},{2,14},{6,10},... | collective-permute-start | bytes 196616 | tf_op jit(solution)/shard_map/ppermute | solution.py:401

commit v2 on v1

--- a/solution.py
+++ b/solution.py
@@ -89,7 +89,7 @@
 
 
 def slots_of(code_ref, me, strips, capacity, xor):
-    owners = [lax.div(code_ref[q], jnp.int32(strips)) for q in range(strips)]
+    owners = [lax.div(code_ref[0, q], jnp.int32(strips)) for q in range(strips)]
     slots = []
     for q in range(strips):
         rank = jnp.int32(0)
@@ -100,7 +100,6 @@
 
 
 def pick_kernel(n, capacity, strips, xor, *refs):
-    codes, template, outs = refs[:-2] if xor else refs[:1], None, None
     if xor:
         codes, template, outs = refs[:n], refs[n], refs[n + 1 :]
     else:
@@ -110,9 +109,31 @@
         found, _ = matches(codes[g], None if xor else g, me, strips, capacity)
         for j in range(capacity):
             if xor:
-                outs[g][j] = template[found[j]]
+                outs[g][j] = template[strip_rows_at(found[j], template.shape[0] // strips), :]
             else:
-                outs[0][g * capacity + j] = template[found[j]]
+                outs[0][g * capacity + j] = template[strip_rows_at(found[j], template.shape[0] // strips), :]
+
+
+def two_of(value, owner, strips):
+    lane = lax.broadcasted_iota(jnp.int32, value.shape, 1).astype(F32)
+    low = (owner * strips).astype(F32)
+    hit = (value >= low) & (value < low + strips)
+    key = lane * strips + (value - low)
+    first = jnp.min(jnp.where(hit, key, 1024.0)).astype(jnp.int32)
+    last = jnp.max(jnp.where(hit, key, 0.0)).astype(jnp.int32)
+    return lax.rem(first, jnp.int32(strips)), lax.rem(last, jnp.int32(strips))
+
+
+def strip_rows_at(strip, strip_rows):
+    return pl.ds(pl.multiple_of(strip * strip_rows, strip_rows), strip_rows)
+
+
+def pick_two_kernel(strips, strip_rows, *refs):
+    count = len(refs) // 2
+    template = refs[count]
+    for code, out in zip(refs[:count], refs[count + 1 :]):
+        for j, strip in enumerate(two_of(code[...].astype(F32), lax.axis_index("ccd"), strips)):
+            out[j] = template[strip_rows_at(strip, strip_rows), :]
 
 
 def load_kernel(source, target, sem):
@@ -121,10 +142,26 @@
     copy.wait()
 
 
-def prepare_kernel(strips, strip_rows, tiles, amp_count, coefs_in, shifts_in, fractions_in, bands_in, science_in,
-                   row_band_in, after, de, forward, mid, edge, spread, gather, science, row_band,
-                   coefs, shifts, fractions, bands, sems):
+def turned(base, first, rows):
+    return pltpu.roll(jnp.broadcast_to(base, (rows, base.shape[1])), first, 1, stride=1, stride_axis=0)
+
+
+def base_row(taps, q, start, sign, size):
+    lane = lax.broadcasted_iota(jnp.int32, (1, size), 1)
+    value = jnp.zeros((1, size), F32)
+    for t in range(TAPS):
+        at = lax.rem(start + sign * (t - 2) + size, jnp.int32(size))
+        value = jnp.where(lane == at, jnp.broadcast_to(taps[t : t + 1, q : q + 1], (1, size)), value)
+    return value
+
+
+def prepare_kernel(n, capacity, strips, strip_rows, tiles, amp_count, xor, two, coefs_in, shifts_in, fractions_in,
+                   bands_in, science_in, row_band_in, after, code, *refs):
     del after
+    if two:
+        own_code, template, own = refs[:3]
+        refs = refs[3:]
+    de, forward, backward, spread, gather, science, row_band, coefs, shifts, fractions, bands, sems = refs
     pairs = [(fractions_in, fractions), (shifts_in, shifts), (coefs_in, coefs),
              (bands_in, bands), (row_band_in, row_band), (science_in, science)]
     copies = [pltpu.make_async_copy(source, target, sems.at[i]) for i, (source, target) in enumerate(pairs)]
@@ -133,58 +170,85 @@
     for copy in copies[:2]:
         copy.wait()
     taps = [lanczos_taps(fractions[d : d + 1, :]) for d in range(2)]
-
-    def operator(out, chosen, transposed):
-        size = out.shape[1]
-        lane = lax.broadcasted_iota(jnp.int32, (strip_rows, size), 1)
-        row = lax.broadcasted_iota(jnp.int32, (strip_rows, size), 0)
-        for place, q in enumerate(chosen):
-            low = place * strip_rows
-            within = (lane >= low) & (lane < low + strip_rows)
-            step = lane - low - row
-            offset = (-step if transposed else step) - shifts[0, q]
-            offset = jnp.where(within, offset, jnp.int32(1 << 20))
-            value = jnp.zeros((strip_rows, size), F32)
-            for t in range(TAPS):
-                tap = jnp.broadcast_to(taps[0][t : t + 1, q : q + 1], (strip_rows, size))
-                value = jnp.where(offset == t - 2, tap, value)
-            out[pl.ds(low, strip_rows), :] = value.astype(BF16)
-
-    operator(forward, range(strips), False)
-    operator(mid, range(1, strips - 1), True)
-    operator(edge, (0, strips - 1), True)
+    me = lax.axis_index("ccd")
+    band, slots = strips * strip_rows, n * capacity
+    size = slots * strip_rows
+    if slots != strips:
+        backward[...] = jnp.zeros(backward.shape, BF16)
+    forward_lane = lax.broadcasted_iota(jnp.int32, (strip_rows, size), 1)
+    backward_lane = lax.broadcasted_iota(jnp.int32, (strip_rows, band), 1)
+    for q, slot in enumerate(slots_of(code, me, strips, capacity, xor)):
+        low, high = slot * strip_rows, q * strip_rows
+        value = turned(base_row(taps[0], q, low + shifts[0, q], 1, size), 0, strip_rows)
+        value = jnp.where((forward_lane >= low) & (forward_lane < low + strip_rows), value, 0.0)
+        forward[high : high + strip_rows, :] = value.astype(BF16)
+        value = turned(base_row(taps[0], q, high - shifts[0, q], -1, band), 0, strip_rows)
+        value = jnp.where((backward_lane >= high) & (backward_lane < high + strip_rows), value, 0.0)
+        backward[strip_rows_at(slot, strip_rows), :] = value.astype(BF16)
+
+    if two:
+        for j, strip in enumerate(two_of(own_code[...].astype(F32), me, strips)):
+            own[j] = template[strip_rows_at(strip, strip_rows), :]
 
     rows = 160
-    away = lane_index(rows) - lax.broadcasted_iota(jnp.int32, (rows, LANES), 0)
-    for out, low, centre, sign in ((spread, 48, HALF_TILE, 1), (gather, 112, LANES, -1)):
-        size = out.shape[1]
+    away = lax.broadcasted_iota(jnp.int32, (rows, LANES), 0) - lane_index(rows)
+    for out, low, centre, sign in ((spread, 48, HALF_TILE, -1), (gather, 112, LANES, 1)):
+        within = (away >= centre - low - 8) & (away <= centre - low + 8)
+        end = out.shape[1]
         for q in range(strips):
-            step = -sign * (away + (centre - low)) - shifts[1, q]
-            value = jnp.zeros((rows, LANES), F32)
-            for t in range(TAPS):
-                tap = jnp.broadcast_to(taps[1][t : t + 1, q : q + 1], (rows, LANES))
-                value = jnp.where(step == t - 2, tap, value)
+            start = (low - centre) + sign * shifts[1, q] + LANES
+            value = turned(base_row(taps[1], q, start, sign, LANES), 0, rows)
             out[q, 0:low, :] = jnp.zeros((low, LANES), BF16)
-            out[q, low : low + rows, :] = value.astype(BF16)
-            out[q, low + rows : size, :] = jnp.zeros((size - low - rows, LANES), BF16)
+            out[q, low : low + rows, :] = jnp.where(within, value, 0.0).astype(BF16)
+            out[q, low + rows : end, :] = jnp.zeros((end - low - rows, LANES), BF16)
     for copy in copies[2:4]:
         copy.wait()
     amp = lax.axis_index("amp")
     width = tiles * LANES
-    for first in range(KINDS):
-        for half in range(2):
-            rows = pl.ds(half * LANES, LANES)
-            at = pl.ds((half * KINDS + first) * LANES, LANES)
-            band = [bands[second, rows, :].astype(F32) for second in range(KINDS)]
-            e = sum(band[b] * coefs[2, 0, first * KINDS + b] for b in range(KINDS)).astype(BF16)
+    rows = 80
+    for half in range(2):
+        low = half * LANES + (0 if half else LANES - rows)
+        for first in range(KINDS):
+            at = (half * KINDS + first) * LANES
+            band_rows = [bands[second, low : low + rows, :].astype(F32) for second in range(KINDS)]
+            e = sum(band_rows[b] * coefs[2, 0, first * KINDS + b] for b in range(KINDS)).astype(BF16)
+            empty = jnp.zeros((LANES - rows, 2 * LANES), BF16)
+            begin = at + (0 if half else LANES - rows)
             for tile in range(tiles):
                 column = lane_index(1) + (amp * width + tile * LANES)
                 px = (column.astype(F32) + 0.5) / (width * amp_count) * 2.0 - 1.0
                 weight = [coefs[0, 0, first * KINDS + b] + coefs[1, 0, first * KINDS + b] * px for b in range(KINDS)]
-                de[tile, at, 0:LANES] = sum(band[b] * weight[b] for b in range(KINDS)).astype(BF16)
-                de[tile, at, LANES : 2 * LANES] = e
+                d = sum(band_rows[b] * weight[b] for b in range(KINDS)).astype(BF16)
+                de[tile, begin : begin + rows, 0:LANES] = d
+                de[tile, begin : begin + rows, LANES : 2 * LANES] = e
+                hollow = at + (rows if half else 0)
+                de[tile, hollow : hollow + LANES - rows, :] = empty
     for copy in copies[4:]:
         copy.wait()
+
+
+def collect_kernel(n, capacity, strips, strip_rows, xor, two, after, *refs):
+    del after
+    out = refs[-1]
+    me = lax.axis_index("ccd")
+    size = n * capacity * strip_rows
+    lane = lax.broadcasted_iota(jnp.int32, (1, size), 1)
+    named = jnp.full(lane.shape, -1, jnp.int32)
+    for g in range(n):
+        if two:
+            found = two_of(refs[g][...].astype(F32), me, strips)
+        else:
+            found, total = matches(refs[g if xor else 0], None if xor else g, me, strips, capacity)
+            found = [jnp.where(total > j, strip, -1) for j, strip in enumerate(found)]
+        for j in range(capacity):
+            low = (g * capacity + j) * strip_rows
+            named = jnp.where((lane >= low) & (lane < low + strip_rows), found[j], named)
+    lane = lax.broadcasted_iota(jnp.int32, (strip_rows, size), 1)
+    row = lax.broadcasted_iota(jnp.int32, lane.shape, 0)
+    same_row = lax.rem(lane, jnp.int32(strip_rows)) == row
+    for p in range(strips):
+        value = jnp.where(same_row & (named == p), 1.0, 0.0)
+        out[p * strip_rows : (p + 1) * strip_rows, :] = value.astype(BF16)
 
 
 def clear_ends(ref, tiles):
@@ -193,28 +257,23 @@
     ref[:, (tiles + 1) * LANES : (tiles + 2) * LANES] = zero
 
 
-def warp_kernel(n, capacity, strips, strip_rows, tiles, xor, paired, *refs):
-    code, forward, spread = refs[:3]
-    if xor:
-        received, rest = refs[3 : 3 + n], refs[3 + n :]
+def stacked(refs):
+    parts = [ref[...].reshape(-1, ref.shape[-1]) for ref in refs]
+    return jnp.concatenate(parts, axis=0) if len(parts) > 1 else parts[0]
+
+
+def warp_kernel(n, strips, strip_rows, tiles, xor, paired, *refs):
+    forward, spread = refs[:2]
+    count = n if xor else 1
+    received, rest = refs[2 : 2 + count][::-1], refs[2 + count :]
+    if paired:
+        image, send_row, send_amp, send_diag, rows_done = rest
     else:
-        received, rest = refs[3:4], refs[4:]
-    if paired:
-        image, send_row, send_amp, send_diag, pool, fetched, rows_done = rest
-    else:
-        image, pool, fetched, rows_done = rest
-    me = lax.axis_index("ccd")
-    if xor:
-        for g in range(n):
-            pool[pl.ds(g * capacity, capacity)] = received[g][...]
-    else:
-        pool[...] = received[0][...]
-    for q, slot in enumerate(slots_of(code, me, strips, capacity, xor)):
-        fetched[pl.ds(q * strip_rows, strip_rows), :] = pool[slot]
+        image, rows_done = rest
     width = tiles * LANES
     clear_ends(rows_done, tiles)
     rows_done[:, LANES : LANES + width] = jnp.dot(
-        forward[...], fetched[...], preferred_element_type=F32
+        forward[...], stacked(received), preferred_element_type=F32
     ).astype(BF16)
     lane = lane_index(strip_rows)
     for q in range(strips):
@@ -277,8 +336,8 @@
     return (row.astype(F32) + 0.5) / (band * row_count) * 2.0 - 1.0
 
 
-def mid_kernel(strips, strip_rows, tiles, row_count, amp_count, image, left, right, science, de, bands, operator,
-               gather, diff, contribution, across, lowered, columns):
+def mid_kernel(strips, strip_rows, tiles, row_count, amp_count, image, left, right, science, de, bands, gather,
+               diff, columns, across, lowered):
     band = strips * strip_rows
     count = band - 2 * strip_rows
     rows = slice(strip_rows - MARGIN, band - strip_rows + MARGIN)
@@ -296,14 +355,13 @@
     )
     for q in range(1, strips - 1):
         columns_returned(lowered, columns, (q - 1) * strip_rows, gather[q], strip_rows, tiles)
-    contribution[...] = jnp.dot(operator[...], columns[...], preferred_element_type=F32).astype(BF16)
 
 
 def edge_kernel(n, capacity, strips, strip_rows, tiles, row_count, amp_count, xor, image, left, right, top, bottom,
-                top_left, top_right, bottom_left, bottom_right, science, de, bands, operator, gather, code,
-                contribution_mid, diff, *rest):
+                top_left, top_right, bottom_left, bottom_right, science, de, bands, backward, gather,
+                columns_mid, diff, *rest):
     outs = rest[: n if xor else 1]
-    across, lowered, columns, pool = rest[len(outs) :]
+    across, lowered, columns = rest[len(outs) :]
     band = strips * strip_rows
     inner = strip_rows + MARGIN
     row = lax.axis_index("row")
@@ -335,38 +393,26 @@
     subtracted(edge_science, across, de, store, 2 * strip_rows, tiles, place)
     columns_returned(lowered, columns, 0, gather[0], strip_rows, tiles)
     columns_returned(lowered, columns, strip_rows, gather[strips - 1], strip_rows, tiles)
-    ends = jnp.dot(operator[...], columns[...], preferred_element_type=F32).astype(BF16)
-    me = lax.axis_index("ccd")
-    target = pool if xor else outs[0]
-    if n * capacity != strips:
-        target[...] = jnp.zeros(target.shape, BF16)
-    for q, slot in enumerate(slots_of(code, me, strips, capacity, xor)):
-        if q == 0:
-            target[slot] = ends[0:strip_rows]
-        elif q == strips - 1:
-            target[slot] = ends[strip_rows:]
-        else:
-            target[slot] = contribution_mid[(q - 1) * strip_rows : q * strip_rows, :]
-    if xor:
-        for g in range(n):
-            outs[g][...] = pool[pl.ds(g * capacity, capacity)]
-
-
-def sum_kernel(n, capacity, strips, xor, *refs):
-    if xor:
-        codes, returned, stack = refs[:n], refs[n : 2 * n], refs[2 * n]
-    else:
-        codes, returned, stack = [refs[0]] * n, [refs[1]] * n, refs[2]
-    me = lax.axis_index("ccd")
-    stack[...] = jnp.zeros(stack.shape, F32)
-    for g in range(n):
-        found, count = matches(codes[g], None if xor else g, me, strips, capacity)
-        for j in range(capacity):
-
-            @pl.when(count > j)
-            def _(g=g, j=j, strip=found[j]):
-                at = j if xor else g * capacity + j
-                stack[strip] += returned[g][at].astype(F32)
+    whole = jnp.concatenate([columns[:strip_rows, :], columns_mid[...], columns[strip_rows:, :]], axis=0)
+    result = jnp.dot(backward[...], whole, preferred_element_type=F32).astype(BF16)
+    size = capacity * strip_rows * (1 if xor else n)
+    for g, out in enumerate(outs):
+        out[...] = result[g * size : (g + 1) * size].reshape(out.shape)
+
+
+def sum_kernel(collect, *refs):
+    *returned, stack, total, sems = refs
+    values = stacked(returned[::-1])
+    copies = []
+    half = total.shape[0] // 2
+    for i in range(2):
+        rows = pl.ds(i * half, half)
+        total[rows, :] = jnp.dot(collect[rows, :], values, preferred_element_type=F32)
+        copy = pltpu.make_async_copy(total.at[rows], stack.at[rows], sems.at[i])
+        copy.start()
+        copies.append(copy)
+    for copy in copies:
+        copy.wait()
 
 
 def body(science, template, owners, patch_strip, shifts, fractions, coefs):
@@ -379,19 +425,21 @@
     tiles = width // LANES
     padded = width + LANES
     xor = n in (2, 4)
+    two = xor and capacity == 2 and strips == 2 * n
     paired = row_count == 2 and amp_count == 2
     swap = [(0, 1), (1, 0)]
     strip_shape = (capacity, strip_rows, width)
 
-    def call(kernel, out_shape, operands, spaces, scratch=(), megabytes=8, flops=0):
+    def call(kernel, out_shape, operands, spaces, scratch=(), megabytes=8):
+        shapes = [jax.ShapeDtypeStruct(*s) if isinstance(s, tuple) else s for s in out_shape]
         return pl.pallas_call(
             kernel,
-            out_shape=[jax.ShapeDtypeStruct(s, d) for s, d in out_shape],
+            out_shape=shapes,
             in_specs=list(spaces),
-            out_specs=[VMEM] * len(out_shape),
+            out_specs=[VMEM if isinstance(s, tuple) else HBM for s in out_shape],
             scratch_shapes=[pltpu.VMEM(*s) if isinstance(s, tuple) else s for s in scratch],
             compiler_params=pltpu.CompilerParams(vmem_limit_bytes=megabytes << 20),
-            cost_estimate=pl.CostEstimate(flops=flops, bytes_accessed=1 << 20, transcendentals=0),
+            cost_estimate=pl.CostEstimate(flops=0, bytes_accessed=1 << 20, transcendentals=0),
         )(*operands)
 
     def exchange(parts):
@@ -401,35 +449,48 @@
             lax.ppermute(parts[g], "ccd", [(i, i ^ g) for i in range(n)]) for g in range(1, n)
         ]
 
-    code = owners.reshape(strips) * strips + patch_strip.reshape(strips)
-    if xor:
-        codes = [code] + [lax.ppermute(code, "ccd", [(i, i ^ g) for i in range(n)]) for g in range(1, n)]
+    code = owners.reshape(1, strips) * strips + patch_strip.reshape(1, strips)
+    (template_rows,) = call(
+        load_kernel,
+        [((band, width), BF16)],
+        [in_hbm(template.reshape(band, width))],
+        [HBM],
+        [pltpu.SemaphoreType.DMA],
+    )
+
+    def exchanged(value, g):
+        return lax.ppermute(value, "ccd", [(i, i ^ g) for i in range(n)])
+
+    if two:
+        codes = [code] + [exchanged(code, g) for g in range(1, n)]
+        picked = call(
+            functools.partial(pick_two_kernel, strips, strip_rows),
+            [(strip_shape, BF16)] * (n - 1),
+            [*codes[1:], template_rows],
+            [VMEM] * n,
+        )
+    elif xor:
+        codes = [code.reshape(strips)] + [exchanged(code.reshape(strips), g) for g in range(1, n)]
         picked_shapes = [(strip_shape, BF16)] * n
     else:
-        codes = [lax.all_gather(code, "ccd", axis=0, tiled=True)]
+        codes = [lax.all_gather(code.reshape(strips), "ccd", axis=0, tiled=True)]
         picked_shapes = [((n * capacity, strip_rows, width), BF16)]
-    (template_strips,) = call(
-        load_kernel,
-        [((strips, strip_rows, width), BF16)],
-        [in_hbm(template.reshape(strips, strip_rows, width))],
-        [HBM],
-        [pltpu.SemaphoreType.DMA],
-    )
-    picked = call(
-        functools.partial(pick_kernel, n, capacity, strips, xor),
-        picked_shapes,
-        [*codes, template_strips],
-        [SMEM] * len(codes) + [VMEM],
-    )
+    if not two:
+        picked = call(
+            functools.partial(pick_kernel, n, capacity, strips, xor),
+            picked_shapes,
+            [*codes, template_rows],
+            [SMEM] * len(codes) + [VMEM],
+        )
     mid_rows = band - 2 * strip_rows
     mid_bands = jnp.asarray(row_bands(mid_rows))
-    de, forward, mid_operator, edge_operator, spread, gather, science, mid_bands = call(
-        functools.partial(prepare_kernel, strips, strip_rows, tiles, amp_count),
-        [
+    slot_rows = n * capacity * strip_rows
+    *own, de, forward, backward, spread, gather, science, mid_bands = call(
+        functools.partial(prepare_kernel, n, capacity, strips, strip_rows, tiles, amp_count, xor, two),
+        ([(strip_shape, BF16)] if two else []) + [
             ((tiles, 2 * KINDS * LANES, 2 * LANES), BF16),
-            ((band, band), BF16),
-            ((mid_rows, mid_rows), BF16),
-            ((2 * strip_rows, 2 * strip_rows), BF16),
+            ((band, slot_rows), BF16),
+            ((slot_rows, band), BF16),
             ((strips, 2 * LANES, LANES), BF16),
             ((strips, 3 * LANES, LANES), BF16),
             ((band, width), F32),
@@ -437,21 +498,25 @@
         ],
         [in_hbm(value) for value in (
             coefs.transpose(1, 0, 2), shifts.reshape(2, strips), fractions.reshape(2, strips),
-            jnp.asarray(column_bands()), science.reshape(band, width), mid_bands)] + [picked[0]],
-        [HBM] * 6 + [VMEM],
+            jnp.asarray(column_bands()), science.reshape(band, width), mid_bands)]
+        + [picked[-1], code] + ([code, template_rows] if two else []),
+        [HBM] * 6 + [VMEM, SMEM] + [VMEM] * (2 if two else 0),
         [pltpu.SMEM((3, 1, 9), F32), pltpu.SMEM((2, strips), jnp.int32),
          ((2, strips), F32), ((KINDS, 2 * LANES, LANES), BF16), pltpu.SemaphoreType.DMA((6,))],
-    )
-    received = exchange(picked)
+        megabytes=10,
+    )
+    if two:
+        received = exchange([*own, *picked])[::-1]
+    else:
+        received = exchange(picked)[::-1]
     image_shape = ((band, padded), BF16)
     halo_shapes = [((MARGIN, padded), BF16), ((band, LANES), BF16), ((MARGIN, LANES), BF16)]
     warped = call(
-        functools.partial(warp_kernel, n, capacity, strips, strip_rows, tiles, xor, paired),
+        functools.partial(warp_kernel, n, strips, strip_rows, tiles, xor, paired),
         [image_shape] + (halo_shapes if paired else []),
-        [code, forward, spread, *received],
-        [SMEM, VMEM, VMEM] + [VMEM] * len(received),
-        [((n * capacity, strip_rows, width), BF16), ((band, width), BF16),
-         ((band, padded + LANES), BF16)],
+        [forward, spread, *received],
+        [VMEM] * (2 + len(received)),
+        [((band, padded + LANES), BF16)],
     )
     image = warped[0]
     if paired:
@@ -480,32 +545,36 @@
         bottom_left = moved(first[:, padded - LANES :], -1, 1)
         bottom_right = moved(first[:, :LANES], -1, -1)
 
-    diff_mid, contribution_mid = call(
+    diff_mid, columns_mid = call(
         functools.partial(mid_kernel, strips, strip_rows, tiles, row_count, amp_count),
         [((mid_rows, width), F32), ((mid_rows, width), BF16)],
-        [image, left, right, science, de, mid_bands, mid_operator, gather],
-        [VMEM] * 8,
-        [((mid_rows, (tiles + 1) * KINDS * LANES), BF16), ((mid_rows, padded + LANES), BF16),
-         ((mid_rows, width), BF16)],
-        megabytes=12,
-    )
-    outgoing_shapes = picked_shapes
+        [image, left, right, science, de, mid_bands, gather],
+        [VMEM] * 7,
+        [((mid_rows, (tiles + 1) * KINDS * LANES), BF16), ((mid_rows, padded + LANES), BF16)],
+    )
+    outgoing_shapes = [(strip_shape, BF16)] * n if xor else [((n * capacity, strip_rows, width), BF16)]
     diff_edge, *outgoing = call(
         functools.partial(edge_kernel, n, capacity, strips, strip_rows, tiles, row_count, amp_count, xor),
         [((2 * strip_rows, width), F32)] + outgoing_shapes,
         [image, left, right, top, bottom, top_left, top_right, bottom_left, bottom_right, science, de,
-         jnp.asarray(row_bands(strip_rows)), edge_operator, gather, code, contribution_mid],
-        [VMEM] * 14 + [SMEM, VMEM],
+         jnp.asarray(row_bands(strip_rows)), backward, gather, columns_mid],
+        [VMEM] * 15,
         [((2 * strip_rows, (tiles + 1) * KINDS * LANES), BF16), ((2 * strip_rows, padded + LANES), BF16),
-         ((2 * strip_rows, width), BF16), ((n * capacity, strip_rows, width), BF16)],
-        megabytes=12,
-    )
-    returned = exchange(outgoing)
+         ((2 * strip_rows, width), BF16)],
+    )
+    returned = exchange(outgoing)[::-1]
+    (collect,) = call(
+        functools.partial(collect_kernel, n, capacity, strips, strip_rows, xor, two),
+        [((band, slot_rows), BF16)],
+        [outgoing[0], *codes],
+        [VMEM] + [VMEM if two else SMEM] * len(codes),
+    )
     (stack,) = call(
-        functools.partial(sum_kernel, n, capacity, strips, xor),
-        [((strips, strip_rows, width), F32)],
-        [*codes, *returned],
-        [SMEM] * len(codes) + [VMEM] * len(returned),
+        sum_kernel,
+        [pltpu.HBM((band, width), F32)],
+        [collect, *returned],
+        [VMEM] * (1 + len(returned)),
+        [((band, width), F32), pltpu.SemaphoreType.DMA((2,))],
     )
     difference = jnp.concatenate([diff_edge[:strip_rows], diff_mid, diff_edge[strip_rows:]])
     return difference[None], stack.reshape(template.shape)

time: 38 us -> 35.4 us (0.932)
  Pallas kernels: 9.48 us -> 7.37 us
  waiting for transfers between devices: 9.62 us -> 9.1 us
    pallas_call x7 -> x8, Pallas kernels: 9.48 us -> 7.37 us  [call(): pl.pallas_call(kernel, out_shape=shapes, in_specs=list(spaces), out_specs...]
    ppermute x6, waiting for transfers between devices: 5.33 us -> 4.61 us  [exchange(): lax.ppermute(parts[g], 'ccd', [(i, i ^ g) for i in range(n)])]
  transfers between devices with their start and end apart: 12 -> 12, of which waited for: 4 -> 5; matrix products, arithmetic and copies ran while one was open for 2% -> 2% of each run, Pallas kernels for 12% -> 14%
where the time goes in v2:
time: 35.4 us; the launch traced here: 35.2 us
  starting transfers between devices  16.5 us (47%)
  waiting for transfers between devices  9.1 us (26%)
  Pallas kernels  7.37 us (21%)
  other arithmetic  1.51 us (4%)
  between operations  0.73 us (2%)
    ppermute x6, starting transfers between devices, exchange(): lax.ppermute(parts[g], 'ccd', [(i, i ^ g) for i in range(n)])  8.9 us
    pallas_call x8, Pallas kernels, call(): pl.pallas_call(kernel, out_shape=shapes, in_specs=list(spaces), out_specs...  7.37 us
    ppermute x3, starting transfers between devices, exchanged(): return lax.ppermute(value, 'ccd', [(i, i ^ g) for i in range(n)])  5.62 us
    ppermute x6, waiting for transfers between devices, exchange(): lax.ppermute(parts[g], 'ccd', [(i, i ^ g) for i in range(n)])  4.61 us
    ppermute x3, waiting for transfers between devices, exchanged(): return lax.ppermute(value, 'ccd', [(i, i ^ g) for i in range(n)])  2.9 us
    ppermute x1, waiting for transfers between devices, body(): lax.ppermute(warped[3], ('row', 'amp'), [(0, 3), (3, 0), (1, 2), (2, 1)])  1.58 us
    ppermute x1, starting transfers between devices, body(): ends = lax.ppermute(warped[1], 'row', swap)  1.55 us
    broadcast_in_dim x1, other arithmetic, body(): return (difference[None], stack.reshape(template.shape))  0.83 us
  transfers between devices with their start and end apart: 12, of which 5 were waited for; matrix products, arithmetic and copies ran while one was open for 2% of the time, Pallas kernels for 14%

profile of v2, /device:TPU:0, one launch (start us, length us, event | category | flops | bytes accessed | tf_op | source)
XLA Modules:
  0.0 35.2 jit_solution(13144809540534639341)
XLA Ops:
  0.6 0.7 %bitcast_add_fusion.code.refs_0_ = s32[1,8]{1,0:T(1,128)S(1)} fusion(s32[1,1,1,8]{3,2,1,0:T(1,128)} %param.13, s32[1,1,1,8,1]{3,4,2,1,0:T(1,128)} %param.12), kind=kLoop, calls=%fused_computation.1 | loop fusion | flops 16 | bytes 96 | tf_op jit(solution)/shard_map/add | solution.py:452
  1.3 5.0 %collective-permute-start.2 = (s32[1,8]{1,0:T(1,128)S(1)}, s32[1,8]{1,0:T(1,128)S(1)}, u32[]{:S(2)}, u32[]{:S(2)}) collective-permute-start(s32[1,8]{1,0:T(1,128)S(1)} %bitcast_add_fusion.code.refs_0_), channel_id=1, source_target_pairs={{0,12},{4,8},{8,4},{12,0},{1,13},{5,9},{9,5},{13,1},{2,14},{6,10},... | collective-permute-start | bytes 104 | tf_op jit(solution)/shard_map/ppermute | solution.py:462
  6.4 0.0 collective-permute-start.1
  6.4 0.6 %collective-permute-start = (s32[1,8]{1,0:T(1,128)S(1)}, s32[1,8]{1,0:T(1,128)S(1)}, u32[]{:S(2)}, u32[]{:S(2)}) collective-permute-start(s32[1,8]{1,0:T(1,128)S(1)} %bitcast_add_fusion.code.refs_0_), channel_id=1, source_target_pairs={{0,4},{4,0},{8,12},{12,8},{1,5},{5,1},{9,13},{13,9},{2,6},{6,2},{1... | collective-permute-start | bytes 104 | tf_op jit(solution)/shard_map/ppermute | solution.py:462
  6.9 1.0 %shard_map.113.refs_3_.refs_1_ = bf16[256,512]{1,0:T(8,128)(2,1)S(1)} custom-call(bf16[256,512]{1,0:T(8,128)(2,1)} %bitcast.14), custom_call_target="tpu_custom_call" | custom-call | bytes 1048576 | tf_op jit(solution)/shard_map/pallas_call | solution.py:435
  7.9 0.0 collective-permute-done.2.refs_2_.refs_3_
  7.9 2.9 %collective-permute-done.1.refs_1_.refs_2_ = s32[1,8]{1,0:T(1,128)S(1)} collective-permute-done((s32[1,8]{1,0:T(1,128)S(1)}, s32[1,8]{1,0:T(1,128)S(1)}, u32[]{:S(2)}, u32[]{:S(2)}) %collective-permute-start.1) | collective-permute-done | bytes 64 | tf_op jit(solution)/shard_map/ppermute | solution.py:462
  10.8 0.2 shard_map.114
  11.0 2.1 %collective-permute-start.4 = (bf16[2,32,512]{2,1,0:T(8,128)(2,1)S(1)}, bf16[2,32,512]{2,1,0:T(8,128)(2,1)S(1)}, u32[]{:S(2)}, u32[]{:S(2)}) collective-permute-start(bf16[2,32,512]{2,1,0:T(8,128)(2,1)S(1)} %get-tuple-element.27), channel_id=1, source_target_pairs={{0,8},{4,12},{8,0},{12,4},{1,9},{5,13},{9,1},{13,5},{2,10},{6,14},... | collective-permute-start | bytes 196616 | tf_op jit(solution)/shard_map/ppermute | solution.py:449
  13.1 0.0 collective-permute-start.5
  13.1 2.4 %collective-permute-start.3 = (bf16[2,32,512]{2,1,0:T(8,128)(2,1)S(1)}, bf16[2,32,512]{2,1,0:T(8,128)(2,1)S(1)}, u32[]{:S(2)}, u32[]{:S(2)}) collective-permute-start(bf16[2,32,512]{2,1,0:T(8,128)(2,1)S(1)} %get-tuple-element.24.after), channel_id=1, source_target_pairs={{0,12},{4,8},{8,4},{12,0},{1,13},{5,9},{9,5},{13,1},{2,14},{6,10},... | collective-permute-start | bytes 196616 | tf_op jit(solution)/shard_map/ppermute | solution.py:449
  15.4 2.6 %shard_map.115 = (bf16[2,32,512]{2,1,0:T(8,128)(2,1)S(1)}, bf16[4,768,256]{2,1,0:T(8,128)(2,1)S(1)}, bf16[256,256]{1,0:T(8,128)(2,1)S(1)}, bf16[256,256]{1,0:T(8...) custom-call(f32[3,1,9]{2,1,0:T(1,128)} %bitcast.15, ...), custom_call_target="tpu_custom_call" | custom-call | bytes 1048576 | tf_op jit(solution)/shard_map/pallas_call | solution.py:435
  18.0 0.0 collective-permute-done.4.refs_3_
  18.0 0.0 collective-permute-done.5.refs_4_
  18.0 1.2 %collective-permute-done.3.refs_2_ = bf16[2,32,512]{2,1,0:T(8,128)(2,1)S(1)} collective-permute-done((bf16[2,32,512]{2,1,0:T(8,128)(2,1)S(1)}, bf16[2,32,512]{2,1,0:T(8,128)(2,1)S(1)}, u32[]{:S(2)}, u32[]{:S(2)}) %collective-permute-start.3) | collective-permute-done | bytes 65568 | tf_op jit(solution)/shard_map/ppermute | solution.py:449
  19.2 0.5 %shard_map.116 = (bf16[256,640]{1,0:T(8,128)(2,1)S(1)}, bf16[16,640]{1,0:T(8,128)(2,1)S(1)}, bf16[256,128]{1,0:T(8,128)(2,1)S(1)}, bf16[16,128]{1,0:T(8,128)(2,1)S(1)}) custom-call(bf16[256,256]{1,0:T(8,128)(2,1)S(1)} %get-tuple-element.25.refs_0_, bf16[8,256,128]{2,1,0:T(8,128)(2,1)S(1)} %get-tuple-element.26.refs_1_, ...), custom_call_target="tpu_custom_call" | custom-call | bytes 1048576 | tf_op jit(solution)/shard_map/pallas_call | solution.py:435
  19.7 0.1 collective-permute-start.6
  19.8 1.6 %collective-permute-start.7 = (bf16[16,640]{1,0:T(8,128)(2,1)S(1)}, bf16[16,640]{1,0:T(8,128)(2,1)S(1)}, u32[]{:S(2)}, u32[]{:S(2)}) collective-permute-start(bf16[16,640]{1,0:T(8,128)(2,1)S(1)} %get-tuple-element.32), channel_id=1, source_target_pairs={{0,2},{2,0},{1,3},{3,1},{4,6},{6,4},{5,7},{7,5},{8,10},{10,8},{9,1... | collective-permute-start | bytes 61448 | tf_op jit(solution)/shard_map/ppermute | solution.py:524
  21.4 0.3 collective-permute-start.8
  21.7 1.1 %shard_map.117 = (f32[192,512]{1,0:T(8,128)S(1)}, bf16[192,512]{1,0:T(8,128)(2,1)S(1)}) custom-call(bf16[256,640]{1,0:T(8,128)(2,1)S(1)} %get-tuple-element.30.image, bf16[256,128]{1,0:T(8,128)(2,1)S(1)} %collective-permute-done.6.left.right, bf16[256,128]{1,0:T(8,128)(2,1)S(1)} %collective-permute-done.6.left.right, ...), custom_call_target="tpu_custom_call" | custom-call | bytes 1048576 | tf_op jit(solution)/shard_map/pallas_call | solution.py:435
  22.8 1.6 %collective-permute-done.8.top_left.top_right.bottom_left.bottom_right = bf16[16,128]{1,0:T(8,128)(2,1)S(1)} collective-permute-done((bf16[16,128]{1,0:T(8,128)(2,1)S(1)}, bf16[16,128]{1,0:T(8,128)(2,1)S(1)}, u32[]{:S(2)}, u32[]{:S(2)}) %collective-permute-start.8) | collective-permute-done | bytes 4128 | tf_op jit(solution)/shard_map/ppermute | solution.py:525
  24.4 0.0 collective-permute-done.7.top.bottom
  24.4 0.9 %shard_map.118 = (f32[64,512]{1,0:T(8,128)S(1)}, bf16[2,32,512]{2,1,0:T(8,128)(2,1)S(1)}, bf16[2,32,512]{2,1,0:T(8,128)(2,1)S(1)}, bf16[2,32,512]{2,1,0:T(8,128)(2,1)S(1)}, bf16[2,32,512]{2,1,0:T(8,128)(2,1)S(1)}) custom-call(bf16[256,640]{1,0:T(8,128)(2,1)S(1)} %get-tuple-element.30.image, bf16[256,128]{1,0:T(8,128)(2,1)S(1)} %collective-permute-done.6.left.right, ...), custom_call_target="tpu_custom_call" | custom-call | bytes 1048576 | tf_op jit(solution)/shard_map/pallas_call | solution.py:435
  25.3 2.3 %collective-permute-start.9 = (bf16[2,32,512]{2,1,0:T(8,128)(2,1)S(1)}, bf16[2,32,512]{2,1,0:T(8,128)(2,1)S(1)}, u32[]{:S(2)}, u32[]{:S(2)}) collective-permute-start(bf16[2,32,512]{2,1,0:T(8,128)(2,1)S(1)} %get-tuple-element.43), channel_id=1, source_target_pairs={{0,12},{4,8},{8,4},{12,0},{1,13},{5,9},{9,5},{13,1},{2,14},{6,10},... | collective-permute-start | bytes 196616 | tf_op jit(solution)/shard_map/ppermute | solution.py:449
  27.7 0.0 collective-permute-start.10
  27.7 2.1 %collective-permute-start.11 = (bf16[2,32,512]{2,1,0:T(8,128)(2,1)S(1)}, bf16[2,32,512]{2,1,0:T(8,128)(2,1)S(1)}, u32[]{:S(2)}, u32[]{:S(2)}) collective-permute-start(bf16[2,32,512]{2,1,0:T(8,128)(2,1)S(1)} %get-tuple-element.45), channel_id=1, source_target_pairs={{0,4},{4,0},{8,12},{12,8},{1,5},{5,1},{9,13},{13,9},{2,6},{6,2},{1... | collective-permute-start | bytes 196616 | tf_op jit(solution)/shard_map/ppermute | solution.py:449
  29.8 0.2 shard_map.119.collect
  30.0 0.8 %maximum_bitcast_fusion = f32[1,256,512]{2,1,0:T(8,128)} fusion(f32[32,512]{1,0:T(8,128)S(1)} %get-tuple-element.47, f32[192,512]{1,0:T(8,128)S(1)} %get-tuple-element.41, f32[32,512]{1,0:T(8,128)S(1)} %get-tuple-element.46), kind=kLoop, calls=%fused_computation | loop fusion | flops 262144 | bytes 1048576 | tf_op jit(solution)/shard_map/broadcast_in_dim | solution.py:580
  30.8 1.4 %collective-permute-done.9.refs_0_ = bf16[2,32,512]{2,1,0:T(8,128)(2,1)S(1)} collective-permute-done((bf16[2,32,512]{2,1,0:T(8,128)(2,1)S(1)}, bf16[2,32,512]{2,1,0:T(8,128)(2,1)S(1)}, u32[]{:S(2)}, u32[]{:S(2)}) %collective-permute-start.9) | collective-permute-done | bytes 65568 | tf_op jit(solution)/shard_map/ppermute | solution.py:449
  32.2 2.0 %collective-permute-done.10.refs_1_ = bf16[2,32,512]{2,1,0:T(8,128)(2,1)S(1)} collective-permute-done((bf16[2,32,512]{2,1,0:T(8,128)(2,1)S(1)}, bf16[2,32,512]{2,1,0:T(8,128)(2,1)S(1)}, u32[]{:S(2)}, u32[]{:S(2)}) %collective-permute-start.10) | collective-permute-done | bytes 65568 | tf_op jit(solution)/shard_map/ppermute | solution.py:449
  34.2 0.0 collective-permute-done.11.refs_2_
  34.2 1.0 %shard_map.120 = f32[256,512]{1,0:T(8,128)} custom-call(bf16[256,256]{1,0:T(8,128)(2,1)S(1)} %shard_map.119.collect, bf16[2,32,512]{2,1,0:T(8,128)(2,1)S(1)} %collective-permute-done.9.refs_0_, bf16[2,32,512]{2,1,0:T(8,128)(2,1)S(1)} %collective-permute-done.10.refs_1_, bf16[2,32,512]{2,1,0:T(8,128)(2,1)S(1)} %collective-permute-done.11.refs_2_, ...), custom_call_target="tpu_custom_call" | custom-call | bytes 1048576 | tf_op jit(solution)/shard_map/pallas_call | solution.py:435
  (5 shorter events, 0.0 us)
Async XLA Ops:
  1.3 6.6 %collective-permute-start.2 = (s32[1,8]{1,0:T(1,128)S(1)}, s32[1,8]{1,0:T(1,128)S(1)}, u32[]{:S(2)}, u32[]{:S(2)}) collective-permute-start(s32[1,8]{1,0:T(1,128)S(1)} %bitcast_add_fusion.code.refs_0_), channel_id=1, source_target_pairs={{0,12},{4,8},{8,4},{12,0},{1,13},{5,9},{9,5},{13,1},{2,14},{6,10},... | collective-permute-start | bytes 104 | tf_op jit(solution)/shard_map/ppermute | solution.py:462
  6.4 4.4 %collective-permute-start.1 = (s32[1,8]{1,0:T(1,128)S(1)}, s32[1,8]{1,0:T(1,128)S(1)}, u32[]{:S(2)}, u32[]{:S(2)}) collective-permute-start(s32[1,8]{1,0:T(1,128)S(1)} %bitcast_add_fusion.code.refs_0_), channel_id=1, source_target_pairs={{0,8},{4,12},{8,0},{12,4},{1,9},{5,13},{9,1},{13,5},{2,10},{6,14},... | collective-permute-start | bytes 104 | tf_op jit(solution)/shard_map/ppermute | solution.py:462
  6.4 4.4 %collective-permute-start = (s32[1,8]{1,0:T(1,128)S(1)}, s32[1,8]{1,0:T(1,128)S(1)}, u32[]{:S(2)}, u32[]{:S(2)}) collective-permute-start(s32[1,8]{1,0:T(1,128)S(1)} %bitcast_add_fusion.code.refs_0_), channel_id=1, source_target_pairs={{0,4},{4,0},{8,12},{12,8},{1,5},{5,1},{9,13},{13,9},{2,6},{6,2},{1... | collective-permute-start | bytes 104 | tf_op jit(solution)/shard_map/ppermute | solution.py:462
  11.0 7.0 %collective-permute-start.4 = (bf16[2,32,512]{2,1,0:T(8,128)(2,1)S(1)}, bf16[2,32,512]{2,1,0:T(8,128)(2,1)S(1)}, u32[]{:S(2)}, u32[]{:S(2)}) collective-permute-start(bf16[2,32,512]{2,1,0:T(8,128)(2,1)S(1)} %get-tuple-element.27), channel_id=1, source_target_pairs={{0,8},{4,12},{8,0},{12,4},{1,9},{5,13},{9,1},{13,5},{2,10},{6,14},... | collective-permute-start | bytes 196616 | tf_op jit(solution)/shard_map/ppermute | solution.py:449
  13.1 4.9 %collective-permute-start.5 = (bf16[2,32,512]{2,1,0:T(8,128)(2,1)S(1)}, bf16[2,32,512]{2,1,0:T(8,128)(2,1)S(1)}, u32[]{:S(2)}, u32[]{:S(2)}) collective-permute-start(bf16[2,32,512]{2,1,0:T(8,128)(2,1)S(1)} %get-tuple-element.28), channel_id=1, source_target_pairs={{0,4},{4,0},{8,12},{12,8},{1,5},{5,1},{9,13},{13,9},{2,6},{6,2},{1... | collective-permute-start | bytes 196616 | tf_op jit(solution)/shard_map/ppermute | solution.py:449
  13.1 6.2 %collective-permute-start.3 = (bf16[2,32,512]{2,1,0:T(8,128)(2,1)S(1)}, bf16[2,32,512]{2,1,0:T(8,128)(2,1)S(1)}, u32[]{:S(2)}, u32[]{:S(2)}) collective-permute-start(bf16[2,32,512]{2,1,0:T(8,128)(2,1)S(1)} %get-tuple-element.24.after), channel_id=1, source_target_pairs={{0,12},{4,8},{8,4},{12,0},{1,13},{5,9},{9,5},{13,1},{2,14},{6,10},... | collective-permute-start | bytes 196616 | tf_op jit(solution)/shard_map/ppermute | solution.py:449
  19.7 1.9 %collective-permute-start.6 = (bf16[256,128]{1,0:T(8,128)(2,1)S(1)}, bf16[256,128]{1,0:T(8,128)(2,1)S(1)}, u32[]{:S(2)}, u32[]{:S(2)}) collective-permute-start(bf16[256,128]{1,0:T(8,128)(2,1)S(1)} %get-tuple-element.31), channel_id=1, source_target_pairs={{0,1},{1,0},{2,3},{3,2},{4,5},{5,4},{6,7},{7,6},{8,9},{9,8},{10,11... | collective-permute-start | bytes 196616 | tf_op jit(solution)/shard_map/ppermute | solution.py:523
  19.8 4.6 %collective-permute-start.7 = (bf16[16,640]{1,0:T(8,128)(2,1)S(1)}, bf16[16,640]{1,0:T(8,128)(2,1)S(1)}, u32[]{:S(2)}, u32[]{:S(2)}) collective-permute-start(bf16[16,640]{1,0:T(8,128)(2,1)S(1)} %get-tuple-element.32), channel_id=1, source_target_pairs={{0,2},{2,0},{1,3},{3,1},{4,6},{6,4},{5,7},{7,5},{8,10},{10,8},{9,1... | collective-permute-start | bytes 61448 | tf_op jit(solution)/shard_map/ppermute | solution.py:524
  21.4 3.0 %collective-permute-start.8 = (bf16[16,128]{1,0:T(8,128)(2,1)S(1)}, bf16[16,128]{1,0:T(8,128)(2,1)S(1)}, u32[]{:S(2)}, u32[]{:S(2)}) collective-permute-start(bf16[16,128]{1,0:T(8,128)(2,1)S(1)} %get-tuple-element.33), channel_id=1, source_target_pairs={{0,3},{3,0},{1,2},{2,1},{4,7},{7,4},{5,6},{6,5},{8,11},{11,8},{9,1... | collective-permute-start | bytes 12296 | tf_op jit(solution)/shard_map/ppermute | solution.py:525
  21.7 2.7 %copy-start = (bf16[96,64]{1,0:T(8,128)(2,1)S(1)}, bf16[96,64]{1,0:T(8,128)(2,1)}, u32[]{:S(2)}) copy-start(bf16[96,64]{1,0:T(8,128)(2,1)} %constant.10.clone.bands) | copy-start | bytes 36868
  25.3 6.8 %collective-permute-start.9 = (bf16[2,32,512]{2,1,0:T(8,128)(2,1)S(1)}, bf16[2,32,512]{2,1,0:T(8,128)(2,1)S(1)}, u32[]{:S(2)}, u32[]{:S(2)}) collective-permute-start(bf16[2,32,512]{2,1,0:T(8,128)(2,1)S(1)} %get-tuple-element.43), channel_id=1, source_target_pairs={{0,12},{4,8},{8,4},{12,0},{1,13},{5,9},{9,5},{13,1},{2,14},{6,10},... | collective-permute-start | bytes 196616 | tf_op jit(solution)/shard_map/ppermute | solution.py:449
  27.7 6.5 %collective-permute-start.10 = (bf16[2,32,512]{2,1,0:T(8,128)(2,1)S(1)}, bf16[2,32,512]{2,1,0:T(8,128)(2,1)S(1)}, u32[]{:S(2)}, u32[]{:S(2)}) collective-permute-start(bf16[2,32,512]{2,1,0:T(8,128)(2,1)S(1)} %get-tuple-element.44), channel_id=1, source_target_pairs={{0,8},{4,12},{8,0},{12,4},{1,9},{5,13},{9,1},{13,5},{2,10},{6,14},... | collective-permute-start | bytes 196616 | tf_op jit(solution)/shard_map/ppermute | solution.py:449
  27.7 6.5 %collective-permute-start.11 = (bf16[2,32,512]{2,1,0:T(8,128)(2,1)S(1)}, bf16[2,32,512]{2,1,0:T(8,128)(2,1)S(1)}, u32[]{:S(2)}, u32[]{:S(2)}) collective-permute-start(bf16[2,32,512]{2,1,0:T(8,128)(2,1)S(1)} %get-tuple-element.45), channel_id=1, source_target_pairs={{0,4},{4,0},{8,12},{12,8},{1,5},{5,1},{9,13},{13,9},{2,6},{6,2},{1... | collective-permute-start | bytes 196616 | tf_op jit(solution)/shard_map/ppermute | solution.py:449

commit v3 on v2

--- a/solution.py
+++ b/solution.py
@@ -73,8 +73,17 @@
     return lax.broadcasted_iota(jnp.int32, (rows, LANES), 1)
 
 
-def partner_of(me, group, xor):
-    return me ^ group if xor else group
+def order_of(n):
+    return (2, 3, 1, 0) if n == 4 else (*range(1, n), 0)
+
+
+def in_order(values):
+    return [values[g] for g in order_of(len(values))]
+
+
+def from_order(values):
+    order = order_of(len(values))
+    return [values[order.index(g)] for g in range(len(values))]
 
 
 def matches(code_ref, group, me, strips, capacity):
@@ -88,27 +97,28 @@
     return found, count
 
 
-def slots_of(code_ref, me, strips, capacity, xor):
+def slots_of(code_ref, me, strips, capacity, n, ring):
     owners = [lax.div(code_ref[0, q], jnp.int32(strips)) for q in range(strips)]
     slots = []
     for q in range(strips):
         rank = jnp.int32(0)
         for p in range(q):
             rank = rank + (owners[p] == owners[q]).astype(jnp.int32)
-        slots.append(partner_of(me, owners[q], xor) * capacity + rank)
+        group = lax.rem(owners[q] - me + n, jnp.int32(n)) if ring else owners[q]
+        slots.append(group * capacity + rank)
     return slots
 
 
-def pick_kernel(n, capacity, strips, xor, *refs):
-    if xor:
+def pick_kernel(n, capacity, strips, ring, *refs):
+    if ring:
         codes, template, outs = refs[:n], refs[n], refs[n + 1 :]
     else:
         codes, template, outs = [refs[0]] * n, refs[1], refs[2:]
     me = lax.axis_index("ccd")
     for g in range(n):
-        found, _ = matches(codes[g], None if xor else g, me, strips, capacity)
+        found, _ = matches(codes[g], None if ring else g, me, strips, capacity)
         for j in range(capacity):
-            if xor:
+            if ring:
                 outs[g][j] = template[strip_rows_at(found[j], template.shape[0] // strips), :]
             else:
                 outs[0][g * capacity + j] = template[strip_rows_at(found[j], template.shape[0] // strips), :]
@@ -131,7 +141,7 @@
 def pick_two_kernel(strips, strip_rows, *refs):
     count = len(refs) // 2
     template = refs[count]
-    for code, out in zip(refs[:count], refs[count + 1 :]):
+    for code, out in zip(from_order([*refs[:count], None])[1:], refs[count + 1 :]):
         for j, strip in enumerate(two_of(code[...].astype(F32), lax.axis_index("ccd"), strips)):
             out[j] = template[strip_rows_at(strip, strip_rows), :]
 
@@ -155,7 +165,7 @@
     return value
 
 
-def prepare_kernel(n, capacity, strips, strip_rows, tiles, amp_count, xor, two, coefs_in, shifts_in, fractions_in,
+def prepare_kernel(n, capacity, strips, strip_rows, tiles, amp_count, ring, two, coefs_in, shifts_in, fractions_in,
                    bands_in, science_in, row_band_in, after, code, *refs):
     del after
     if two:
@@ -177,7 +187,7 @@
         backward[...] = jnp.zeros(backward.shape, BF16)
     forward_lane = lax.broadcasted_iota(jnp.int32, (strip_rows, size), 1)
     backward_lane = lax.broadcasted_iota(jnp.int32, (strip_rows, band), 1)
-    for q, slot in enumerate(slots_of(code, me, strips, capacity, xor)):
+    for q, slot in enumerate(slots_of(code, me, strips, capacity, n, ring)):
         low, high = slot * strip_rows, q * strip_rows
         value = turned(base_row(taps[0], q, low + shifts[0, q], 1, size), 0, strip_rows)
         value = jnp.where((forward_lane >= low) & (forward_lane < low + strip_rows), value, 0.0)
@@ -227,7 +237,7 @@
         copy.wait()
 
 
-def collect_kernel(n, capacity, strips, strip_rows, xor, two, after, *refs):
+def collect_kernel(n, capacity, strips, strip_rows, ring, two, after, *refs):
     del after
     out = refs[-1]
     me = lax.axis_index("ccd")
@@ -238,7 +248,7 @@
         if two:
             found = two_of(refs[g][...].astype(F32), me, strips)
         else:
-            found, total = matches(refs[g if xor else 0], None if xor else g, me, strips, capacity)
+            found, total = matches(refs[g if ring else 0], None if ring else g, me, strips, capacity)
             found = [jnp.where(total > j, strip, -1) for j, strip in enumerate(found)]
         for j in range(capacity):
             low = (g * capacity + j) * strip_rows
@@ -262,10 +272,10 @@
     return jnp.concatenate(parts, axis=0) if len(parts) > 1 else parts[0]
 
 
-def warp_kernel(n, strips, strip_rows, tiles, xor, paired, *refs):
+def warp_kernel(n, strips, strip_rows, tiles, ring, paired, *refs):
     forward, spread = refs[:2]
-    count = n if xor else 1
-    received, rest = refs[2 : 2 + count][::-1], refs[2 + count :]
+    count = n if ring else 1
+    received, rest = from_order(refs[2 : 2 + count]), refs[2 + count :]
     if paired:
         image, send_row, send_amp, send_diag, rows_done = rest
     else:
@@ -357,10 +367,10 @@
         columns_returned(lowered, columns, (q - 1) * strip_rows, gather[q], strip_rows, tiles)
 
 
-def edge_kernel(n, capacity, strips, strip_rows, tiles, row_count, amp_count, xor, image, left, right, top, bottom,
+def edge_kernel(n, capacity, strips, strip_rows, tiles, row_count, amp_count, ring, image, left, right, top, bottom,
                 top_left, top_right, bottom_left, bottom_right, science, de, bands, backward, gather,
                 columns_mid, diff, *rest):
-    outs = rest[: n if xor else 1]
+    outs = rest[: n if ring else 1]
     across, lowered, columns = rest[len(outs) :]
     band = strips * strip_rows
     inner = strip_rows + MARGIN
@@ -395,14 +405,14 @@
     columns_returned(lowered, columns, strip_rows, gather[strips - 1], strip_rows, tiles)
     whole = jnp.concatenate([columns[:strip_rows, :], columns_mid[...], columns[strip_rows:, :]], axis=0)
     result = jnp.dot(backward[...], whole, preferred_element_type=F32).astype(BF16)
-    size = capacity * strip_rows * (1 if xor else n)
+    size = capacity * strip_rows * (1 if ring else n)
     for g, out in enumerate(outs):
         out[...] = result[g * size : (g + 1) * size].reshape(out.shape)
 
 
 def sum_kernel(collect, *refs):
     *returned, stack, total, sems = refs
-    values = stacked(returned[::-1])
+    values = stacked(from_order(returned))
     copies = []
     half = total.shape[0] // 2
     for i in range(2):
@@ -424,8 +434,8 @@
     capacity = max(2, strips // n)
     tiles = width // LANES
     padded = width + LANES
-    xor = n in (2, 4)
-    two = xor and capacity == 2 and strips == 2 * n
+    ring = n <= 4
+    two = ring and capacity == 2 and strips == 2 * n
     paired = row_count == 2 and amp_count == 2
     swap = [(0, 1), (1, 0)]
     strip_shape = (capacity, strip_rows, width)
@@ -442,12 +452,13 @@
             cost_estimate=pl.CostEstimate(flops=0, bytes_accessed=1 << 20, transcendentals=0),
         )(*operands)
 
-    def exchange(parts):
-        if not xor:
+    def turn(value, g):
+        return lax.ppermute(value, "ccd", [(i, (i + g) % n) for i in range(n)])
+
+    def exchange(parts, sign):
+        if not ring:
             return [lax.all_to_all(parts[0], "ccd", split_axis=0, concat_axis=0, tiled=True)]
-        return [parts[0]] + [
-            lax.ppermute(parts[g], "ccd", [(i, i ^ g) for i in range(n)]) for g in range(1, n)
-        ]
+        return [parts[0]] + [turn(parts[g], sign * g) for g in range(1, n)]
 
     code = owners.reshape(1, strips) * strips + patch_strip.reshape(1, strips)
     (template_rows,) = call(
@@ -458,26 +469,23 @@
         [pltpu.SemaphoreType.DMA],
     )
 
-    def exchanged(value, g):
-        return lax.ppermute(value, "ccd", [(i, i ^ g) for i in range(n)])
-
     if two:
-        codes = [code] + [exchanged(code, g) for g in range(1, n)]
+        codes = exchange([code] * n, 1)
         picked = call(
             functools.partial(pick_two_kernel, strips, strip_rows),
             [(strip_shape, BF16)] * (n - 1),
-            [*codes[1:], template_rows],
+            [*in_order(codes)[:-1], template_rows],
             [VMEM] * n,
         )
-    elif xor:
-        codes = [code.reshape(strips)] + [exchanged(code.reshape(strips), g) for g in range(1, n)]
+    elif ring:
+        codes = exchange([code.reshape(strips)] * n, 1)
         picked_shapes = [(strip_shape, BF16)] * n
     else:
         codes = [lax.all_gather(code.reshape(strips), "ccd", axis=0, tiled=True)]
         picked_shapes = [((n * capacity, strip_rows, width), BF16)]
     if not two:
         picked = call(
-            functools.partial(pick_kernel, n, capacity, strips, xor),
+            functools.partial(pick_kernel, n, capacity, strips, ring),
             picked_shapes,
             [*codes, template_rows],
             [SMEM] * len(codes) + [VMEM],
@@ -486,7 +494,7 @@
     mid_bands = jnp.asarray(row_bands(mid_rows))
     slot_rows = n * capacity * strip_rows
     *own, de, forward, backward, spread, gather, science, mid_bands = call(
-        functools.partial(prepare_kernel, n, capacity, strips, strip_rows, tiles, amp_count, xor, two),
+        functools.partial(prepare_kernel, n, capacity, strips, strip_rows, tiles, amp_count, ring, two),
         ([(strip_shape, BF16)] if two else []) + [
             ((tiles, 2 * KINDS * LANES, 2 * LANES), BF16),
             ((band, slot_rows), BF16),
@@ -506,13 +514,13 @@
         megabytes=10,
     )
     if two:
-        received = exchange([*own, *picked])[::-1]
+        received = in_order(exchange([*own, *picked], -1))
     else:
-        received = exchange(picked)[::-1]
+        received = in_order(exchange(picked, -1))
     image_shape = ((band, padded), BF16)
     halo_shapes = [((MARGIN, padded), BF16), ((band, LANES), BF16), ((MARGIN, LANES), BF16)]
     warped = call(
-        functools.partial(warp_kernel, n, strips, strip_rows, tiles, xor, paired),
+        functools.partial(warp_kernel, n, strips, strip_rows, tiles, ring, paired),
         [image_shape] + (halo_shapes if paired else []),
         [forward, spread, *received],
         [VMEM] * (2 + len(received)),
@@ -552,9 +560,9 @@
         [VMEM] * 7,
         [((mid_rows, (tiles + 1) * KINDS * LANES), BF16), ((mid_rows, padded + LANES), BF16)],
     )
-    outgoing_shapes = [(strip_shape, BF16)] * n if xor else [((n * capacity, strip_rows, width), BF16)]
+    outgoing_shapes = [(strip_shape, BF16)] * n if ring else [((n * capacity, strip_rows, width), BF16)]
     diff_edge, *outgoing = call(
-        functools.partial(edge_kernel, n, capacity, strips, strip_rows, tiles, row_count, amp_count, xor),
+        functools.partial(edge_kernel, n, capacity, strips, strip_rows, tiles, row_count, amp_count, ring),
         [((2 * strip_rows, width), F32)] + outgoing_shapes,
         [image, left, right, top, bottom, top_left, top_right, bottom_left, bottom_right, science, de,
          jnp.asarray(row_bands(strip_rows)), backward, gather, columns_mid],
@@ -562,9 +570,9 @@
         [((2 * strip_rows, (tiles + 1) * KINDS * LANES), BF16), ((2 * strip_rows, padded + LANES), BF16),
          ((2 * strip_rows, width), BF16)],
     )
-    returned = exchange(outgoing)[::-1]
+    returned = in_order(exchange(outgoing, 1))
     (collect,) = call(
-        functools.partial(collect_kernel, n, capacity, strips, strip_rows, xor, two),
+        functools.partial(collect_kernel, n, capacity, strips, strip_rows, ring, two),
         [((band, slot_rows), BF16)],
         [outgoing[0], *codes],
         [VMEM] + [VMEM if two else SMEM] * len(codes),

time: 35.4 us -> 34.5 us (0.975)
  starting transfers between devices: 16.5 us -> 13.2 us
  waiting for transfers between devices: 9.1 us -> 11.5 us
    ppermute x9, starting transfers between devices: 14.5 us -> 11.3 us  [turn(): return lax.ppermute(value, 'ccd', [(i, (i + g) % n) for i in range(n)])]
    ppermute x9, waiting for transfers between devices: 7.51 us -> 9.89 us  [turn(): return lax.ppermute(value, 'ccd', [(i, (i + g) % n) for i in range(n)])]
  transfers between devices with their start and end apart: 12 -> 12, of which waited for: 5 -> 7; matrix products, arithmetic and copies ran while one was open for 2% -> 2% of each run, Pallas kernels for 14% -> 14%
where the time goes in v3:
time: 34.5 us; the launch traced here: 34.3 us
  starting transfers between devices  13.2 us (38%)
  waiting for transfers between devices  11.5 us (33%)
  Pallas kernels  7.36 us (21%)
  other arithmetic  1.51 us (4%)
  between operations  0.73 us (2%)
    ppermute x9, starting transfers between devices, turn(): return lax.ppermute(value, 'ccd', [(i, (i + g) % n) for i in range(n)])  11.3 us
    ppermute x9, waiting for transfers between devices, turn(): return lax.ppermute(value, 'ccd', [(i, (i + g) % n) for i in range(n)])  9.89 us
    pallas_call x8, Pallas kernels, call(): pl.pallas_call(kernel, out_shape=shapes, in_specs=list(spaces), out_specs...  7.36 us
    ppermute x1, waiting for transfers between devices, body(): lax.ppermute(warped[3], ('row', 'amp'), [(0, 3), (3, 0), (1, 2), (2, 1)])  1.58 us
    ppermute x1, starting transfers between devices, body(): ends = lax.ppermute(warped[1], 'row', swap)  1.56 us
    broadcast_in_dim x1, other arithmetic, body(): return (difference[None], stack.reshape(template.shape))  0.83 us
  transfers between devices with their start and end apart: 12, of which 7 were waited for; matrix products, arithmetic and copies ran while one was open for 2% of the time, Pallas kernels for 14%

profile of v3, /device:TPU:0, one launch (start us, length us, event | category | flops | bytes accessed | tf_op | source)
XLA Modules:
  0.0 34.3 jit_solution(15997063518378297011)
XLA Ops:
  0.6 0.7 %bitcast_add_fusion.code.refs_0_ = s32[1,8]{1,0:T(1,128)S(1)} fusion(s32[1,1,1,8]{3,2,1,0:T(1,128)} %param.13, s32[1,1,1,8,1]{3,4,2,1,0:T(1,128)} %param.12), kind=kLoop, calls=%fused_computation.1 | loop fusion | flops 16 | bytes 96 | tf_op jit(solution)/shard_map/add | solution.py:463
  1.3 3.0 %collective-permute-start.2 = (s32[1,8]{1,0:T(1,128)S(1)}, s32[1,8]{1,0:T(1,128)S(1)}, u32[]{:S(2)}, u32[]{:S(2)}) collective-permute-start(s32[1,8]{1,0:T(1,128)S(1)} %bitcast_add_fusion.code.refs_0_), channel_id=1, source_target_pairs={{0,4},{4,8},{8,12},{12,0},{1,5},{5,9},{9,13},{13,1},{2,6},{6,10},{... | collective-permute-start | bytes 104 | tf_op jit(solution)/shard_map/ppermute | solution.py:456
  4.3 2.0 %collective-permute-start.1 = (s32[1,8]{1,0:T(1,128)S(1)}, s32[1,8]{1,0:T(1,128)S(1)}, u32[]{:S(2)}, u32[]{:S(2)}) collective-permute-start(s32[1,8]{1,0:T(1,128)S(1)} %bitcast_add_fusion.code.refs_0_), channel_id=1, source_target_pairs={{0,12},{4,0},{8,4},{12,8},{1,13},{5,1},{9,5},{13,9},{2,14},{6,2},{... | collective-permute-start | bytes 104 | tf_op jit(solution)/shard_map/ppermute | solution.py:456
  6.4 1.0 %collective-permute-start = (s32[1,8]{1,0:T(1,128)S(1)}, s32[1,8]{1,0:T(1,128)S(1)}, u32[]{:S(2)}, u32[]{:S(2)}) collective-permute-start(s32[1,8]{1,0:T(1,128)S(1)} %bitcast_add_fusion.code.refs_0_), channel_id=1, source_target_pairs={{0,8},{4,12},{8,0},{12,4},{1,9},{5,13},{9,1},{13,5},{2,10},{6,14},... | collective-permute-start | bytes 104 | tf_op jit(solution)/shard_map/ppermute | solution.py:456
  7.4 1.0 %shard_map.113.refs_3_.refs_1_ = bf16[256,512]{1,0:T(8,128)(2,1)S(1)} custom-call(bf16[256,512]{1,0:T(8,128)(2,1)} %bitcast.14), custom_call_target="tpu_custom_call" | custom-call | bytes 1048576 | tf_op jit(solution)/shard_map/pallas_call | solution.py:445
  8.3 0.0 collective-permute-done.2.refs_2_.refs_1_
  8.4 2.4 %collective-permute-done.refs_0_.refs_2_ = s32[1,8]{1,0:T(1,128)S(1)} collective-permute-done((s32[1,8]{1,0:T(1,128)S(1)}, s32[1,8]{1,0:T(1,128)S(1)}, u32[]{:S(2)}, u32[]{:S(2)}) %collective-permute-start) | collective-permute-done | bytes 64 | tf_op jit(solution)/shard_map/ppermute | solution.py:456
  10.8 0.2 shard_map.114
  11.0 1.1 %collective-permute-start.3 = (bf16[2,32,512]{2,1,0:T(8,128)(2,1)S(1)}, bf16[2,32,512]{2,1,0:T(8,128)(2,1)S(1)}, u32[]{:S(2)}, u32[]{:S(2)}) collective-permute-start(bf16[2,32,512]{2,1,0:T(8,128)(2,1)S(1)} %get-tuple-element.27), channel_id=1, source_target_pairs={{0,8},{4,12},{8,0},{12,4},{1,9},{5,13},{9,1},{13,5},{2,10},{6,14},... | collective-permute-start | bytes 196616 | tf_op jit(solution)/shard_map/ppermute | solution.py:456
  12.0 1.3 %collective-permute-start.5 = (bf16[2,32,512]{2,1,0:T(8,128)(2,1)S(1)}, bf16[2,32,512]{2,1,0:T(8,128)(2,1)S(1)}, u32[]{:S(2)}, u32[]{:S(2)}) collective-permute-start(bf16[2,32,512]{2,1,0:T(8,128)(2,1)S(1)} %get-tuple-element.28), channel_id=1, source_target_pairs={{0,12},{4,0},{8,4},{12,8},{1,13},{5,1},{9,5},{13,9},{2,14},{6,2},{... | collective-permute-start | bytes 196616 | tf_op jit(solution)/shard_map/ppermute | solution.py:456
  13.4 0.7 %collective-permute-start.4 = (bf16[2,32,512]{2,1,0:T(8,128)(2,1)S(1)}, bf16[2,32,512]{2,1,0:T(8,128)(2,1)S(1)}, u32[]{:S(2)}, u32[]{:S(2)}) collective-permute-start(bf16[2,32,512]{2,1,0:T(8,128)(2,1)S(1)} %get-tuple-element.24.after), channel_id=1, source_target_pairs={{0,4},{4,8},{8,12},{12,0},{1,5},{5,9},{9,13},{13,1},{2,6},{6,10},{... | collective-permute-start | bytes 196616 | tf_op jit(solution)/shard_map/ppermute | solution.py:456
  14.1 2.5 %shard_map.115 = (bf16[2,32,512]{2,1,0:T(8,128)(2,1)S(1)}, bf16[4,768,256]{2,1,0:T(8,128)(2,1)S(1)}, bf16[256,256]{1,0:T(8,128)(2,1)S(1)}, bf16[256,256]{1,0:T(8...) custom-call(f32[3,1,9]{2,1,0:T(1,128)} %bitcast.15, ...), custom_call_target="tpu_custom_call" | custom-call | bytes 1048576 | tf_op jit(solution)/shard_map/pallas_call | solution.py:445
  16.6 0.5 %collective-permute-done.3.refs_2_ = bf16[2,32,512]{2,1,0:T(8,128)(2,1)S(1)} collective-permute-done((bf16[2,32,512]{2,1,0:T(8,128)(2,1)S(1)}, bf16[2,32,512]{2,1,0:T(8,128)(2,1)S(1)}, u32[]{:S(2)}, u32[]{:S(2)}) %collective-permute-start.3) | collective-permute-done | bytes 65568 | tf_op jit(solution)/shard_map/ppermute | solution.py:456
  17.1 0.5 %collective-permute-done.5.refs_4_ = bf16[2,32,512]{2,1,0:T(8,128)(2,1)S(1)} collective-permute-done((bf16[2,32,512]{2,1,0:T(8,128)(2,1)S(1)}, bf16[2,32,512]{2,1,0:T(8,128)(2,1)S(1)}, u32[]{:S(2)}, u32[]{:S(2)}) %collective-permute-start.5) | collective-permute-done | bytes 65568 | tf_op jit(solution)/shard_map/ppermute | solution.py:456
  17.5 1.9 %collective-permute-done.4.refs_3_ = bf16[2,32,512]{2,1,0:T(8,128)(2,1)S(1)} collective-permute-done((bf16[2,32,512]{2,1,0:T(8,128)(2,1)S(1)}, bf16[2,32,512]{2,1,0:T(8,128)(2,1)S(1)}, u32[]{:S(2)}, u32[]{:S(2)}) %collective-permute-start.4) | collective-permute-done | bytes 65568 | tf_op jit(solution)/shard_map/ppermute | solution.py:456
  19.4 0.5 %shard_map.116 = (bf16[256,640]{1,0:T(8,128)(2,1)S(1)}, bf16[16,640]{1,0:T(8,128)(2,1)S(1)}, bf16[256,128]{1,0:T(8,128)(2,1)S(1)}, bf16[16,128]{1,0:T(8,128)(2,1)S(1)}) custom-call(bf16[256,256]{1,0:T(8,128)(2,1)S(1)} %get-tuple-element.25.refs_0_, bf16[8,256,128]{2,1,0:T(8,128)(2,1)S(1)} %get-tuple-element.26.refs_1_, ...), custom_call_target="tpu_custom_call" | custom-call | bytes 1048576 | tf_op jit(solution)/shard_map/pallas_call | solution.py:445
  20.0 0.1 collective-permute-start.6
  20.0 1.6 %collective-permute-start.7 = (bf16[16,640]{1,0:T(8,128)(2,1)S(1)}, bf16[16,640]{1,0:T(8,128)(2,1)S(1)}, u32[]{:S(2)}, u32[]{:S(2)}) collective-permute-start(bf16[16,640]{1,0:T(8,128)(2,1)S(1)} %get-tuple-element.32), channel_id=1, source_target_pairs={{0,2},{2,0},{1,3},{3,1},{4,6},{6,4},{5,7},{7,5},{8,10},{10,8},{9,1... | collective-permute-start | bytes 61448 | tf_op jit(solution)/shard_map/ppermute | solution.py:532
  21.6 0.3 collective-permute-start.8
  21.9 0.0 collective-permute-done.6.left.right
  21.9 1.1 %shard_map.117 = (f32[192,512]{1,0:T(8,128)S(1)}, bf16[192,512]{1,0:T(8,128)(2,1)S(1)}) custom-call(bf16[256,640]{1,0:T(8,128)(2,1)S(1)} %get-tuple-element.30.image, bf16[256,128]{1,0:T(8,128)(2,1)S(1)} %collective-permute-done.6.left.right, bf16[256,128]{1,0:T(8,128)(2,1)S(1)} %collective-permute-done.6.left.right, ...), custom_call_target="tpu_custom_call" | custom-call | bytes 1048576 | tf_op jit(solution)/shard_map/pallas_call | solution.py:445
  23.0 1.6 %collective-permute-done.8.top_left.top_right.bottom_left.bottom_right = bf16[16,128]{1,0:T(8,128)(2,1)S(1)} collective-permute-done((bf16[16,128]{1,0:T(8,128)(2,1)S(1)}, bf16[16,128]{1,0:T(8,128)(2,1)S(1)}, u32[]{:S(2)}, u32[]{:S(2)}) %collective-permute-start.8) | collective-permute-done | bytes 4128 | tf_op jit(solution)/shard_map/ppermute | solution.py:533
  24.6 0.0 collective-permute-done.7.top.bottom
  24.6 0.9 %shard_map.118 = (f32[64,512]{1,0:T(8,128)S(1)}, bf16[2,32,512]{2,1,0:T(8,128)(2,1)S(1)}, bf16[2,32,512]{2,1,0:T(8,128)(2,1)S(1)}, bf16[2,32,512]{2,1,0:T(8,128)(2,1)S(1)}, bf16[2,32,512]{2,1,0:T(8,128)(2,1)S(1)}) custom-call(bf16[256,640]{1,0:T(8,128)(2,1)S(1)} %get-tuple-element.30.image, bf16[256,128]{1,0:T(8,128)(2,1)S(1)} %collective-permute-done.6.left.right, ...), custom_call_target="tpu_custom_call" | custom-call | bytes 1048576 | tf_op jit(solution)/shard_map/pallas_call | solution.py:445
  25.6 0.1 collective-permute-start.9
  25.6 1.2 %collective-permute-start.10 = (bf16[2,32,512]{2,1,0:T(8,128)(2,1)S(1)}, bf16[2,32,512]{2,1,0:T(8,128)(2,1)S(1)}, u32[]{:S(2)}, u32[]{:S(2)}) collective-permute-start(bf16[2,32,512]{2,1,0:T(8,128)(2,1)S(1)} %get-tuple-element.44), channel_id=1, source_target_pairs={{0,12},{4,0},{8,4},{12,8},{1,13},{5,1},{9,5},{13,9},{2,14},{6,2},{... | collective-permute-start | bytes 196616 | tf_op jit(solution)/shard_map/ppermute | solution.py:456
  26.9 0.8 %collective-permute-start.11 = (bf16[2,32,512]{2,1,0:T(8,128)(2,1)S(1)}, bf16[2,32,512]{2,1,0:T(8,128)(2,1)S(1)}, u32[]{:S(2)}, u32[]{:S(2)}) collective-permute-start(bf16[2,32,512]{2,1,0:T(8,128)(2,1)S(1)} %get-tuple-element.45), channel_id=1, source_target_pairs={{0,4},{4,8},{8,12},{12,0},{1,5},{5,9},{9,13},{13,1},{2,6},{6,10},{... | collective-permute-start | bytes 196616 | tf_op jit(solution)/shard_map/ppermute | solution.py:456
  27.7 0.2 shard_map.119.collect
  27.9 0.8 %maximum_bitcast_fusion = f32[1,256,512]{2,1,0:T(8,128)} fusion(f32[32,512]{1,0:T(8,128)S(1)} %get-tuple-element.47, f32[192,512]{1,0:T(8,128)S(1)} %get-tuple-element.41, f32[32,512]{1,0:T(8,128)S(1)} %get-tuple-element.46), kind=kLoop, calls=%fused_computation | loop fusion | flops 262144 | bytes 1048576 | tf_op jit(solution)/shard_map/broadcast_in_dim | solution.py:588
  28.7 3.3 %collective-permute-done.9.refs_0_ = bf16[2,32,512]{2,1,0:T(8,128)(2,1)S(1)} collective-permute-done((bf16[2,32,512]{2,1,0:T(8,128)(2,1)S(1)}, bf16[2,32,512]{2,1,0:T(8,128)(2,1)S(1)}, u32[]{:S(2)}, u32[]{:S(2)}) %collective-permute-start.9) | collective-permute-done | bytes 65568 | tf_op jit(solution)/shard_map/ppermute | solution.py:456
  32.0 1.3 %collective-permute-done.11.refs_2_ = bf16[2,32,512]{2,1,0:T(8,128)(2,1)S(1)} collective-permute-done((bf16[2,32,512]{2,1,0:T(8,128)(2,1)S(1)}, bf16[2,32,512]{2,1,0:T(8,128)(2,1)S(1)}, u32[]{:S(2)}, u32[]{:S(2)}) %collective-permute-start.11) | collective-permute-done | bytes 65568 | tf_op jit(solution)/shard_map/ppermute | solution.py:456
  33.3 1.0 %shard_map.120 = f32[256,512]{1,0:T(8,128)} custom-call(bf16[256,256]{1,0:T(8,128)(2,1)S(1)} %shard_map.119.collect, bf16[2,32,512]{2,1,0:T(8,128)(2,1)S(1)} %collective-permute-done.9.refs_0_, bf16[2,32,512]{2,1,0:T(8,128)(2,1)S(1)} %collective-permute-done.10.refs_1_, bf16[2,32,512]{2,1,0:T(8,128)(2,1)S(1)} %collective-permute-done.11.refs_2_, ...), custom_call_target="tpu_custom_call" | custom-call | bytes 1048576 | tf_op jit(solution)/shard_map/pallas_call | solution.py:445
  (5 shorter events, 0.0 us)
Async XLA Ops:
  1.3 7.0 %collective-permute-start.2 = (s32[1,8]{1,0:T(1,128)S(1)}, s32[1,8]{1,0:T(1,128)S(1)}, u32[]{:S(2)}, u32[]{:S(2)}) collective-permute-start(s32[1,8]{1,0:T(1,128)S(1)} %bitcast_add_fusion.code.refs_0_), channel_id=1, source_target_pairs={{0,4},{4,8},{8,12},{12,0},{1,5},{5,9},{9,13},{13,1},{2,6},{6,10},{... | collective-permute-start | bytes 104 | tf_op jit(solution)/shard_map/ppermute | solution.py:456
  4.3 4.0 %collective-permute-start.1 = (s32[1,8]{1,0:T(1,128)S(1)}, s32[1,8]{1,0:T(1,128)S(1)}, u32[]{:S(2)}, u32[]{:S(2)}) collective-permute-start(s32[1,8]{1,0:T(1,128)S(1)} %bitcast_add_fusion.code.refs_0_), channel_id=1, source_target_pairs={{0,12},{4,0},{8,4},{12,8},{1,13},{5,1},{9,5},{13,9},{2,14},{6,2},{... | collective-permute-start | bytes 104 | tf_op jit(solution)/shard_map/ppermute | solution.py:456
  6.4 4.4 %collective-permute-start = (s32[1,8]{1,0:T(1,128)S(1)}, s32[1,8]{1,0:T(1,128)S(1)}, u32[]{:S(2)}, u32[]{:S(2)}) collective-permute-start(s32[1,8]{1,0:T(1,128)S(1)} %bitcast_add_fusion.code.refs_0_), channel_id=1, source_target_pairs={{0,8},{4,12},{8,0},{12,4},{1,9},{5,13},{9,1},{13,5},{2,10},{6,14},... | collective-permute-start | bytes 104 | tf_op jit(solution)/shard_map/ppermute | solution.py:456
  11.0 6.1 %collective-permute-start.3 = (bf16[2,32,512]{2,1,0:T(8,128)(2,1)S(1)}, bf16[2,32,512]{2,1,0:T(8,128)(2,1)S(1)}, u32[]{:S(2)}, u32[]{:S(2)}) collective-permute-start(bf16[2,32,512]{2,1,0:T(8,128)(2,1)S(1)} %get-tuple-element.27), channel_id=1, source_target_pairs={{0,8},{4,12},{8,0},{12,4},{1,9},{5,13},{9,1},{13,5},{2,10},{6,14},... | collective-permute-start | bytes 196616 | tf_op jit(solution)/shard_map/ppermute | solution.py:456
  12.0 5.5 %collective-permute-start.5 = (bf16[2,32,512]{2,1,0:T(8,128)(2,1)S(1)}, bf16[2,32,512]{2,1,0:T(8,128)(2,1)S(1)}, u32[]{:S(2)}, u32[]{:S(2)}) collective-permute-start(bf16[2,32,512]{2,1,0:T(8,128)(2,1)S(1)} %get-tuple-element.28), channel_id=1, source_target_pairs={{0,12},{4,0},{8,4},{12,8},{1,13},{5,1},{9,5},{13,9},{2,14},{6,2},{... | collective-permute-start | bytes 196616 | tf_op jit(solution)/shard_map/ppermute | solution.py:456
  13.4 6.1 %collective-permute-start.4 = (bf16[2,32,512]{2,1,0:T(8,128)(2,1)S(1)}, bf16[2,32,512]{2,1,0:T(8,128)(2,1)S(1)}, u32[]{:S(2)}, u32[]{:S(2)}) collective-permute-start(bf16[2,32,512]{2,1,0:T(8,128)(2,1)S(1)} %get-tuple-element.24.after), channel_id=1, source_target_pairs={{0,4},{4,8},{8,12},{12,0},{1,5},{5,9},{9,13},{13,1},{2,6},{6,10},{... | collective-permute-start | bytes 196616 | tf_op jit(solution)/shard_map/ppermute | solution.py:456
  20.0 1.9 %collective-permute-start.6 = (bf16[256,128]{1,0:T(8,128)(2,1)S(1)}, bf16[256,128]{1,0:T(8,128)(2,1)S(1)}, u32[]{:S(2)}, u32[]{:S(2)}) collective-permute-start(bf16[256,128]{1,0:T(8,128)(2,1)S(1)} %get-tuple-element.31), channel_id=1, source_target_pairs={{0,1},{1,0},{2,3},{3,2},{4,5},{5,4},{6,7},{7,6},{8,9},{9,8},{10,11... | collective-permute-start | bytes 196616 | tf_op jit(solution)/shard_map/ppermute | solution.py:531
  20.0 4.6 %collective-permute-start.7 = (bf16[16,640]{1,0:T(8,128)(2,1)S(1)}, bf16[16,640]{1,0:T(8,128)(2,1)S(1)}, u32[]{:S(2)}, u32[]{:S(2)}) collective-permute-start(bf16[16,640]{1,0:T(8,128)(2,1)S(1)} %get-tuple-element.32), channel_id=1, source_target_pairs={{0,2},{2,0},{1,3},{3,1},{4,6},{6,4},{5,7},{7,5},{8,10},{10,8},{9,1... | collective-permute-start | bytes 61448 | tf_op jit(solution)/shard_map/ppermute | solution.py:532
  21.6 3.0 %collective-permute-start.8 = (bf16[16,128]{1,0:T(8,128)(2,1)S(1)}, bf16[16,128]{1,0:T(8,128)(2,1)S(1)}, u32[]{:S(2)}, u32[]{:S(2)}) collective-permute-start(bf16[16,128]{1,0:T(8,128)(2,1)S(1)} %get-tuple-element.33), channel_id=1, source_target_pairs={{0,3},{3,0},{1,2},{2,1},{4,7},{7,4},{5,6},{6,5},{8,11},{11,8},{9,1... | collective-permute-start | bytes 12296 | tf_op jit(solution)/shard_map/ppermute | solution.py:533
  21.9 2.7 %copy-start = (bf16[96,64]{1,0:T(8,128)(2,1)S(1)}, bf16[96,64]{1,0:T(8,128)(2,1)}, u32[]{:S(2)}) copy-start(bf16[96,64]{1,0:T(8,128)(2,1)} %constant.10.clone.bands) | copy-start | bytes 36868
  25.6 6.4 %collective-permute-start.9 = (bf16[2,32,512]{2,1,0:T(8,128)(2,1)S(1)}, bf16[2,32,512]{2,1,0:T(8,128)(2,1)S(1)}, u32[]{:S(2)}, u32[]{:S(2)}) collective-permute-start(bf16[2,32,512]{2,1,0:T(8,128)(2,1)S(1)} %get-tuple-element.43), channel_id=1, source_target_pairs={{0,8},{4,12},{8,0},{12,4},{1,9},{5,13},{9,1},{13,5},{2,10},{6,14},... | collective-permute-start | bytes 196616 | tf_op jit(solution)/shard_map/ppermute | solution.py:456
  25.6 6.4 %collective-permute-start.10 = (bf16[2,32,512]{2,1,0:T(8,128)(2,1)S(1)}, bf16[2,32,512]{2,1,0:T(8,128)(2,1)S(1)}, u32[]{:S(2)}, u32[]{:S(2)}) collective-permute-start(bf16[2,32,512]{2,1,0:T(8,128)(2,1)S(1)} %get-tuple-element.44), channel_id=1, source_target_pairs={{0,12},{4,0},{8,4},{12,8},{1,13},{5,1},{9,5},{13,9},{2,14},{6,2},{... | collective-permute-start | bytes 196616 | tf_op jit(solution)/shard_map/ppermute | solution.py:456
  26.9 6.4 %collective-permute-start.11 = (bf16[2,32,512]{2,1,0:T(8,128)(2,1)S(1)}, bf16[2,32,512]{2,1,0:T(8,128)(2,1)S(1)}, u32[]{:S(2)}, u32[]{:S(2)}) collective-permute-start(bf16[2,32,512]{2,1,0:T(8,128)(2,1)S(1)} %get-tuple-element.45), channel_id=1, source_target_pairs={{0,4},{4,8},{8,12},{12,0},{1,5},{5,9},{9,13},{13,1},{2,6},{6,10},{... | collective-permute-start | bytes 196616 | tf_op jit(solution)/shard_map/ppermute | solution.py:456

commit v4 on v3

--- a/solution.py
+++ b/solution.py
@@ -138,12 +138,9 @@
     return pl.ds(pl.multiple_of(strip * strip_rows, strip_rows), strip_rows)
 
 
-def pick_two_kernel(strips, strip_rows, *refs):
-    count = len(refs) // 2
-    template = refs[count]
-    for code, out in zip(from_order([*refs[:count], None])[1:], refs[count + 1 :]):
-        for j, strip in enumerate(two_of(code[...].astype(F32), lax.axis_index("ccd"), strips)):
-            out[j] = template[strip_rows_at(strip, strip_rows), :]
+def pick_two_kernel(strips, strip_rows, code, template, out):
+    for j, strip in enumerate(two_of(code[...].astype(F32), lax.axis_index("ccd"), strips)):
+        out[j] = template[strip_rows_at(strip, strip_rows), :]
 
 
 def load_kernel(source, target, sem):
@@ -471,12 +468,15 @@
 
     if two:
         codes = exchange([code] * n, 1)
-        picked = call(
-            functools.partial(pick_two_kernel, strips, strip_rows),
-            [(strip_shape, BF16)] * (n - 1),
-            [*in_order(codes)[:-1], template_rows],
-            [VMEM] * n,
-        )
+        picked = [
+            call(
+                functools.partial(pick_two_kernel, strips, strip_rows),
+                [(strip_shape, BF16)],
+                [other, template_rows],
+                [VMEM] * 2,
+            )[0]
+            for other in codes[1:]
+        ]
     elif ring:
         codes = exchange([code.reshape(strips)] * n, 1)
         picked_shapes = [(strip_shape, BF16)] * n
@@ -507,7 +507,7 @@
         [in_hbm(value) for value in (
             coefs.transpose(1, 0, 2), shifts.reshape(2, strips), fractions.reshape(2, strips),
             jnp.asarray(column_bands()), science.reshape(band, width), mid_bands)]
-        + [picked[-1], code] + ([code, template_rows] if two else []),
+        + [picked[n // 2 - 1] if two else picked[-1], code] + ([code, template_rows] if two else []),
         [HBM] * 6 + [VMEM, SMEM] + [VMEM] * (2 if two else 0),
         [pltpu.SMEM((3, 1, 9), F32), pltpu.SMEM((2, strips), jnp.int32),
          ((2, strips), F32), ((KINDS, 2 * LANES, LANES), BF16), pltpu.SemaphoreType.DMA((6,))],

time: 34.5 us -> 33.8 us (0.980)
  waiting for transfers between devices: 11.5 us -> 8.85 us
  starting transfers between devices: 13.2 us -> 14.9 us
    ppermute x9, waiting for transfers between devices: 9.89 us -> 7.27 us  [turn(): return lax.ppermute(value, 'ccd', [(i, (i + g) % n) for i in range(n)])]
    ppermute x9, starting transfers between devices: 11.3 us -> 13 us  [turn(): return lax.ppermute(value, 'ccd', [(i, (i + g) % n) for i in range(n)])]
    pallas_call x8 -> x10, Pallas kernels: 7.36 us -> 7.63 us  [call(): pl.pallas_call(kernel, out_shape=shapes, in_specs=list(spaces), out_specs...]
  transfers between devices with their start and end apart: 12 -> 12, of which waited for: 7 -> 5; matrix products, arithmetic and copies ran while one was open for 2% -> 2% of each run, Pallas kernels for 14% -> 16%
where the time goes in v4:
time: 33.8 us; the launch traced here: 33.6 us
  starting transfers between devices  14.9 us (44%)
  waiting for transfers between devices  8.85 us (26%)
  Pallas kernels  7.63 us (23%)
  other arithmetic  1.51 us (4%)
  between operations  0.75 us (2%)
    ppermute x9, starting transfers between devices, turn(): return lax.ppermute(value, 'ccd', [(i, (i + g) % n) for i in range(n)])  13 us
    pallas_call x10, Pallas kernels, call(): pl.pallas_call(kernel, out_shape=shapes, in_specs=list(spaces), out_specs...  7.63 us
    ppermute x9, waiting for transfers between devices, turn(): return lax.ppermute(value, 'ccd', [(i, (i + g) % n) for i in range(n)])  7.27 us
    ppermute x1, waiting for transfers between devices, body(): lax.ppermute(warped[3], ('row', 'amp'), [(0, 3), (3, 0), (1, 2), (2, 1)])  1.58 us
    ppermute x1, starting transfers between devices, body(): ends = lax.ppermute(warped[1], 'row', swap)  1.56 us
    broadcast_in_dim x1, other arithmetic, body(): return (difference[None], stack.reshape(template.shape))  0.83 us
    add x1, other arithmetic, body(): code = owners.reshape(1, strips) * strips + patch_strip.reshape(1, strips)  0.68 us
  transfers between devices with their start and end apart: 12, of which 5 were waited for; matrix products, arithmetic and copies ran while one was open for 2% of the time, Pallas kernels for 16%

profile of v4, /device:TPU:0, one launch (start us, length us, event | category | flops | bytes accessed | tf_op | source)
XLA Modules:
  0.0 33.6 jit_solution(10451615279828005401)
XLA Ops:
  0.6 0.7 %bitcast_add_fusion.code.refs_0_ = s32[1,8]{1,0:T(1,128)S(1)} fusion(s32[1,1,1,8]{3,2,1,0:T(1,128)} %param.13, s32[1,1,1,8,1]{3,4,2,1,0:T(1,128)} %param.12), kind=kLoop, calls=%fused_computation.1 | loop fusion | flops 16 | bytes 96 | tf_op jit(solution)/shard_map/add | solution.py:460
  1.3 3.0 %collective-permute-start.4 = (s32[1,8]{1,0:T(1,128)S(1)}, s32[1,8]{1,0:T(1,128)S(1)}, u32[]{:S(2)}, u32[]{:S(2)}) collective-permute-start(s32[1,8]{1,0:T(1,128)S(1)} %bitcast_add_fusion.code.refs_0_), channel_id=1, source_target_pairs={{0,4},{4,8},{8,12},{12,0},{1,5},{5,9},{9,13},{13,1},{2,6},{6,10},{... | collective-permute-start | bytes 104 | tf_op jit(solution)/shard_map/ppermute | solution.py:453
  4.3 2.0 %collective-permute-start.2 = (s32[1,8]{1,0:T(1,128)S(1)}, s32[1,8]{1,0:T(1,128)S(1)}, u32[]{:S(2)}, u32[]{:S(2)}) collective-permute-start(s32[1,8]{1,0:T(1,128)S(1)} %bitcast_add_fusion.code.refs_0_), channel_id=1, source_target_pairs={{0,12},{4,0},{8,4},{12,8},{1,13},{5,1},{9,5},{13,9},{2,14},{6,2},{... | collective-permute-start | bytes 104 | tf_op jit(solution)/shard_map/ppermute | solution.py:453
  6.4 1.0 %collective-permute-start = (s32[1,8]{1,0:T(1,128)S(1)}, s32[1,8]{1,0:T(1,128)S(1)}, u32[]{:S(2)}, u32[]{:S(2)}) collective-permute-start(s32[1,8]{1,0:T(1,128)S(1)} %bitcast_add_fusion.code.refs_0_), channel_id=1, source_target_pairs={{0,8},{4,12},{8,0},{12,4},{1,9},{5,13},{9,1},{13,5},{2,10},{6,14},... | collective-permute-start | bytes 104 | tf_op jit(solution)/shard_map/ppermute | solution.py:453
  7.4 1.0 %shard_map.113.template.refs_1_ = bf16[256,512]{1,0:T(8,128)(2,1)S(1)} custom-call(bf16[256,512]{1,0:T(8,128)(2,1)} %bitcast.14), custom_call_target="tpu_custom_call" | custom-call | bytes 1048576 | tf_op jit(solution)/shard_map/pallas_call | solution.py:442
  8.3 0.1 shard_map.116
  8.5 1.6 %collective-permute-start.3 = (bf16[2,32,512]{2,1,0:T(8,128)(2,1)S(1)}, bf16[2,32,512]{2,1,0:T(8,128)(2,1)S(1)}, u32[]{:S(2)}, u32[]{:S(2)}) collective-permute-start(bf16[2,32,512]{2,1,0:T(8,128)(2,1)S(1)} %shard_map.116), channel_id=1, source_target_pairs={{0,4},{4,8},{8,12},{12,0},{1,5},{5,9},{9,13},{13,1},{2,6},{6,10},{... | collective-permute-start | bytes 196616 | tf_op jit(solution)/shard_map/ppermute | solution.py:453
  10.1 0.1 shard_map.117
  10.3 2.3 %collective-permute-start.5 = (bf16[2,32,512]{2,1,0:T(8,128)(2,1)S(1)}, bf16[2,32,512]{2,1,0:T(8,128)(2,1)S(1)}, u32[]{:S(2)}, u32[]{:S(2)}) collective-permute-start(bf16[2,32,512]{2,1,0:T(8,128)(2,1)S(1)} %shard_map.117), channel_id=1, source_target_pairs={{0,12},{4,0},{8,4},{12,8},{1,13},{5,1},{9,5},{13,9},{2,14},{6,2},{... | collective-permute-start | bytes 196616 | tf_op jit(solution)/shard_map/ppermute | solution.py:453
  12.6 0.1 shard_map.114.after
  12.7 0.4 %collective-permute-start.1 = (bf16[2,32,512]{2,1,0:T(8,128)(2,1)S(1)}, bf16[2,32,512]{2,1,0:T(8,128)(2,1)S(1)}, u32[]{:S(2)}, u32[]{:S(2)}) collective-permute-start(bf16[2,32,512]{2,1,0:T(8,128)(2,1)S(1)} %shard_map.114.after), channel_id=1, source_target_pairs={{0,8},{4,12},{8,0},{12,4},{1,9},{5,13},{9,1},{13,5},{2,10},{6,14},... | collective-permute-start | bytes 196616 | tf_op jit(solution)/shard_map/ppermute | solution.py:453
  13.1 2.5 %shard_map.115 = (bf16[2,32,512]{2,1,0:T(8,128)(2,1)S(1)}, bf16[4,768,256]{2,1,0:T(8,128)(2,1)S(1)}, bf16[256,256]{1,0:T(8,128)(2,1)S(1)}, bf16[256,256]{1,0:T(8...) custom-call(f32[3,1,9]{2,1,0:T(1,128)} %bitcast.15, ...), custom_call_target="tpu_custom_call" | custom-call | bytes 1048576 | tf_op jit(solution)/shard_map/pallas_call | solution.py:442
  15.7 0.0 collective-permute-done.3.refs_3_
  15.7 0.0 collective-permute-done.5.refs_4_
  15.7 2.5 %collective-permute-done.1.refs_2_ = bf16[2,32,512]{2,1,0:T(8,128)(2,1)S(1)} collective-permute-done((bf16[2,32,512]{2,1,0:T(8,128)(2,1)S(1)}, bf16[2,32,512]{2,1,0:T(8,128)(2,1)S(1)}, u32[]{:S(2)}, u32[]{:S(2)}) %collective-permute-start.1) | collective-permute-done | bytes 65568 | tf_op jit(solution)/shard_map/ppermute | solution.py:453
  18.1 0.5 %shard_map.118 = (bf16[256,640]{1,0:T(8,128)(2,1)S(1)}, bf16[16,640]{1,0:T(8,128)(2,1)S(1)}, bf16[256,128]{1,0:T(8,128)(2,1)S(1)}, bf16[16,128]{1,0:T(8,128)(2,1)S(1)}) custom-call(bf16[256,256]{1,0:T(8,128)(2,1)S(1)} %get-tuple-element.21.refs_0_, bf16[8,256,128]{2,1,0:T(8,128)(2,1)S(1)} %get-tuple-element.22.refs_1_, ...), custom_call_target="tpu_custom_call" | custom-call | bytes 1048576 | tf_op jit(solution)/shard_map/pallas_call | solution.py:442
  18.6 0.1 collective-permute-start.6
  18.7 1.6 %collective-permute-start.7 = (bf16[16,640]{1,0:T(8,128)(2,1)S(1)}, bf16[16,640]{1,0:T(8,128)(2,1)S(1)}, u32[]{:S(2)}, u32[]{:S(2)}) collective-permute-start(bf16[16,640]{1,0:T(8,128)(2,1)S(1)} %get-tuple-element.26), channel_id=1, source_target_pairs={{0,2},{2,0},{1,3},{3,1},{4,6},{6,4},{5,7},{7,5},{8,10},{10,8},{9,1... | collective-permute-start | bytes 61448 | tf_op jit(solution)/shard_map/ppermute | solution.py:532
  20.3 0.3 collective-permute-start.8
  20.6 0.0 collective-permute-done.6.left.right
  20.6 1.1 %shard_map.119 = (f32[192,512]{1,0:T(8,128)S(1)}, bf16[192,512]{1,0:T(8,128)(2,1)S(1)}) custom-call(bf16[256,640]{1,0:T(8,128)(2,1)S(1)} %get-tuple-element.24.image, bf16[256,128]{1,0:T(8,128)(2,1)S(1)} %collective-permute-done.6.left.right, bf16[256,128]{1,0:T(8,128)(2,1)S(1)} %collective-permute-done.6.left.right, ...), custom_call_target="tpu_custom_call" | custom-call | bytes 1048576 | tf_op jit(solution)/shard_map/pallas_call | solution.py:442
  21.7 1.6 %collective-permute-done.8.top_left.top_right.bottom_left.bottom_right = bf16[16,128]{1,0:T(8,128)(2,1)S(1)} collective-permute-done((bf16[16,128]{1,0:T(8,128)(2,1)S(1)}, bf16[16,128]{1,0:T(8,128)(2,1)S(1)}, u32[]{:S(2)}, u32[]{:S(2)}) %collective-permute-start.8) | collective-permute-done | bytes 4128 | tf_op jit(solution)/shard_map/ppermute | solution.py:533
  23.3 0.9 %shard_map.120 = (f32[64,512]{1,0:T(8,128)S(1)}, bf16[2,32,512]{2,1,0:T(8,128)(2,1)S(1)}, bf16[2,32,512]{2,1,0:T(8,128)(2,1)S(1)}, bf16[2,32,512]{2,1,0:T(8,128)(2,1)S(1)}, bf16[2,32,512]{2,1,0:T(8,128)(2,1)S(1)}) custom-call(bf16[256,640]{1,0:T(8,128)(2,1)S(1)} %get-tuple-element.24.image, bf16[256,128]{1,0:T(8,128)(2,1)S(1)} %collective-permute-done.6.left.right, ...), custom_call_target="tpu_custom_call" | custom-call | bytes 1048576 | tf_op jit(solution)/shard_map/pallas_call | solution.py:442
  24.2 0.4 %collective-permute-start.9 = (bf16[2,32,512]{2,1,0:T(8,128)(2,1)S(1)}, bf16[2,32,512]{2,1,0:T(8,128)(2,1)S(1)}, u32[]{:S(2)}, u32[]{:S(2)}) collective-permute-start(bf16[2,32,512]{2,1,0:T(8,128)(2,1)S(1)} %get-tuple-element.37), channel_id=1, source_target_pairs={{0,8},{4,12},{8,0},{12,4},{1,9},{5,13},{9,1},{13,5},{2,10},{6,14},... | collective-permute-start | bytes 196616 | tf_op jit(solution)/shard_map/ppermute | solution.py:453
  24.6 1.9 %collective-permute-start.10 = (bf16[2,32,512]{2,1,0:T(8,128)(2,1)S(1)}, bf16[2,32,512]{2,1,0:T(8,128)(2,1)S(1)}, u32[]{:S(2)}, u32[]{:S(2)}) collective-permute-start(bf16[2,32,512]{2,1,0:T(8,128)(2,1)S(1)} %get-tuple-element.38), channel_id=1, source_target_pairs={{0,12},{4,0},{8,4},{12,8},{1,13},{5,1},{9,5},{13,9},{2,14},{6,2},{... | collective-permute-start | bytes 196616 | tf_op jit(solution)/shard_map/ppermute | solution.py:453
  26.5 0.3 collective-permute-start.11
  26.8 0.2 shard_map.121.collect
  27.0 0.8 %maximum_bitcast_fusion = f32[1,256,512]{2,1,0:T(8,128)} fusion(f32[32,512]{1,0:T(8,128)S(1)} %get-tuple-element.41, f32[192,512]{1,0:T(8,128)S(1)} %get-tuple-element.35, f32[32,512]{1,0:T(8,128)S(1)} %get-tuple-element.40), kind=kLoop, calls=%fused_computation | loop fusion | flops 262144 | bytes 1048576 | tf_op jit(solution)/shard_map/broadcast_in_dim | solution.py:588
  27.8 2.4 %collective-permute-done.9.refs_0_ = bf16[2,32,512]{2,1,0:T(8,128)(2,1)S(1)} collective-permute-done((bf16[2,32,512]{2,1,0:T(8,128)(2,1)S(1)}, bf16[2,32,512]{2,1,0:T(8,128)(2,1)S(1)}, u32[]{:S(2)}, u32[]{:S(2)}) %collective-permute-start.9) | collective-permute-done | bytes 65568 | tf_op jit(solution)/shard_map/ppermute | solution.py:453
  30.2 0.1 collective-permute-done.10.refs_1_
  30.4 2.3 %collective-permute-done.11.refs_2_ = bf16[2,32,512]{2,1,0:T(8,128)(2,1)S(1)} collective-permute-done((bf16[2,32,512]{2,1,0:T(8,128)(2,1)S(1)}, bf16[2,32,512]{2,1,0:T(8,128)(2,1)S(1)}, u32[]{:S(2)}, u32[]{:S(2)}) %collective-permute-start.11) | collective-permute-done | bytes 65568 | tf_op jit(solution)/shard_map/ppermute | solution.py:453
  32.6 1.0 %shard_map.122 = f32[256,512]{1,0:T(8,128)} custom-call(bf16[256,256]{1,0:T(8,128)(2,1)S(1)} %shard_map.121.collect, bf16[2,32,512]{2,1,0:T(8,128)(2,1)S(1)} %collective-permute-done.9.refs_0_, bf16[2,32,512]{2,1,0:T(8,128)(2,1)S(1)} %collective-permute-done.10.refs_1_, bf16[2,32,512]{2,1,0:T(8,128)(2,1)S(1)} %collective-permute-done.11.refs_2_, ...), custom_call_target="tpu_custom_call" | custom-call | bytes 1048576 | tf_op jit(solution)/shard_map/pallas_call | solution.py:442
  (7 shorter events, 0.0 us)
Async XLA Ops:
  1.3 8.8 %collective-permute-start.4 = (s32[1,8]{1,0:T(1,128)S(1)}, s32[1,8]{1,0:T(1,128)S(1)}, u32[]{:S(2)}, u32[]{:S(2)}) collective-permute-start(s32[1,8]{1,0:T(1,128)S(1)} %bitcast_add_fusion.code.refs_0_), channel_id=1, source_target_pairs={{0,4},{4,8},{8,12},{12,0},{1,5},{5,9},{9,13},{13,1},{2,6},{6,10},{... | collective-permute-start | bytes 104 | tf_op jit(solution)/shard_map/ppermute | solution.py:453
  4.3 4.0 %collective-permute-start.2 = (s32[1,8]{1,0:T(1,128)S(1)}, s32[1,8]{1,0:T(1,128)S(1)}, u32[]{:S(2)}, u32[]{:S(2)}) collective-permute-start(s32[1,8]{1,0:T(1,128)S(1)} %bitcast_add_fusion.code.refs_0_), channel_id=1, source_target_pairs={{0,12},{4,0},{8,4},{12,8},{1,13},{5,1},{9,5},{13,9},{2,14},{6,2},{... | collective-permute-start | bytes 104 | tf_op jit(solution)/shard_map/ppermute | solution.py:453
  6.4 6.2 %collective-permute-start = (s32[1,8]{1,0:T(1,128)S(1)}, s32[1,8]{1,0:T(1,128)S(1)}, u32[]{:S(2)}, u32[]{:S(2)}) collective-permute-start(s32[1,8]{1,0:T(1,128)S(1)} %bitcast_add_fusion.code.refs_0_), channel_id=1, source_target_pairs={{0,8},{4,12},{8,0},{12,4},{1,9},{5,13},{9,1},{13,5},{2,10},{6,14},... | collective-permute-start | bytes 104 | tf_op jit(solution)/shard_map/ppermute | solution.py:453
  8.5 7.2 %collective-permute-start.3 = (bf16[2,32,512]{2,1,0:T(8,128)(2,1)S(1)}, bf16[2,32,512]{2,1,0:T(8,128)(2,1)S(1)}, u32[]{:S(2)}, u32[]{:S(2)}) collective-permute-start(bf16[2,32,512]{2,1,0:T(8,128)(2,1)S(1)} %shard_map.116), channel_id=1, source_target_pairs={{0,4},{4,8},{8,12},{12,0},{1,5},{5,9},{9,13},{13,1},{2,6},{6,10},{... | collective-permute-start | bytes 196616 | tf_op jit(solution)/shard_map/ppermute | solution.py:453
  10.3 5.4 %collective-permute-start.5 = (bf16[2,32,512]{2,1,0:T(8,128)(2,1)S(1)}, bf16[2,32,512]{2,1,0:T(8,128)(2,1)S(1)}, u32[]{:S(2)}, u32[]{:S(2)}) collective-permute-start(bf16[2,32,512]{2,1,0:T(8,128)(2,1)S(1)} %shard_map.117), channel_id=1, source_target_pairs={{0,12},{4,0},{8,4},{12,8},{1,13},{5,1},{9,5},{13,9},{2,14},{6,2},{... | collective-permute-start | bytes 196616 | tf_op jit(solution)/shard_map/ppermute | solution.py:453
  12.7 5.4 %collective-permute-start.1 = (bf16[2,32,512]{2,1,0:T(8,128)(2,1)S(1)}, bf16[2,32,512]{2,1,0:T(8,128)(2,1)S(1)}, u32[]{:S(2)}, u32[]{:S(2)}) collective-permute-start(bf16[2,32,512]{2,1,0:T(8,128)(2,1)S(1)} %shard_map.114.after), channel_id=1, source_target_pairs={{0,8},{4,12},{8,0},{12,4},{1,9},{5,13},{9,1},{13,5},{2,10},{6,14},... | collective-permute-start | bytes 196616 | tf_op jit(solution)/shard_map/ppermute | solution.py:453
  18.6 1.9 %collective-permute-start.6 = (bf16[256,128]{1,0:T(8,128)(2,1)S(1)}, bf16[256,128]{1,0:T(8,128)(2,1)S(1)}, u32[]{:S(2)}, u32[]{:S(2)}) collective-permute-start(bf16[256,128]{1,0:T(8,128)(2,1)S(1)} %get-tuple-element.25), channel_id=1, source_target_pairs={{0,1},{1,0},{2,3},{3,2},{4,5},{5,4},{6,7},{7,6},{8,9},{9,8},{10,11... | collective-permute-start | bytes 196616 | tf_op jit(solution)/shard_map/ppermute | solution.py:531
  18.7 4.6 %collective-permute-start.7 = (bf16[16,640]{1,0:T(8,128)(2,1)S(1)}, bf16[16,640]{1,0:T(8,128)(2,1)S(1)}, u32[]{:S(2)}, u32[]{:S(2)}) collective-permute-start(bf16[16,640]{1,0:T(8,128)(2,1)S(1)} %get-tuple-element.26), channel_id=1, source_target_pairs={{0,2},{2,0},{1,3},{3,1},{4,6},{6,4},{5,7},{7,5},{8,10},{10,8},{9,1... | collective-permute-start | bytes 61448 | tf_op jit(solution)/shard_map/ppermute | solution.py:532
  20.3 3.0 %collective-permute-start.8 = (bf16[16,128]{1,0:T(8,128)(2,1)S(1)}, bf16[16,128]{1,0:T(8,128)(2,1)S(1)}, u32[]{:S(2)}, u32[]{:S(2)}) collective-permute-start(bf16[16,128]{1,0:T(8,128)(2,1)S(1)} %get-tuple-element.27), channel_id=1, source_target_pairs={{0,3},{3,0},{1,2},{2,1},{4,7},{7,4},{5,6},{6,5},{8,11},{11,8},{9,1... | collective-permute-start | bytes 12296 | tf_op jit(solution)/shard_map/ppermute | solution.py:533
  20.6 2.7 %copy-start = (bf16[96,64]{1,0:T(8,128)(2,1)S(1)}, bf16[96,64]{1,0:T(8,128)(2,1)}, u32[]{:S(2)}) copy-start(bf16[96,64]{1,0:T(8,128)(2,1)} %constant.10.clone.bands) | copy-start | bytes 36868
  24.2 6.0 %collective-permute-start.9 = (bf16[2,32,512]{2,1,0:T(8,128)(2,1)S(1)}, bf16[2,32,512]{2,1,0:T(8,128)(2,1)S(1)}, u32[]{:S(2)}, u32[]{:S(2)}) collective-permute-start(bf16[2,32,512]{2,1,0:T(8,128)(2,1)S(1)} %get-tuple-element.37), channel_id=1, source_target_pairs={{0,8},{4,12},{8,0},{12,4},{1,9},{5,13},{9,1},{13,5},{2,10},{6,14},... | collective-permute-start | bytes 196616 | tf_op jit(solution)/shard_map/ppermute | solution.py:453
  24.6 5.7 %collective-permute-start.10 = (bf16[2,32,512]{2,1,0:T(8,128)(2,1)S(1)}, bf16[2,32,512]{2,1,0:T(8,128)(2,1)S(1)}, u32[]{:S(2)}, u32[]{:S(2)}) collective-permute-start(bf16[2,32,512]{2,1,0:T(8,128)(2,1)S(1)} %get-tuple-element.38), channel_id=1, source_target_pairs={{0,12},{4,0},{8,4},{12,8},{1,13},{5,1},{9,5},{13,9},{2,14},{6,2},{... | collective-permute-start | bytes 196616 | tf_op jit(solution)/shard_map/ppermute | solution.py:453
  26.5 6.1 %collective-permute-start.11 = (bf16[2,32,512]{2,1,0:T(8,128)(2,1)S(1)}, bf16[2,32,512]{2,1,0:T(8,128)(2,1)S(1)}, u32[]{:S(2)}, u32[]{:S(2)}) collective-permute-start(bf16[2,32,512]{2,1,0:T(8,128)(2,1)S(1)} %get-tuple-element.39), channel_id=1, source_target_pairs={{0,4},{4,8},{8,12},{12,0},{1,5},{5,9},{9,13},{13,1},{2,6},{6,10},{... | collective-permute-start | bytes 196616 | tf_op jit(solution)/shard_map/ppermute | solution.py:453

commit v5 on v4

--- a/solution.py
+++ b/solution.py
@@ -74,7 +74,7 @@
 
 
 def order_of(n):
-    return (2, 3, 1, 0) if n == 4 else (*range(1, n), 0)
+    return (1, 3, 2, 0) if n == 4 else (*range(1, n), 0)
 
 
 def in_order(values):
@@ -274,7 +274,7 @@
     count = n if ring else 1
     received, rest = from_order(refs[2 : 2 + count]), refs[2 + count :]
     if paired:
-        image, send_row, send_amp, send_diag, rows_done = rest
+        image, send_amp, rows_done = rest
     else:
         image, rows_done = rest
     width = tiles * LANES
@@ -295,13 +295,8 @@
                 value = jnp.where(lane < HALF_TILE, value, 0.0)
             image[rows, b * LANES : (b + 1) * LANES] = value.astype(BF16)
     if paired:
-        band = strips * strip_rows
-        row_first = lax.axis_index("row") == 0
         amp_first = lax.axis_index("amp") == 0
-        edge_rows = jnp.where(row_first, image[band - MARGIN : band, :], image[0:MARGIN, :])
-        send_row[...] = edge_rows
         send_amp[...] = jnp.where(amp_first, image[:, tiles * LANES :], image[:, 0:LANES])
-        send_diag[...] = jnp.where(amp_first, edge_rows[:, tiles * LANES :], edge_rows[:, 0:LANES])
 
 
 def joined(ref, rows, left, right, tiles, amp_count):
@@ -310,6 +305,18 @@
     first = ref[rows, 0:LANES] + jnp.where(amp > 0, left, zero)
     last = ref[rows, tiles * LANES :] + jnp.where(amp < amp_count - 1, right, zero)
     return [first] + [ref[rows, b * LANES : (b + 1) * LANES] for b in range(1, tiles)] + [last]
+
+
+def join_kernel(tiles, amp_count, paired, image, left, right, *outs):
+    size = image.shape[0]
+    edges = []
+    for rows in (slice(0, MARGIN), slice(size - MARGIN, size)):
+        parts = joined(image, rows, left[rows, :], right[rows, :], tiles, amp_count)
+        edges.append(jnp.concatenate(parts, axis=1))
+    if paired:
+        edges = [jnp.where(lax.axis_index("row") == 0, edges[1], edges[0])]
+    for edge, out in zip(edges, outs):
+        out[...] = edge
 
 
 def row_convolved(bands, parts, across, at, count):
@@ -365,19 +372,16 @@
 
 
 def edge_kernel(n, capacity, strips, strip_rows, tiles, row_count, amp_count, ring, image, left, right, top, bottom,
-                top_left, top_right, bottom_left, bottom_right, science, de, bands, backward, gather,
-                columns_mid, diff, *rest):
+                science, de, bands, backward, gather, columns_mid, diff, *rest):
     outs = rest[: n if ring else 1]
     across, lowered, columns = rest[len(outs) :]
     band = strips * strip_rows
     inner = strip_rows + MARGIN
     row = lax.axis_index("row")
     zero = jnp.zeros((), BF16)
-    everything = slice(0, MARGIN)
-    above = [jnp.where(row > 0, part, zero)
-             for part in joined(top, everything, top_left[...], top_right[...], tiles, amp_count)]
-    below = [jnp.where(row < row_count - 1, part, zero)
-             for part in joined(bottom, everything, bottom_left[...], bottom_right[...], tiles, amp_count)]
+    tile = [slice(b * LANES, (b + 1) * LANES) for b in range(tiles + 1)]
+    above = [jnp.where(row > 0, top[:, t], zero) for t in tile]
+    below = [jnp.where(row < row_count - 1, bottom[:, t], zero) for t in tile]
     first, last = slice(0, inner), slice(band - inner, band)
     upper = joined(image, first, left[first, :], right[first, :], tiles, amp_count)
     lower = joined(image, last, left[last, :], right[last, :], tiles, amp_count)
@@ -409,7 +413,7 @@
 
 def sum_kernel(collect, *refs):
     *returned, stack, total, sems = refs
-    values = stacked(from_order(returned))
+    values = stacked(returned[-1:] + returned[:-1])
     copies = []
     half = total.shape[0] // 2
     for i in range(2):
@@ -507,7 +511,7 @@
         [in_hbm(value) for value in (
             coefs.transpose(1, 0, 2), shifts.reshape(2, strips), fractions.reshape(2, strips),
             jnp.asarray(column_bands()), science.reshape(band, width), mid_bands)]
-        + [picked[n // 2 - 1] if two else picked[-1], code] + ([code, template_rows] if two else []),
+        + [picked[0], code] + ([code, template_rows] if two else []),
         [HBM] * 6 + [VMEM, SMEM] + [VMEM] * (2 if two else 0),
         [pltpu.SMEM((3, 1, 9), F32), pltpu.SMEM((2, strips), jnp.int32),
          ((2, strips), F32), ((KINDS, 2 * LANES, LANES), BF16), pltpu.SemaphoreType.DMA((6,))],
@@ -518,40 +522,29 @@
     else:
         received = in_order(exchange(picked, -1))
     image_shape = ((band, padded), BF16)
-    halo_shapes = [((MARGIN, padded), BF16), ((band, LANES), BF16), ((MARGIN, LANES), BF16)]
     warped = call(
         functools.partial(warp_kernel, n, strips, strip_rows, tiles, ring, paired),
-        [image_shape] + (halo_shapes if paired else []),
+        [image_shape] + ([((band, LANES), BF16)] if paired else []),
         [forward, spread, *received],
         [VMEM] * (2 + len(received)),
         [((band, padded + LANES), BF16)],
     )
     image = warped[0]
+    edge_shape = ((MARGIN, padded), BF16)
+    join = functools.partial(join_kernel, tiles, amp_count, paired)
     if paired:
-        side = lax.ppermute(warped[2], "amp", swap)
-        ends = lax.ppermute(warped[1], "row", swap)
-        corner = lax.ppermute(warped[3], ("row", "amp"), [(0, 3), (3, 0), (1, 2), (2, 1)])
-        left = right = side
-        top = bottom = ends
-        top_left = top_right = bottom_left = bottom_right = corner
+        left = right = lax.ppermute(warped[1], "amp", swap)
+        (edge,) = call(join, [edge_shape], [image, left, right], [VMEM] * 3)
+        top = bottom = lax.ppermute(edge, "row", swap)
     else:
-        first, last = image[:MARGIN], image[band - MARGIN :]
-
-        def moved(value, down, along):
-            pairs = []
-            for r in range(row_count):
-                for a in range(amp_count):
-                    if 0 <= r + down < row_count and 0 <= a + along < amp_count:
-                        pairs.append((r * amp_count + a, (r + down) * amp_count + a + along))
-            return lax.ppermute(value, ("row", "amp"), pairs)
-
-        left = moved(image[:, padded - LANES :], 0, 1)
-        right = moved(image[:, :LANES], 0, -1)
-        top, bottom = moved(last, 1, 0), moved(first, -1, 0)
-        top_left = moved(last[:, padded - LANES :], 1, 1)
-        top_right = moved(last[:, :LANES], 1, -1)
-        bottom_left = moved(first[:, padded - LANES :], -1, 1)
-        bottom_right = moved(first[:, :LANES], -1, -1)
+
+        def moved(value, axis, step):
+            count = lax.axis_size(axis)
+            return lax.ppermute(value, axis, [(i, i + step) for i in range(count) if 0 <= i + step < count])
+
+        left, right = moved(image[:, padded - LANES :], "amp", 1), moved(image[:, :LANES], "amp", -1)
+        first, last = call(join, [edge_shape] * 2, [image, left, right], [VMEM] * 3)
+        top, bottom = moved(last, "row", 1), moved(first, "row", -1)
 
     diff_mid, columns_mid = call(
         functools.partial(mid_kernel, strips, strip_rows, tiles, row_count, amp_count),
@@ -564,13 +557,14 @@
     diff_edge, *outgoing = call(
         functools.partial(edge_kernel, n, capacity, strips, strip_rows, tiles, row_count, amp_count, ring),
         [((2 * strip_rows, width), F32)] + outgoing_shapes,
-        [image, left, right, top, bottom, top_left, top_right, bottom_left, bottom_right, science, de,
-         jnp.asarray(row_bands(strip_rows)), backward, gather, columns_mid],
-        [VMEM] * 15,
+        [image, left, right, top, bottom, science, de, jnp.asarray(row_bands(strip_rows)), backward, gather,
+         columns_mid],
+        [VMEM] * 11,
         [((2 * strip_rows, (tiles + 1) * KINDS * LANES), BF16), ((2 * strip_rows, padded + LANES), BF16),
          ((2 * strip_rows, width), BF16)],
     )
-    returned = in_order(exchange(outgoing, 1))
+    returned = exchange(outgoing, 1)
+    returned = returned[1:] + returned[:1]
     (collect,) = call(
         functools.partial(collect_kernel, n, capacity, strips, strip_rows, ring, two),
         [((band, slot_rows), BF16)],

time: 33.8 us -> 33.2 us (0.982)
  waiting for transfers between devices: 8.85 us -> 7.38 us
  starting transfers between devices: 14.9 us -> 15.7 us
    ppermute x9, waiting for transfers between devices: 7.27 us -> 4.99 us  [turn(): return lax.ppermute(value, 'ccd', [(i, (i + g) % n) for i in range(n)])]
    ppermute x9, starting transfers between devices: 13 us -> 14.1 us  [turn(): return lax.ppermute(value, 'ccd', [(i, (i + g) % n) for i in range(n)])]
    ppermute x3 -> x2, waiting for transfers between devices: 1.59 us -> 2.39 us  [the longest x1 1.24 us: body(): left = right = lax.ppermute(warped[1], 'amp', swap)]
    ppermute x3 -> x2, starting transfers between devices: 1.93 us -> 1.63 us  [the longest x1 1.56 us: body(): top = bottom = lax.ppermute(edge, 'row', swap)]
    pallas_call x10 -> x11, Pallas kernels: 7.63 us -> 7.63 us  [call(): pl.pallas_call(kernel, out_shape=shapes, in_specs=list(spaces), out_specs...]
  transfers between devices with their start and end apart: 12 -> 11, of which waited for: 5 -> 7; matrix products, arithmetic and copies ran while one was open for 2% -> 3% of each run, Pallas kernels for 16% -> 16%
where the time goes in v5:
time: 33.2 us; the launch traced here: 33 us
  starting transfers between devices  15.7 us (47%)
  Pallas kernels  7.63 us (23%)
  waiting for transfers between devices  7.38 us (22%)
  other arithmetic  1.51 us (5%)
  between operations  0.73 us (2%)
    ppermute x9, starting transfers between devices, turn(): return lax.ppermute(value, 'ccd', [(i, (i + g) % n) for i in range(n)])  14.1 us
    pallas_call x11, Pallas kernels, call(): pl.pallas_call(kernel, out_shape=shapes, in_specs=list(spaces), out_specs...  7.63 us
    ppermute x9, waiting for transfers between devices, turn(): return lax.ppermute(value, 'ccd', [(i, (i + g) % n) for i in range(n)])  4.99 us
    ppermute x1, starting transfers between devices, body(): top = bottom = lax.ppermute(edge, 'row', swap)  1.56 us
    ppermute x1, waiting for transfers between devices, body(): left = right = lax.ppermute(warped[1], 'amp', swap)  1.24 us
    ppermute x1, waiting for transfers between devices, body(): top = bottom = lax.ppermute(edge, 'row', swap)  1.15 us
    broadcast_in_dim x1, other arithmetic, body(): return (difference[None], stack.reshape(template.shape))  0.83 us
    add x1, other arithmetic, body(): code = owners.reshape(1, strips) * strips + patch_strip.reshape(1, strips)  0.68 us
  transfers between devices with their start and end apart: 11, of which 7 were waited for; matrix products, arithmetic and copies ran while one was open for 3% of the time, Pallas kernels for 16%

profile of v5, /device:TPU:0, one launch (start us, length us, event | category | flops | bytes accessed | tf_op | source)
XLA Modules:
  0.0 33.0 jit_solution(9697254335735431497)
XLA Ops:
  0.6 0.7 %bitcast_add_fusion.code.refs_0_ = s32[1,8]{1,0:T(1,128)S(1)} fusion(s32[1,1,1,8]{3,2,1,0:T(1,128)} %param.13, s32[1,1,1,8,1]{3,4,2,1,0:T(1,128)} %param.12), kind=kLoop, calls=%fused_computation.1 | loop fusion | flops 16 | bytes 96 | tf_op jit(solution)/shard_map/add | solution.py:464
  1.3 4.0 %collective-permute-start.4 = (s32[1,8]{1,0:T(1,128)S(1)}, s32[1,8]{1,0:T(1,128)S(1)}, u32[]{:S(2)}, u32[]{:S(2)}) collective-permute-start(s32[1,8]{1,0:T(1,128)S(1)} %bitcast_add_fusion.code.refs_0_), channel_id=1, source_target_pairs={{0,8},{4,12},{8,0},{12,4},{1,9},{5,13},{9,1},{13,5},{2,10},{6,14},... | collective-permute-start | bytes 104 | tf_op jit(solution)/shard_map/ppermute | solution.py:457
  5.3 1.3 %collective-permute-start.2 = (s32[1,8]{1,0:T(1,128)S(1)}, s32[1,8]{1,0:T(1,128)S(1)}, u32[]{:S(2)}, u32[]{:S(2)}) collective-permute-start(s32[1,8]{1,0:T(1,128)S(1)} %bitcast_add_fusion.code.refs_0_), channel_id=1, source_target_pairs={{0,12},{4,0},{8,4},{12,8},{1,13},{5,1},{9,5},{13,9},{2,14},{6,2},{... | collective-permute-start | bytes 104 | tf_op jit(solution)/shard_map/ppermute | solution.py:457
  6.7 0.7 %collective-permute-start = (s32[1,8]{1,0:T(1,128)S(1)}, s32[1,8]{1,0:T(1,128)S(1)}, u32[]{:S(2)}, u32[]{:S(2)}) collective-permute-start(s32[1,8]{1,0:T(1,128)S(1)} %bitcast_add_fusion.code.refs_0_), channel_id=1, source_target_pairs={{0,4},{4,8},{8,12},{12,0},{1,5},{5,9},{9,13},{13,1},{2,6},{6,10},{... | collective-permute-start | bytes 104 | tf_op jit(solution)/shard_map/ppermute | solution.py:457
  7.4 1.0 %shard_map.113.template.refs_1_ = bf16[256,512]{1,0:T(8,128)(2,1)S(1)} custom-call(bf16[256,512]{1,0:T(8,128)(2,1)} %bitcast.14), custom_call_target="tpu_custom_call" | custom-call | bytes 1048576 | tf_op jit(solution)/shard_map/pallas_call | solution.py:446
  8.3 0.5 %collective-permute-done.2.code.refs_3_ = s32[1,8]{1,0:T(1,128)S(1)} collective-permute-done((s32[1,8]{1,0:T(1,128)S(1)}, s32[1,8]{1,0:T(1,128)S(1)}, u32[]{:S(2)}, u32[]{:S(2)}) %collective-permute-start.2) | collective-permute-done | bytes 64 | tf_op jit(solution)/shard_map/ppermute | solution.py:457
  8.9 0.1 shard_map.116
  9.0 1.6 %collective-permute-start.3 = (bf16[2,32,512]{2,1,0:T(8,128)(2,1)S(1)}, bf16[2,32,512]{2,1,0:T(8,128)(2,1)S(1)}, u32[]{:S(2)}, u32[]{:S(2)}) collective-permute-start(bf16[2,32,512]{2,1,0:T(8,128)(2,1)S(1)} %shard_map.116), channel_id=1, source_target_pairs={{0,4},{4,8},{8,12},{12,0},{1,5},{5,9},{9,13},{13,1},{2,6},{6,10},{... | collective-permute-start | bytes 196616 | tf_op jit(solution)/shard_map/ppermute | solution.py:457
  10.7 0.1 shard_map.117
  10.8 2.2 %collective-permute-start.5 = (bf16[2,32,512]{2,1,0:T(8,128)(2,1)S(1)}, bf16[2,32,512]{2,1,0:T(8,128)(2,1)S(1)}, u32[]{:S(2)}, u32[]{:S(2)}) collective-permute-start(bf16[2,32,512]{2,1,0:T(8,128)(2,1)S(1)} %shard_map.117), channel_id=1, source_target_pairs={{0,8},{4,12},{8,0},{12,4},{1,9},{5,13},{9,1},{13,5},{2,10},{6,14},... | collective-permute-start | bytes 196616 | tf_op jit(solution)/shard_map/ppermute | solution.py:457
  13.0 0.0 collective-permute-done.code.refs_1_
  13.0 0.1 shard_map.114.after
  13.2 0.3 collective-permute-start.1
  13.5 2.5 %shard_map.115 = (bf16[2,32,512]{2,1,0:T(8,128)(2,1)S(1)}, bf16[4,768,256]{2,1,0:T(8,128)(2,1)S(1)}, bf16[256,256]{1,0:T(8,128)(2,1)S(1)}, bf16[256,256]{1,0:T(8...) custom-call(f32[3,1,9]{2,1,0:T(1,128)} %bitcast.15, ...), custom_call_target="tpu_custom_call" | custom-call | bytes 1048576 | tf_op jit(solution)/shard_map/pallas_call | solution.py:446
  16.0 0.0 collective-permute-done.3.refs_3_
  16.0 0.8 %collective-permute-done.5.refs_4_ = bf16[2,32,512]{2,1,0:T(8,128)(2,1)S(1)} collective-permute-done((bf16[2,32,512]{2,1,0:T(8,128)(2,1)S(1)}, bf16[2,32,512]{2,1,0:T(8,128)(2,1)S(1)}, u32[]{:S(2)}, u32[]{:S(2)}) %collective-permute-start.5) | collective-permute-done | bytes 65568 | tf_op jit(solution)/shard_map/ppermute | solution.py:457
  16.9 0.7 %collective-permute-done.1.refs_2_ = bf16[2,32,512]{2,1,0:T(8,128)(2,1)S(1)} collective-permute-done((bf16[2,32,512]{2,1,0:T(8,128)(2,1)S(1)}, bf16[2,32,512]{2,1,0:T(8,128)(2,1)S(1)}, u32[]{:S(2)}, u32[]{:S(2)}) %collective-permute-start.1) | collective-permute-done | bytes 65568 | tf_op jit(solution)/shard_map/ppermute | solution.py:457
  17.6 0.5 %shard_map.118 = (bf16[256,640]{1,0:T(8,128)(2,1)S(1)}, bf16[256,128]{1,0:T(8,128)(2,1)S(1)}) custom-call(bf16[256,256]{1,0:T(8,128)(2,1)S(1)} %get-tuple-element.19.refs_0_, bf16[8,256,128]{2,1,0:T(8,128)(2,1)S(1)} %get-tuple-element.20.refs_1_, bf16[2,32,512]{2,1,0:T(8,128)(2,1)S(1)} %collective-permute-done.1.refs_2_, ...), custom_call_target="tpu_custom_call" | custom-call | bytes 1048576 | tf_op jit(solution)/shard_map/pallas_call | solution.py:446
  18.1 0.1 collective-permute-start.6
  18.1 1.2 %collective-permute-done.6.left.right = bf16[256,128]{1,0:T(8,128)(2,1)S(1)} collective-permute-done((bf16[256,128]{1,0:T(8,128)(2,1)S(1)}, bf16[256,128]{1,0:T(8,128)(2,1)S(1)}, u32[]{:S(2)}, u32[]{:S(2)}) %collective-permute-start.6) | collective-permute-done | bytes 65568 | tf_op jit(solution)/shard_map/ppermute | solution.py:536
  19.4 1.6 %collective-permute-start.7 = (bf16[16,640]{1,0:T(8,128)(2,1)S(1)}, bf16[16,640]{1,0:T(8,128)(2,1)S(1)}, u32[]{:S(2)}, u32[]{:S(2)}) collective-permute-start(bf16[16,640]{1,0:T(8,128)(2,1)S(1)} %shard_map.119), channel_id=1, source_target_pairs={{0,2},{2,0},{1,3},{3,1},{4,6},{6,4},{5,7},{7,5},{8,10},{10,8},{9,1... | collective-permute-start | bytes 61448 | tf_op jit(solution)/shard_map/ppermute | solution.py:538
  21.0 1.1 %shard_map.120 = (f32[192,512]{1,0:T(8,128)S(1)}, bf16[192,512]{1,0:T(8,128)(2,1)S(1)}) custom-call(bf16[256,640]{1,0:T(8,128)(2,1)S(1)} %get-tuple-element.22.image, bf16[256,128]{1,0:T(8,128)(2,1)S(1)} %collective-permute-done.6.left.right, bf16[256,128]{1,0:T(8,128)(2,1)S(1)} %collective-permute-done.6.left.right, ...), custom_call_target="tpu_custom_call" | custom-call | bytes 1048576 | tf_op jit(solution)/shard_map/pallas_call | solution.py:446
  22.1 1.1 %collective-permute-done.7.top.bottom = bf16[16,640]{1,0:T(8,128)(2,1)S(1)} collective-permute-done((bf16[16,640]{1,0:T(8,128)(2,1)S(1)}, bf16[16,640]{1,0:T(8,128)(2,1)S(1)}, u32[]{:S(2)}, u32[]{:S(2)}) %collective-permute-start.7) | collective-permute-done | bytes 20512 | tf_op jit(solution)/shard_map/ppermute | solution.py:538
  23.3 0.9 %shard_map.121 = (f32[64,512]{1,0:T(8,128)S(1)}, bf16[2,32,512]{2,1,0:T(8,128)(2,1)S(1)}, bf16[2,32,512]{2,1,0:T(8,128)(2,1)S(1)}, bf16[2,32,512]{2,1,0:T(8,128)(2,1)S(1)}, bf16[2,32,512]{2,1,0:T(8,128)(2,1)S(1)}) custom-call(bf16[256,640]{1,0:T(8,128)(2,1)S(1)} %get-tuple-element.22.image, bf16[256,128]{1,0:T(8,128)(2,1)S(1)} %collective-permute-done.6.left.right, ...), custom_call_target="tpu_custom_call" | custom-call | bytes 1048576 | tf_op jit(solution)/shard_map/pallas_call | solution.py:446
  24.2 0.6 %collective-permute-start.8 = (bf16[2,32,512]{2,1,0:T(8,128)(2,1)S(1)}, bf16[2,32,512]{2,1,0:T(8,128)(2,1)S(1)}, u32[]{:S(2)}, u32[]{:S(2)}) collective-permute-start(bf16[2,32,512]{2,1,0:T(8,128)(2,1)S(1)} %get-tuple-element.33), channel_id=1, source_target_pairs={{0,4},{4,8},{8,12},{12,0},{1,5},{5,9},{9,13},{13,1},{2,6},{6,10},{... | collective-permute-start | bytes 196616 | tf_op jit(solution)/shard_map/ppermute | solution.py:457
  24.8 2.2 %collective-permute-start.9 = (bf16[2,32,512]{2,1,0:T(8,128)(2,1)S(1)}, bf16[2,32,512]{2,1,0:T(8,128)(2,1)S(1)}, u32[]{:S(2)}, u32[]{:S(2)}) collective-permute-start(bf16[2,32,512]{2,1,0:T(8,128)(2,1)S(1)} %get-tuple-element.34), channel_id=1, source_target_pairs={{0,8},{4,12},{8,0},{12,4},{1,9},{5,13},{9,1},{13,5},{2,10},{6,14},... | collective-permute-start | bytes 196616 | tf_op jit(solution)/shard_map/ppermute | solution.py:457
  27.0 1.0 %collective-permute-start.10 = (bf16[2,32,512]{2,1,0:T(8,128)(2,1)S(1)}, bf16[2,32,512]{2,1,0:T(8,128)(2,1)S(1)}, u32[]{:S(2)}, u32[]{:S(2)}) collective-permute-start(bf16[2,32,512]{2,1,0:T(8,128)(2,1)S(1)} %get-tuple-element.35), channel_id=1, source_target_pairs={{0,12},{4,0},{8,4},{12,8},{1,13},{5,1},{9,5},{13,9},{2,14},{6,2},{... | collective-permute-start | bytes 196616 | tf_op jit(solution)/shard_map/ppermute | solution.py:457
  28.1 0.2 shard_map.122.collect
  28.2 0.8 %maximum_bitcast_fusion = f32[1,256,512]{2,1,0:T(8,128)} fusion(f32[32,512]{1,0:T(8,128)S(1)} %get-tuple-element.37, f32[192,512]{1,0:T(8,128)S(1)} %get-tuple-element.31, f32[32,512]{1,0:T(8,128)S(1)} %get-tuple-element.36), kind=kLoop, calls=%fused_computation | loop fusion | flops 262144 | bytes 1048576 | tf_op jit(solution)/shard_map/broadcast_in_dim | solution.py:582
  29.1 1.5 %collective-permute-done.8.refs_0_ = bf16[2,32,512]{2,1,0:T(8,128)(2,1)S(1)} collective-permute-done((bf16[2,32,512]{2,1,0:T(8,128)(2,1)S(1)}, bf16[2,32,512]{2,1,0:T(8,128)(2,1)S(1)}, u32[]{:S(2)}, u32[]{:S(2)}) %collective-permute-start.8) | collective-permute-done | bytes 65568 | tf_op jit(solution)/shard_map/ppermute | solution.py:457
  30.6 1.4 %collective-permute-done.9.refs_1_ = bf16[2,32,512]{2,1,0:T(8,128)(2,1)S(1)} collective-permute-done((bf16[2,32,512]{2,1,0:T(8,128)(2,1)S(1)}, bf16[2,32,512]{2,1,0:T(8,128)(2,1)S(1)}, u32[]{:S(2)}, u32[]{:S(2)}) %collective-permute-start.9) | collective-permute-done | bytes 65568 | tf_op jit(solution)/shard_map/ppermute | solution.py:457
  32.0 1.0 %shard_map.123 = f32[256,512]{1,0:T(8,128)} custom-call(bf16[256,256]{1,0:T(8,128)(2,1)S(1)} %shard_map.122.collect, bf16[2,32,512]{2,1,0:T(8,128)(2,1)S(1)} %collective-permute-done.8.refs_0_, bf16[2,32,512]{2,1,0:T(8,128)(2,1)S(1)} %collective-permute-done.9.refs_1_, bf16[2,32,512]{2,1,0:T(8,128)(2,1)S(1)} %collective-permute-done.10.refs_2_, ...), custom_call_target="tpu_custom_call" | custom-call | bytes 1048576 | tf_op jit(solution)/shard_map/pallas_call | solution.py:446
  (6 shorter events, 0.0 us)
Async XLA Ops:
  1.3 9.4 %collective-permute-start.4 = (s32[1,8]{1,0:T(1,128)S(1)}, s32[1,8]{1,0:T(1,128)S(1)}, u32[]{:S(2)}, u32[]{:S(2)}) collective-permute-start(s32[1,8]{1,0:T(1,128)S(1)} %bitcast_add_fusion.code.refs_0_), channel_id=1, source_target_pairs={{0,8},{4,12},{8,0},{12,4},{1,9},{5,13},{9,1},{13,5},{2,10},{6,14},... | collective-permute-start | bytes 104 | tf_op jit(solution)/shard_map/ppermute | solution.py:457
  5.3 3.5 %collective-permute-start.2 = (s32[1,8]{1,0:T(1,128)S(1)}, s32[1,8]{1,0:T(1,128)S(1)}, u32[]{:S(2)}, u32[]{:S(2)}) collective-permute-start(s32[1,8]{1,0:T(1,128)S(1)} %bitcast_add_fusion.code.refs_0_), channel_id=1, source_target_pairs={{0,12},{4,0},{8,4},{12,8},{1,13},{5,1},{9,5},{13,9},{2,14},{6,2},{... | collective-permute-start | bytes 104 | tf_op jit(solution)/shard_map/ppermute | solution.py:457
  6.7 6.3 %collective-permute-start = (s32[1,8]{1,0:T(1,128)S(1)}, s32[1,8]{1,0:T(1,128)S(1)}, u32[]{:S(2)}, u32[]{:S(2)}) collective-permute-start(s32[1,8]{1,0:T(1,128)S(1)} %bitcast_add_fusion.code.refs_0_), channel_id=1, source_target_pairs={{0,4},{4,8},{8,12},{12,0},{1,5},{5,9},{9,13},{13,1},{2,6},{6,10},{... | collective-permute-start | bytes 104 | tf_op jit(solution)/shard_map/ppermute | solution.py:457
  9.0 7.0 %collective-permute-start.3 = (bf16[2,32,512]{2,1,0:T(8,128)(2,1)S(1)}, bf16[2,32,512]{2,1,0:T(8,128)(2,1)S(1)}, u32[]{:S(2)}, u32[]{:S(2)}) collective-permute-start(bf16[2,32,512]{2,1,0:T(8,128)(2,1)S(1)} %shard_map.116), channel_id=1, source_target_pairs={{0,4},{4,8},{8,12},{12,0},{1,5},{5,9},{9,13},{13,1},{2,6},{6,10},{... | collective-permute-start | bytes 196616 | tf_op jit(solution)/shard_map/ppermute | solution.py:457
  10.8 6.1 %collective-permute-start.5 = (bf16[2,32,512]{2,1,0:T(8,128)(2,1)S(1)}, bf16[2,32,512]{2,1,0:T(8,128)(2,1)S(1)}, u32[]{:S(2)}, u32[]{:S(2)}) collective-permute-start(bf16[2,32,512]{2,1,0:T(8,128)(2,1)S(1)} %shard_map.117), channel_id=1, source_target_pairs={{0,8},{4,12},{8,0},{12,4},{1,9},{5,13},{9,1},{13,5},{2,10},{6,14},... | collective-permute-start | bytes 196616 | tf_op jit(solution)/shard_map/ppermute | solution.py:457
  13.2 4.4 %collective-permute-start.1 = (bf16[2,32,512]{2,1,0:T(8,128)(2,1)S(1)}, bf16[2,32,512]{2,1,0:T(8,128)(2,1)S(1)}, u32[]{:S(2)}, u32[]{:S(2)}) collective-permute-start(bf16[2,32,512]{2,1,0:T(8,128)(2,1)S(1)} %shard_map.114.after), channel_id=1, source_target_pairs={{0,12},{4,0},{8,4},{12,8},{1,13},{5,1},{9,5},{13,9},{2,14},{6,2},{... | collective-permute-start | bytes 196616 | tf_op jit(solution)/shard_map/ppermute | solution.py:457
  18.1 1.3 %collective-permute-start.6 = (bf16[256,128]{1,0:T(8,128)(2,1)S(1)}, bf16[256,128]{1,0:T(8,128)(2,1)S(1)}, u32[]{:S(2)}, u32[]{:S(2)}) collective-permute-start(bf16[256,128]{1,0:T(8,128)(2,1)S(1)} %get-tuple-element.23), channel_id=1, source_target_pairs={{0,1},{1,0},{2,3},{3,2},{4,5},{5,4},{6,7},{7,6},{8,9},{9,8},{10,11... | collective-permute-start | bytes 196616 | tf_op jit(solution)/shard_map/ppermute | solution.py:536
  19.4 3.8 %collective-permute-start.7 = (bf16[16,640]{1,0:T(8,128)(2,1)S(1)}, bf16[16,640]{1,0:T(8,128)(2,1)S(1)}, u32[]{:S(2)}, u32[]{:S(2)}) collective-permute-start(bf16[16,640]{1,0:T(8,128)(2,1)S(1)} %shard_map.119), channel_id=1, source_target_pairs={{0,2},{2,0},{1,3},{3,1},{4,6},{6,4},{5,7},{7,5},{8,10},{10,8},{9,1... | collective-permute-start | bytes 61448 | tf_op jit(solution)/shard_map/ppermute | solution.py:538
  21.0 2.3 %copy-start = (bf16[96,64]{1,0:T(8,128)(2,1)S(1)}, bf16[96,64]{1,0:T(8,128)(2,1)}, u32[]{:S(2)}) copy-start(bf16[96,64]{1,0:T(8,128)(2,1)} %constant.10.clone.bands) | copy-start | bytes 36868
  24.2 6.4 %collective-permute-start.8 = (bf16[2,32,512]{2,1,0:T(8,128)(2,1)S(1)}, bf16[2,32,512]{2,1,0:T(8,128)(2,1)S(1)}, u32[]{:S(2)}, u32[]{:S(2)}) collective-permute-start(bf16[2,32,512]{2,1,0:T(8,128)(2,1)S(1)} %get-tuple-element.33), channel_id=1, source_target_pairs={{0,4},{4,8},{8,12},{12,0},{1,5},{5,9},{9,13},{13,1},{2,6},{6,10},{... | collective-permute-start | bytes 196616 | tf_op jit(solution)/shard_map/ppermute | solution.py:457
  24.8 7.1 %collective-permute-start.9 = (bf16[2,32,512]{2,1,0:T(8,128)(2,1)S(1)}, bf16[2,32,512]{2,1,0:T(8,128)(2,1)S(1)}, u32[]{:S(2)}, u32[]{:S(2)}) collective-permute-start(bf16[2,32,512]{2,1,0:T(8,128)(2,1)S(1)} %get-tuple-element.34), channel_id=1, source_target_pairs={{0,8},{4,12},{8,0},{12,4},{1,9},{5,13},{9,1},{13,5},{2,10},{6,14},... | collective-permute-start | bytes 196616 | tf_op jit(solution)/shard_map/ppermute | solution.py:457
  27.0 4.9 %collective-permute-start.10 = (bf16[2,32,512]{2,1,0:T(8,128)(2,1)S(1)}, bf16[2,32,512]{2,1,0:T(8,128)(2,1)S(1)}, u32[]{:S(2)}, u32[]{:S(2)}) collective-permute-start(bf16[2,32,512]{2,1,0:T(8,128)(2,1)S(1)} %get-tuple-element.35), channel_id=1, source_target_pairs={{0,12},{4,0},{8,4},{12,8},{1,13},{5,1},{9,5},{13,9},{2,14},{6,2},{... | collective-permute-start | bytes 196616 | tf_op jit(solution)/shard_map/ppermute | solution.py:457

commit v6 on v5

--- a/solution.py
+++ b/solution.py
@@ -269,14 +269,26 @@
     return jnp.concatenate(parts, axis=0) if len(parts) > 1 else parts[0]
 
 
-def warp_kernel(n, strips, strip_rows, tiles, ring, paired, *refs):
+def side_kernel(n, strips, strip_rows, tiles, forward, spread, *refs):
+    out = refs[-1]
+    pool = stacked(from_order(refs[:n]))
+    first = lax.axis_index("amp") == 0
+    source = jnp.where(first, pool[:, (tiles - 1) * LANES :], pool[:, 0:LANES])
+    rows_done = jnp.dot(forward[...], source, preferred_element_type=F32).astype(BF16)
+    lane = lane_index(strip_rows)
+    inside = (lane < HALF_TILE) == first
+    for q in range(strips):
+        rows = slice(q * strip_rows, (q + 1) * strip_rows)
+        taps = jnp.where(first, spread[q, 0:LANES, :], spread[q, LANES : 2 * LANES, :])
+        value = jnp.dot(rows_done[rows], taps, preferred_element_type=F32)
+        out[rows, :] = jnp.where(inside, value, 0.0).astype(BF16)
+
+
+def warp_kernel(n, strips, strip_rows, tiles, ring, *refs):
     forward, spread = refs[:2]
     count = n if ring else 1
     received, rest = from_order(refs[2 : 2 + count]), refs[2 + count :]
-    if paired:
-        image, send_amp, rows_done = rest
-    else:
-        image, rows_done = rest
+    image, rows_done = rest
     width = tiles * LANES
     clear_ends(rows_done, tiles)
     rows_done[:, LANES : LANES + width] = jnp.dot(
@@ -294,9 +306,6 @@
             if b == tiles:
                 value = jnp.where(lane < HALF_TILE, value, 0.0)
             image[rows, b * LANES : (b + 1) * LANES] = value.astype(BF16)
-    if paired:
-        amp_first = lax.axis_index("amp") == 0
-        send_amp[...] = jnp.where(amp_first, image[:, tiles * LANES :], image[:, 0:LANES])
 
 
 def joined(ref, rows, left, right, tiles, amp_count):
@@ -437,7 +446,7 @@
     padded = width + LANES
     ring = n <= 4
     two = ring and capacity == 2 and strips == 2 * n
-    paired = row_count == 2 and amp_count == 2
+    paired = row_count == 2 and amp_count == 2 and two
     swap = [(0, 1), (1, 0)]
     strip_shape = (capacity, strip_rows, width)
 
@@ -522,18 +531,24 @@
     else:
         received = in_order(exchange(picked, -1))
     image_shape = ((band, padded), BF16)
-    warped = call(
-        functools.partial(warp_kernel, n, strips, strip_rows, tiles, ring, paired),
-        [image_shape] + ([((band, LANES), BF16)] if paired else []),
+    if paired:
+        (beside,) = call(
+            functools.partial(side_kernel, n, strips, strip_rows, tiles),
+            [((band, LANES), BF16)],
+            [forward, spread, *received],
+            [VMEM] * (2 + n),
+        )
+        left = right = lax.ppermute(beside, "amp", swap)
+    (image,) = call(
+        functools.partial(warp_kernel, n, strips, strip_rows, tiles, ring),
+        [image_shape],
         [forward, spread, *received],
         [VMEM] * (2 + len(received)),
         [((band, padded + LANES), BF16)],
     )
-    image = warped[0]
     edge_shape = ((MARGIN, padded), BF16)
     join = functools.partial(join_kernel, tiles, amp_count, paired)
     if paired:
-        left = right = lax.ppermute(warped[1], "amp", swap)
         (edge,) = call(join, [edge_shape], [image, left, right], [VMEM] * 3)
         top = bottom = lax.ppermute(edge, "row", swap)
     else:

time: 33.2 us -> 33 us (level)
  waiting for transfers between devices: 7.38 us -> 6.89 us
    ppermute x1, waiting for transfers between devices: 1.24 us -> 0.75 us  [body(): left = right = lax.ppermute(beside, 'amp', swap)]
    pallas_call x11 -> x12, Pallas kernels: 7.63 us -> 7.95 us  [call(): pl.pallas_call(kernel, out_shape=shapes, in_specs=list(spaces), out_specs...]
  transfers between devices with their start and end apart: 11 -> 11, of which waited for: 7 -> 7; matrix products, arithmetic and copies ran while one was open for 3% -> 3% of each run, Pallas kernels for 16% -> 17%
where the time goes in v6:
time: 33 us; the launch traced here: 32.8 us
  starting transfers between devices  15.7 us (48%)
  Pallas kernels  7.95 us (24%)
  waiting for transfers between devices  6.89 us (21%)
  other arithmetic  1.51 us (5%)
  between operations  0.74 us (2%)
    ppermute x9, starting transfers between devices, turn(): return lax.ppermute(value, 'ccd', [(i, (i + g) % n) for i in range(n)])  14.1 us
    pallas_call x12, Pallas kernels, call(): pl.pallas_call(kernel, out_shape=shapes, in_specs=list(spaces), out_specs...  7.95 us
    ppermute x9, waiting for transfers between devices, turn(): return lax.ppermute(value, 'ccd', [(i, (i + g) % n) for i in range(n)])  4.99 us
    ppermute x1, starting transfers between devices, body(): top = bottom = lax.ppermute(edge, 'row', swap)  1.56 us
    ppermute x1, waiting for transfers between devices, body(): top = bottom = lax.ppermute(edge, 'row', swap)  1.15 us
    broadcast_in_dim x1, other arithmetic, body(): return (difference[None], stack.reshape(template.shape))  0.83 us
    ppermute x1, waiting for transfers between devices, body(): left = right = lax.ppermute(beside, 'amp', swap)  0.75 us
    add x1, other arithmetic, body(): code = owners.reshape(1, strips) * strips + patch_strip.reshape(1, strips)  0.68 us
  transfers between devices with their start and end apart: 11, of which 7 were waited for; matrix products, arithmetic and copies ran while one was open for 3% of the time, Pallas kernels for 17%

profile of v6, /device:TPU:0, one launch (start us, length us, event | category | flops | bytes accessed | tf_op | source)
XLA Modules:
  0.0 32.8 jit_solution(8505622191487383745)
XLA Ops:
  0.6 0.7 %bitcast_add_fusion.code.refs_0_ = s32[1,8]{1,0:T(1,128)S(1)} fusion(s32[1,1,1,8]{3,2,1,0:T(1,128)} %param.13, s32[1,1,1,8,1]{3,4,2,1,0:T(1,128)} %param.12), kind=kLoop, calls=%fused_computation.1 | loop fusion | flops 16 | bytes 96 | tf_op jit(solution)/shard_map/add | solution.py:473
  1.3 4.0 %collective-permute-start.4 = (s32[1,8]{1,0:T(1,128)S(1)}, s32[1,8]{1,0:T(1,128)S(1)}, u32[]{:S(2)}, u32[]{:S(2)}) collective-permute-start(s32[1,8]{1,0:T(1,128)S(1)} %bitcast_add_fusion.code.refs_0_), channel_id=1, source_target_pairs={{0,8},{4,12},{8,0},{12,4},{1,9},{5,13},{9,1},{13,5},{2,10},{6,14},... | collective-permute-start | bytes 104 | tf_op jit(solution)/shard_map/ppermute | solution.py:466
  5.3 1.3 %collective-permute-start.2 = (s32[1,8]{1,0:T(1,128)S(1)}, s32[1,8]{1,0:T(1,128)S(1)}, u32[]{:S(2)}, u32[]{:S(2)}) collective-permute-start(s32[1,8]{1,0:T(1,128)S(1)} %bitcast_add_fusion.code.refs_0_), channel_id=1, source_target_pairs={{0,12},{4,0},{8,4},{12,8},{1,13},{5,1},{9,5},{13,9},{2,14},{6,2},{... | collective-permute-start | bytes 104 | tf_op jit(solution)/shard_map/ppermute | solution.py:466
  6.7 0.7 %collective-permute-start = (s32[1,8]{1,0:T(1,128)S(1)}, s32[1,8]{1,0:T(1,128)S(1)}, u32[]{:S(2)}, u32[]{:S(2)}) collective-permute-start(s32[1,8]{1,0:T(1,128)S(1)} %bitcast_add_fusion.code.refs_0_), channel_id=1, source_target_pairs={{0,4},{4,8},{8,12},{12,0},{1,5},{5,9},{9,13},{13,1},{2,6},{6,10},{... | collective-permute-start | bytes 104 | tf_op jit(solution)/shard_map/ppermute | solution.py:466
  7.4 1.0 %shard_map.113.template.refs_1_ = bf16[256,512]{1,0:T(8,128)(2,1)S(1)} custom-call(bf16[256,512]{1,0:T(8,128)(2,1)} %bitcast.14), custom_call_target="tpu_custom_call" | custom-call | bytes 1048576 | tf_op jit(solution)/shard_map/pallas_call | solution.py:455
  8.3 0.5 %collective-permute-done.2.code.refs_3_ = s32[1,8]{1,0:T(1,128)S(1)} collective-permute-done((s32[1,8]{1,0:T(1,128)S(1)}, s32[1,8]{1,0:T(1,128)S(1)}, u32[]{:S(2)}, u32[]{:S(2)}) %collective-permute-start.2) | collective-permute-done | bytes 64 | tf_op jit(solution)/shard_map/ppermute | solution.py:466
  8.9 0.1 shard_map.116
  9.0 1.6 %collective-permute-start.3 = (bf16[2,32,512]{2,1,0:T(8,128)(2,1)S(1)}, bf16[2,32,512]{2,1,0:T(8,128)(2,1)S(1)}, u32[]{:S(2)}, u32[]{:S(2)}) collective-permute-start(bf16[2,32,512]{2,1,0:T(8,128)(2,1)S(1)} %shard_map.116), channel_id=1, source_target_pairs={{0,4},{4,8},{8,12},{12,0},{1,5},{5,9},{9,13},{13,1},{2,6},{6,10},{... | collective-permute-start | bytes 196616 | tf_op jit(solution)/shard_map/ppermute | solution.py:466
  10.7 0.0 collective-permute-done.4.code.refs_2_
  10.7 0.1 shard_map.117
  10.8 2.2 %collective-permute-start.5 = (bf16[2,32,512]{2,1,0:T(8,128)(2,1)S(1)}, bf16[2,32,512]{2,1,0:T(8,128)(2,1)S(1)}, u32[]{:S(2)}, u32[]{:S(2)}) collective-permute-start(bf16[2,32,512]{2,1,0:T(8,128)(2,1)S(1)} %shard_map.117), channel_id=1, source_target_pairs={{0,8},{4,12},{8,0},{12,4},{1,9},{5,13},{9,1},{13,5},{2,10},{6,14},... | collective-permute-start | bytes 196616 | tf_op jit(solution)/shard_map/ppermute | solution.py:466
  13.0 0.1 shard_map.114.after
  13.2 0.3 collective-permute-start.1
  13.5 2.5 %shard_map.115 = (bf16[2,32,512]{2,1,0:T(8,128)(2,1)S(1)}, bf16[4,768,256]{2,1,0:T(8,128)(2,1)S(1)}, bf16[256,256]{1,0:T(8,128)(2,1)S(1)}, bf16[256,256]{1,0:T(8...) custom-call(f32[3,1,9]{2,1,0:T(1,128)} %bitcast.15, ...), custom_call_target="tpu_custom_call" | custom-call | bytes 1048576 | tf_op jit(solution)/shard_map/pallas_call | solution.py:455
  16.0 0.8 %collective-permute-done.5.refs_4_.refs_2_ = bf16[2,32,512]{2,1,0:T(8,128)(2,1)S(1)} collective-permute-done((bf16[2,32,512]{2,1,0:T(8,128)(2,1)S(1)}, bf16[2,32,512]{2,1,0:T(8,128)(2,1)S(1)}, u32[]{:S(2)}, u32[]{:S(2)}) %collective-permute-start.5) | collective-permute-done | bytes 65568 | tf_op jit(solution)/shard_map/ppermute | solution.py:466
  16.9 0.7 %collective-permute-done.1.refs_2_.refs_0_ = bf16[2,32,512]{2,1,0:T(8,128)(2,1)S(1)} collective-permute-done((bf16[2,32,512]{2,1,0:T(8,128)(2,1)S(1)}, bf16[2,32,512]{2,1,0:T(8,128)(2,1)S(1)}, u32[]{:S(2)}, u32[]{:S(2)}) %collective-permute-start.1) | collective-permute-done | bytes 65568 | tf_op jit(solution)/shard_map/ppermute | solution.py:466
  17.6 0.3 %shard_map.119 = bf16[256,128]{1,0:T(8,128)(2,1)S(1)} custom-call(bf16[256,256]{1,0:T(8,128)(2,1)S(1)} %get-tuple-element.17.refs_0_.forward, bf16[8,256,128]{2,1,0:T(8,128)(2,1)S(1)} %get-tuple-element.18.refs_1_.spread, bf16[2,32,512]{2,1,0:T(8,128)(2,1)S(1)} %collective-permute-done.1.refs_2_.refs_0_, ...), custom_call_target="tpu_custom_call" | custom-call | bytes 1048576 | tf_op jit(solution)/shard_map/pallas_call | solution.py:455
  17.9 0.1 collective-permute-start.6
  18.0 0.5 %shard_map.118.image = bf16[256,640]{1,0:T(8,128)(2,1)S(1)} custom-call(bf16[256,256]{1,0:T(8,128)(2,1)S(1)} %get-tuple-element.17.refs_0_.forward, bf16[8,256,128]{2,1,0:T(8,128)(2,1)S(1)} %get-tuple-element.18.refs_1_.spread, bf16[2,32,512]{2,1,0:T(8,128)(2,1)S(1)} %collective-permute-done.1.refs_2_.refs_0_, ...), custom_call_target="tpu_custom_call" | custom-call | bytes 1048576 | tf_op jit(solution)/shard_map/pallas_call | solution.py:455
  18.5 0.8 %collective-permute-done.6.left.right = bf16[256,128]{1,0:T(8,128)(2,1)S(1)} collective-permute-done((bf16[256,128]{1,0:T(8,128)(2,1)S(1)}, bf16[256,128]{1,0:T(8,128)(2,1)S(1)}, u32[]{:S(2)}, u32[]{:S(2)}) %collective-permute-start.6) | collective-permute-done | bytes 65568 | tf_op jit(solution)/shard_map/ppermute | solution.py:541
  19.2 1.6 %collective-permute-start.7 = (bf16[16,640]{1,0:T(8,128)(2,1)S(1)}, bf16[16,640]{1,0:T(8,128)(2,1)S(1)}, u32[]{:S(2)}, u32[]{:S(2)}) collective-permute-start(bf16[16,640]{1,0:T(8,128)(2,1)S(1)} %shard_map.120), channel_id=1, source_target_pairs={{0,2},{2,0},{1,3},{3,1},{4,6},{6,4},{5,7},{7,5},{8,10},{10,8},{9,1... | collective-permute-start | bytes 61448 | tf_op jit(solution)/shard_map/ppermute | solution.py:553
  20.8 1.1 %shard_map.121 = (f32[192,512]{1,0:T(8,128)S(1)}, bf16[192,512]{1,0:T(8,128)(2,1)S(1)}) custom-call(bf16[256,640]{1,0:T(8,128)(2,1)S(1)} %shard_map.118.image, bf16[256,128]{1,0:T(8,128)(2,1)S(1)} %collective-permute-done.6.left.right, bf16[256,128]{1,0:T(8,128)(2,1)S(1)} %collective-permute-done.6.left.right, f32[256,512]{1,0:T(8,128)S(1)} %get-tuple-element.20.science, ...), custom_call_target="tpu_custom_call" | custom-call | bytes 1048576 | tf_op jit(solution)/shard_map/pallas_call | solution.py:455
  21.9 1.1 %collective-permute-done.7.top.bottom = bf16[16,640]{1,0:T(8,128)(2,1)S(1)} collective-permute-done((bf16[16,640]{1,0:T(8,128)(2,1)S(1)}, bf16[16,640]{1,0:T(8,128)(2,1)S(1)}, u32[]{:S(2)}, u32[]{:S(2)}) %collective-permute-start.7) | collective-permute-done | bytes 20512 | tf_op jit(solution)/shard_map/ppermute | solution.py:553
  23.1 0.9 %shard_map.122 = (f32[64,512]{1,0:T(8,128)S(1)}, bf16[2,32,512]{2,1,0:T(8,128)(2,1)S(1)}, bf16[2,32,512]{2,1,0:T(8,128)(2,1)S(1)}, bf16[2,32,512]{2,1,0:T(8,128)(2,1)S(1)}, bf16[2,32,512]{2,1,0:T(8,128)(2,1)S(1)}) custom-call(bf16[256,640]{1,0:T(8,128)(2,1)S(1)} %shard_map.118.image, bf16[256,128]{1,0:T(8,128)(2,1)S(1)} %collective-permute-done.6.left.right, ...), custom_call_target="tpu_custom_call" | custom-call | bytes 1048576 | tf_op jit(solution)/shard_map/pallas_call | solution.py:455
  24.0 0.6 %collective-permute-start.8 = (bf16[2,32,512]{2,1,0:T(8,128)(2,1)S(1)}, bf16[2,32,512]{2,1,0:T(8,128)(2,1)S(1)}, u32[]{:S(2)}, u32[]{:S(2)}) collective-permute-start(bf16[2,32,512]{2,1,0:T(8,128)(2,1)S(1)} %get-tuple-element.29), channel_id=1, source_target_pairs={{0,4},{4,8},{8,12},{12,0},{1,5},{5,9},{9,13},{13,1},{2,6},{6,10},{... | collective-permute-start | bytes 196616 | tf_op jit(solution)/shard_map/ppermute | solution.py:466
  24.7 2.2 %collective-permute-start.9 = (bf16[2,32,512]{2,1,0:T(8,128)(2,1)S(1)}, bf16[2,32,512]{2,1,0:T(8,128)(2,1)S(1)}, u32[]{:S(2)}, u32[]{:S(2)}) collective-permute-start(bf16[2,32,512]{2,1,0:T(8,128)(2,1)S(1)} %get-tuple-element.30), channel_id=1, source_target_pairs={{0,8},{4,12},{8,0},{12,4},{1,9},{5,13},{9,1},{13,5},{2,10},{6,14},... | collective-permute-start | bytes 196616 | tf_op jit(solution)/shard_map/ppermute | solution.py:466
  26.9 1.0 %collective-permute-start.10 = (bf16[2,32,512]{2,1,0:T(8,128)(2,1)S(1)}, bf16[2,32,512]{2,1,0:T(8,128)(2,1)S(1)}, u32[]{:S(2)}, u32[]{:S(2)}) collective-permute-start(bf16[2,32,512]{2,1,0:T(8,128)(2,1)S(1)} %get-tuple-element.31), channel_id=1, source_target_pairs={{0,12},{4,0},{8,4},{12,8},{1,13},{5,1},{9,5},{13,9},{2,14},{6,2},{... | collective-permute-start | bytes 196616 | tf_op jit(solution)/shard_map/ppermute | solution.py:466
  27.9 0.2 shard_map.123.collect
  28.1 0.8 %maximum_bitcast_fusion = f32[1,256,512]{2,1,0:T(8,128)} fusion(f32[32,512]{1,0:T(8,128)S(1)} %get-tuple-element.33, f32[192,512]{1,0:T(8,128)S(1)} %get-tuple-element.27, f32[32,512]{1,0:T(8,128)S(1)} %get-tuple-element.32), kind=kLoop, calls=%fused_computation | loop fusion | flops 262144 | bytes 1048576 | tf_op jit(solution)/shard_map/broadcast_in_dim | solution.py:597
  28.9 1.5 %collective-permute-done.8.refs_0_ = bf16[2,32,512]{2,1,0:T(8,128)(2,1)S(1)} collective-permute-done((bf16[2,32,512]{2,1,0:T(8,128)(2,1)S(1)}, bf16[2,32,512]{2,1,0:T(8,128)(2,1)S(1)}, u32[]{:S(2)}, u32[]{:S(2)}) %collective-permute-start.8) | collective-permute-done | bytes 65568 | tf_op jit(solution)/shard_map/ppermute | solution.py:466
  30.4 1.4 %collective-permute-done.9.refs_1_ = bf16[2,32,512]{2,1,0:T(8,128)(2,1)S(1)} collective-permute-done((bf16[2,32,512]{2,1,0:T(8,128)(2,1)S(1)}, bf16[2,32,512]{2,1,0:T(8,128)(2,1)S(1)}, u32[]{:S(2)}, u32[]{:S(2)}) %collective-permute-start.9) | collective-permute-done | bytes 65568 | tf_op jit(solution)/shard_map/ppermute | solution.py:466
  31.8 1.0 %shard_map.124 = f32[256,512]{1,0:T(8,128)} custom-call(bf16[256,256]{1,0:T(8,128)(2,1)S(1)} %shard_map.123.collect, bf16[2,32,512]{2,1,0:T(8,128)(2,1)S(1)} %collective-permute-done.8.refs_0_, bf16[2,32,512]{2,1,0:T(8,128)(2,1)S(1)} %collective-permute-done.9.refs_1_, bf16[2,32,512]{2,1,0:T(8,128)(2,1)S(1)} %collective-permute-done.10.refs_2_, ...), custom_call_target="tpu_custom_call" | custom-call | bytes 1048576 | tf_op jit(solution)/shard_map/pallas_call | solution.py:455
  (7 shorter events, 0.0 us)
Async XLA Ops:
  1.3 9.4 %collective-permute-start.4 = (s32[1,8]{1,0:T(1,128)S(1)}, s32[1,8]{1,0:T(1,128)S(1)}, u32[]{:S(2)}, u32[]{:S(2)}) collective-permute-start(s32[1,8]{1,0:T(1,128)S(1)} %bitcast_add_fusion.code.refs_0_), channel_id=1, source_target_pairs={{0,8},{4,12},{8,0},{12,4},{1,9},{5,13},{9,1},{13,5},{2,10},{6,14},... | collective-permute-start | bytes 104 | tf_op jit(solution)/shard_map/ppermute | solution.py:466
  5.3 3.5 %collective-permute-start.2 = (s32[1,8]{1,0:T(1,128)S(1)}, s32[1,8]{1,0:T(1,128)S(1)}, u32[]{:S(2)}, u32[]{:S(2)}) collective-permute-start(s32[1,8]{1,0:T(1,128)S(1)} %bitcast_add_fusion.code.refs_0_), channel_id=1, source_target_pairs={{0,12},{4,0},{8,4},{12,8},{1,13},{5,1},{9,5},{13,9},{2,14},{6,2},{... | collective-permute-start | bytes 104 | tf_op jit(solution)/shard_map/ppermute | solution.py:466
  6.7 6.3 %collective-permute-start = (s32[1,8]{1,0:T(1,128)S(1)}, s32[1,8]{1,0:T(1,128)S(1)}, u32[]{:S(2)}, u32[]{:S(2)}) collective-permute-start(s32[1,8]{1,0:T(1,128)S(1)} %bitcast_add_fusion.code.refs_0_), channel_id=1, source_target_pairs={{0,4},{4,8},{8,12},{12,0},{1,5},{5,9},{9,13},{13,1},{2,6},{6,10},{... | collective-permute-start | bytes 104 | tf_op jit(solution)/shard_map/ppermute | solution.py:466
  9.0 7.0 %collective-permute-start.3 = (bf16[2,32,512]{2,1,0:T(8,128)(2,1)S(1)}, bf16[2,32,512]{2,1,0:T(8,128)(2,1)S(1)}, u32[]{:S(2)}, u32[]{:S(2)}) collective-permute-start(bf16[2,32,512]{2,1,0:T(8,128)(2,1)S(1)} %shard_map.116), channel_id=1, source_target_pairs={{0,4},{4,8},{8,12},{12,0},{1,5},{5,9},{9,13},{13,1},{2,6},{6,10},{... | collective-permute-start | bytes 196616 | tf_op jit(solution)/shard_map/ppermute | solution.py:466
  10.8 6.1 %collective-permute-start.5 = (bf16[2,32,512]{2,1,0:T(8,128)(2,1)S(1)}, bf16[2,32,512]{2,1,0:T(8,128)(2,1)S(1)}, u32[]{:S(2)}, u32[]{:S(2)}) collective-permute-start(bf16[2,32,512]{2,1,0:T(8,128)(2,1)S(1)} %shard_map.117), channel_id=1, source_target_pairs={{0,8},{4,12},{8,0},{12,4},{1,9},{5,13},{9,1},{13,5},{2,10},{6,14},... | collective-permute-start | bytes 196616 | tf_op jit(solution)/shard_map/ppermute | solution.py:466
  13.2 4.4 %collective-permute-start.1 = (bf16[2,32,512]{2,1,0:T(8,128)(2,1)S(1)}, bf16[2,32,512]{2,1,0:T(8,128)(2,1)S(1)}, u32[]{:S(2)}, u32[]{:S(2)}) collective-permute-start(bf16[2,32,512]{2,1,0:T(8,128)(2,1)S(1)} %shard_map.114.after), channel_id=1, source_target_pairs={{0,12},{4,0},{8,4},{12,8},{1,13},{5,1},{9,5},{13,9},{2,14},{6,2},{... | collective-permute-start | bytes 196616 | tf_op jit(solution)/shard_map/ppermute | solution.py:466
  17.9 1.3 %collective-permute-start.6 = (bf16[256,128]{1,0:T(8,128)(2,1)S(1)}, bf16[256,128]{1,0:T(8,128)(2,1)S(1)}, u32[]{:S(2)}, u32[]{:S(2)}) collective-permute-start(bf16[256,128]{1,0:T(8,128)(2,1)S(1)} %shard_map.119), channel_id=1, source_target_pairs={{0,1},{1,0},{2,3},{3,2},{4,5},{5,4},{6,7},{7,6},{8,9},{9,8},{10,11... | collective-permute-start | bytes 196616 | tf_op jit(solution)/shard_map/ppermute | solution.py:541
  19.2 3.8 %collective-permute-start.7 = (bf16[16,640]{1,0:T(8,128)(2,1)S(1)}, bf16[16,640]{1,0:T(8,128)(2,1)S(1)}, u32[]{:S(2)}, u32[]{:S(2)}) collective-permute-start(bf16[16,640]{1,0:T(8,128)(2,1)S(1)} %shard_map.120), channel_id=1, source_target_pairs={{0,2},{2,0},{1,3},{3,1},{4,6},{6,4},{5,7},{7,5},{8,10},{10,8},{9,1... | collective-permute-start | bytes 61448 | tf_op jit(solution)/shard_map/ppermute | solution.py:553
  20.8 2.3 %copy-start = (bf16[96,64]{1,0:T(8,128)(2,1)S(1)}, bf16[96,64]{1,0:T(8,128)(2,1)}, u32[]{:S(2)}) copy-start(bf16[96,64]{1,0:T(8,128)(2,1)} %constant.10.clone.bands) | copy-start | bytes 36868
  24.0 6.4 %collective-permute-start.8 = (bf16[2,32,512]{2,1,0:T(8,128)(2,1)S(1)}, bf16[2,32,512]{2,1,0:T(8,128)(2,1)S(1)}, u32[]{:S(2)}, u32[]{:S(2)}) collective-permute-start(bf16[2,32,512]{2,1,0:T(8,128)(2,1)S(1)} %get-tuple-element.29), channel_id=1, source_target_pairs={{0,4},{4,8},{8,12},{12,0},{1,5},{5,9},{9,13},{13,1},{2,6},{6,10},{... | collective-permute-start | bytes 196616 | tf_op jit(solution)/shard_map/ppermute | solution.py:466
  24.7 7.1 %collective-permute-start.9 = (bf16[2,32,512]{2,1,0:T(8,128)(2,1)S(1)}, bf16[2,32,512]{2,1,0:T(8,128)(2,1)S(1)}, u32[]{:S(2)}, u32[]{:S(2)}) collective-permute-start(bf16[2,32,512]{2,1,0:T(8,128)(2,1)S(1)} %get-tuple-element.30), channel_id=1, source_target_pairs={{0,8},{4,12},{8,0},{12,4},{1,9},{5,13},{9,1},{13,5},{2,10},{6,14},... | collective-permute-start | bytes 196616 | tf_op jit(solution)/shard_map/ppermute | solution.py:466
  26.9 4.9 %collective-permute-start.10 = (bf16[2,32,512]{2,1,0:T(8,128)(2,1)S(1)}, bf16[2,32,512]{2,1,0:T(8,128)(2,1)S(1)}, u32[]{:S(2)}, u32[]{:S(2)}) collective-permute-start(bf16[2,32,512]{2,1,0:T(8,128)(2,1)S(1)} %get-tuple-element.31), channel_id=1, source_target_pairs={{0,12},{4,0},{8,4},{12,8},{1,13},{5,1},{9,5},{13,9},{2,14},{6,2},{... | collective-permute-start | bytes 196616 | tf_op jit(solution)/shard_map/ppermute | solution.py:466

commit v7 on v6

--- a/solution.py
+++ b/solution.py
@@ -418,6 +418,27 @@
     size = capacity * strip_rows * (1 if ring else n)
     for g, out in enumerate(outs):
         out[...] = result[g * size : (g + 1) * size].reshape(out.shape)
+
+
+def begin_kernel(collect, own, first, out):
+    values = stacked([own, first])
+    out[...] = jnp.dot(collect[:, 0 : values.shape[0]], values, preferred_element_type=F32)
+
+
+def end_kernel(begun, collect, *refs):
+    *returned, stack, total, sems = refs
+    values = stacked(returned)
+    copies = []
+    half = total.shape[0] // 2
+    for i in range(2):
+        rows = pl.ds(i * half, half)
+        more = jnp.dot(collect[rows, collect.shape[1] - values.shape[0] :], values, preferred_element_type=F32)
+        total[rows, :] = begun[rows, :] + more
+        copy = pltpu.make_async_copy(total.at[rows], stack.at[rows], sems.at[i])
+        copy.start()
+        copies.append(copy)
+    for copy in copies:
+        copy.wait()
 
 
 def sum_kernel(collect, *refs):
@@ -586,13 +607,23 @@
         [outgoing[0], *codes],
         [VMEM] + [VMEM if two else SMEM] * len(codes),
     )
-    (stack,) = call(
-        sum_kernel,
-        [pltpu.HBM((band, width), F32)],
-        [collect, *returned],
-        [VMEM] * (1 + len(returned)),
-        [((band, width), F32), pltpu.SemaphoreType.DMA((2,))],
-    )
+    if two:
+        (begun,) = call(begin_kernel, [((band, width), F32)], [collect, returned[-1], returned[0]], [VMEM] * 3)
+        (stack,) = call(
+            end_kernel,
+            [pltpu.HBM((band, width), F32)],
+            [begun, collect, *returned[1:-1]],
+            [VMEM] * n,
+            [((band, width), F32), pltpu.SemaphoreType.DMA((2,))],
+        )
+    else:
+        (stack,) = call(
+            sum_kernel,
+            [pltpu.HBM((band, width), F32)],
+            [collect, *returned],
+            [VMEM] * (1 + len(returned)),
+            [((band, width), F32), pltpu.SemaphoreType.DMA((2,))],
+        )
     difference = jnp.concatenate([diff_edge[:strip_rows], diff_mid, diff_edge[strip_rows:]])
     return difference[None], stack.reshape(template.shape)
 

time: 33 us -> 33 us (level)
    pallas_call x12 -> x13, Pallas kernels: 7.95 us -> 8.13 us  [call(): pl.pallas_call(kernel, out_shape=shapes, in_specs=list(spaces), out_specs...]
  transfers between devices with their start and end apart: 11 -> 11, of which waited for: 7 -> 7; matrix products, arithmetic and copies ran while one was open for 3% -> 3% of each run, Pallas kernels for 17% -> 18%
where the time goes in v7:
time: 33 us; the launch traced here: 32.8 us
  starting transfers between devices  15.7 us (48%)
  Pallas kernels  8.13 us (25%)
  waiting for transfers between devices  6.68 us (20%)
  other arithmetic  1.51 us (5%)
  between operations  0.75 us (2%)
    ppermute x9, starting transfers between devices, turn(): return lax.ppermute(value, 'ccd', [(i, (i + g) % n) for i in range(n)])  14.1 us
    pallas_call x13, Pallas kernels, call(): pl.pallas_call(kernel, out_shape=shapes, in_specs=list(spaces), out_specs...  8.13 us
    ppermute x9, waiting for transfers between devices, turn(): return lax.ppermute(value, 'ccd', [(i, (i + g) % n) for i in range(n)])  4.78 us
    ppermute x1, starting transfers between devices, body(): top = bottom = lax.ppermute(edge, 'row', swap)  1.56 us
    ppermute x1, waiting for transfers between devices, body(): top = bottom = lax.ppermute(edge, 'row', swap)  1.15 us
    broadcast_in_dim x1, other arithmetic, body(): return (difference[None], stack.reshape(template.shape))  0.83 us
    ppermute x1, waiting for transfers between devices, body(): left = right = lax.ppermute(beside, 'amp', swap)  0.75 us
    add x1, other arithmetic, body(): code = owners.reshape(1, strips) * strips + patch_strip.reshape(1, strips)  0.68 us
  transfers between devices with their start and end apart: 11, of which 7 were waited for; matrix products, arithmetic and copies ran while one was open for 3% of the time, Pallas kernels for 18%

profile of v7, /device:TPU:0, one launch (start us, length us, event | category | flops | bytes accessed | tf_op | source)
XLA Modules:
  0.0 32.8 jit_solution(13597272059117381803)
XLA Ops:
  0.6 0.7 %bitcast_add_fusion.code.refs_0_ = s32[1,8]{1,0:T(1,128)S(1)} fusion(s32[1,1,1,8]{3,2,1,0:T(1,128)} %param.13, s32[1,1,1,8,1]{3,4,2,1,0:T(1,128)} %param.12), kind=kLoop, calls=%fused_computation.1 | loop fusion | flops 16 | bytes 96 | tf_op jit(solution)/shard_map/add | solution.py:494
  1.3 4.0 %collective-permute-start.4 = (s32[1,8]{1,0:T(1,128)S(1)}, s32[1,8]{1,0:T(1,128)S(1)}, u32[]{:S(2)}, u32[]{:S(2)}) collective-permute-start(s32[1,8]{1,0:T(1,128)S(1)} %bitcast_add_fusion.code.refs_0_), channel_id=1, source_target_pairs={{0,8},{4,12},{8,0},{12,4},{1,9},{5,13},{9,1},{13,5},{2,10},{6,14},... | collective-permute-start | bytes 104 | tf_op jit(solution)/shard_map/ppermute | solution.py:487
  5.3 1.3 %collective-permute-start.2 = (s32[1,8]{1,0:T(1,128)S(1)}, s32[1,8]{1,0:T(1,128)S(1)}, u32[]{:S(2)}, u32[]{:S(2)}) collective-permute-start(s32[1,8]{1,0:T(1,128)S(1)} %bitcast_add_fusion.code.refs_0_), channel_id=1, source_target_pairs={{0,12},{4,0},{8,4},{12,8},{1,13},{5,1},{9,5},{13,9},{2,14},{6,2},{... | collective-permute-start | bytes 104 | tf_op jit(solution)/shard_map/ppermute | solution.py:487
  6.7 0.7 %collective-permute-start = (s32[1,8]{1,0:T(1,128)S(1)}, s32[1,8]{1,0:T(1,128)S(1)}, u32[]{:S(2)}, u32[]{:S(2)}) collective-permute-start(s32[1,8]{1,0:T(1,128)S(1)} %bitcast_add_fusion.code.refs_0_), channel_id=1, source_target_pairs={{0,4},{4,8},{8,12},{12,0},{1,5},{5,9},{9,13},{13,1},{2,6},{6,10},{... | collective-permute-start | bytes 104 | tf_op jit(solution)/shard_map/ppermute | solution.py:487
  7.4 1.0 %shard_map.113.template.refs_1_ = bf16[256,512]{1,0:T(8,128)(2,1)S(1)} custom-call(bf16[256,512]{1,0:T(8,128)(2,1)} %bitcast.14), custom_call_target="tpu_custom_call" | custom-call | bytes 1048576 | tf_op jit(solution)/shard_map/pallas_call | solution.py:476
  8.3 0.5 %collective-permute-done.2.code.refs_3_ = s32[1,8]{1,0:T(1,128)S(1)} collective-permute-done((s32[1,8]{1,0:T(1,128)S(1)}, s32[1,8]{1,0:T(1,128)S(1)}, u32[]{:S(2)}, u32[]{:S(2)}) %collective-permute-start.2) | collective-permute-done | bytes 64 | tf_op jit(solution)/shard_map/ppermute | solution.py:487
  8.9 0.1 shard_map.116
  9.0 1.6 %collective-permute-start.3 = (bf16[2,32,512]{2,1,0:T(8,128)(2,1)S(1)}, bf16[2,32,512]{2,1,0:T(8,128)(2,1)S(1)}, u32[]{:S(2)}, u32[]{:S(2)}) collective-permute-start(bf16[2,32,512]{2,1,0:T(8,128)(2,1)S(1)} %shard_map.116), channel_id=1, source_target_pairs={{0,4},{4,8},{8,12},{12,0},{1,5},{5,9},{9,13},{13,1},{2,6},{6,10},{... | collective-permute-start | bytes 196616 | tf_op jit(solution)/shard_map/ppermute | solution.py:487
  10.7 0.1 shard_map.117
  10.8 2.2 %collective-permute-start.5 = (bf16[2,32,512]{2,1,0:T(8,128)(2,1)S(1)}, bf16[2,32,512]{2,1,0:T(8,128)(2,1)S(1)}, u32[]{:S(2)}, u32[]{:S(2)}) collective-permute-start(bf16[2,32,512]{2,1,0:T(8,128)(2,1)S(1)} %shard_map.117), channel_id=1, source_target_pairs={{0,8},{4,12},{8,0},{12,4},{1,9},{5,13},{9,1},{13,5},{2,10},{6,14},... | collective-permute-start | bytes 196616 | tf_op jit(solution)/shard_map/ppermute | solution.py:487
  13.0 0.1 shard_map.114.after
  13.2 0.3 collective-permute-start.1
  13.5 2.5 %shard_map.115 = (bf16[2,32,512]{2,1,0:T(8,128)(2,1)S(1)}, bf16[4,768,256]{2,1,0:T(8,128)(2,1)S(1)}, bf16[256,256]{1,0:T(8,128)(2,1)S(1)}, bf16[256,256]{1,0:T(8...) custom-call(f32[3,1,9]{2,1,0:T(1,128)} %bitcast.15, ...), custom_call_target="tpu_custom_call" | custom-call | bytes 1048576 | tf_op jit(solution)/shard_map/pallas_call | solution.py:476
  16.0 0.8 %collective-permute-done.5.refs_4_.refs_2_ = bf16[2,32,512]{2,1,0:T(8,128)(2,1)S(1)} collective-permute-done((bf16[2,32,512]{2,1,0:T(8,128)(2,1)S(1)}, bf16[2,32,512]{2,1,0:T(8,128)(2,1)S(1)}, u32[]{:S(2)}, u32[]{:S(2)}) %collective-permute-start.5) | collective-permute-done | bytes 65568 | tf_op jit(solution)/shard_map/ppermute | solution.py:487
  16.9 0.7 %collective-permute-done.1.refs_2_.refs_0_ = bf16[2,32,512]{2,1,0:T(8,128)(2,1)S(1)} collective-permute-done((bf16[2,32,512]{2,1,0:T(8,128)(2,1)S(1)}, bf16[2,32,512]{2,1,0:T(8,128)(2,1)S(1)}, u32[]{:S(2)}, u32[]{:S(2)}) %collective-permute-start.1) | collective-permute-done | bytes 65568 | tf_op jit(solution)/shard_map/ppermute | solution.py:487
  17.6 0.3 %shard_map.119 = bf16[256,128]{1,0:T(8,128)(2,1)S(1)} custom-call(bf16[256,256]{1,0:T(8,128)(2,1)S(1)} %get-tuple-element.17.refs_0_.forward, bf16[8,256,128]{2,1,0:T(8,128)(2,1)S(1)} %get-tuple-element.18.refs_1_.spread, bf16[2,32,512]{2,1,0:T(8,128)(2,1)S(1)} %collective-permute-done.1.refs_2_.refs_0_, ...), custom_call_target="tpu_custom_call" | custom-call | bytes 1048576 | tf_op jit(solution)/shard_map/pallas_call | solution.py:476
  17.9 0.1 collective-permute-start.6
  18.0 0.5 %shard_map.118.image = bf16[256,640]{1,0:T(8,128)(2,1)S(1)} custom-call(bf16[256,256]{1,0:T(8,128)(2,1)S(1)} %get-tuple-element.17.refs_0_.forward, bf16[8,256,128]{2,1,0:T(8,128)(2,1)S(1)} %get-tuple-element.18.refs_1_.spread, bf16[2,32,512]{2,1,0:T(8,128)(2,1)S(1)} %collective-permute-done.1.refs_2_.refs_0_, ...), custom_call_target="tpu_custom_call" | custom-call | bytes 1048576 | tf_op jit(solution)/shard_map/pallas_call | solution.py:476
  18.5 0.8 %collective-permute-done.6.left.right = bf16[256,128]{1,0:T(8,128)(2,1)S(1)} collective-permute-done((bf16[256,128]{1,0:T(8,128)(2,1)S(1)}, bf16[256,128]{1,0:T(8,128)(2,1)S(1)}, u32[]{:S(2)}, u32[]{:S(2)}) %collective-permute-start.6) | collective-permute-done | bytes 65568 | tf_op jit(solution)/shard_map/ppermute | solution.py:562
  19.2 1.6 %collective-permute-start.7 = (bf16[16,640]{1,0:T(8,128)(2,1)S(1)}, bf16[16,640]{1,0:T(8,128)(2,1)S(1)}, u32[]{:S(2)}, u32[]{:S(2)}) collective-permute-start(bf16[16,640]{1,0:T(8,128)(2,1)S(1)} %shard_map.120), channel_id=1, source_target_pairs={{0,2},{2,0},{1,3},{3,1},{4,6},{6,4},{5,7},{7,5},{8,10},{10,8},{9,1... | collective-permute-start | bytes 61448 | tf_op jit(solution)/shard_map/ppermute | solution.py:574
  20.8 1.1 %shard_map.121 = (f32[192,512]{1,0:T(8,128)S(1)}, bf16[192,512]{1,0:T(8,128)(2,1)S(1)}) custom-call(bf16[256,640]{1,0:T(8,128)(2,1)S(1)} %shard_map.118.image, bf16[256,128]{1,0:T(8,128)(2,1)S(1)} %collective-permute-done.6.left.right, bf16[256,128]{1,0:T(8,128)(2,1)S(1)} %collective-permute-done.6.left.right, f32[256,512]{1,0:T(8,128)S(1)} %get-tuple-element.20.science, ...), custom_call_target="tpu_custom_call" | custom-call | bytes 1048576 | tf_op jit(solution)/shard_map/pallas_call | solution.py:476
  21.9 1.1 %collective-permute-done.7.top.bottom = bf16[16,640]{1,0:T(8,128)(2,1)S(1)} collective-permute-done((bf16[16,640]{1,0:T(8,128)(2,1)S(1)}, bf16[16,640]{1,0:T(8,128)(2,1)S(1)}, u32[]{:S(2)}, u32[]{:S(2)}) %collective-permute-start.7) | collective-permute-done | bytes 20512 | tf_op jit(solution)/shard_map/ppermute | solution.py:574
  23.1 0.9 %shard_map.122 = (f32[64,512]{1,0:T(8,128)S(1)}, bf16[2,32,512]{2,1,0:T(8,128)(2,1)S(1)}, bf16[2,32,512]{2,1,0:T(8,128)(2,1)S(1)}, bf16[2,32,512]{2,1,0:T(8,128)(2,1)S(1)}, bf16[2,32,512]{2,1,0:T(8,128)(2,1)S(1)}) custom-call(bf16[256,640]{1,0:T(8,128)(2,1)S(1)} %shard_map.118.image, bf16[256,128]{1,0:T(8,128)(2,1)S(1)} %collective-permute-done.6.left.right, ...), custom_call_target="tpu_custom_call" | custom-call | bytes 1048576 | tf_op jit(solution)/shard_map/pallas_call | solution.py:476
  24.0 0.6 %collective-permute-start.8 = (bf16[2,32,512]{2,1,0:T(8,128)(2,1)S(1)}, bf16[2,32,512]{2,1,0:T(8,128)(2,1)S(1)}, u32[]{:S(2)}, u32[]{:S(2)}) collective-permute-start(bf16[2,32,512]{2,1,0:T(8,128)(2,1)S(1)} %get-tuple-element.29), channel_id=1, source_target_pairs={{0,4},{4,8},{8,12},{12,0},{1,5},{5,9},{9,13},{13,1},{2,6},{6,10},{... | collective-permute-start | bytes 196616 | tf_op jit(solution)/shard_map/ppermute | solution.py:487
  24.7 2.2 %collective-permute-start.9 = (bf16[2,32,512]{2,1,0:T(8,128)(2,1)S(1)}, bf16[2,32,512]{2,1,0:T(8,128)(2,1)S(1)}, u32[]{:S(2)}, u32[]{:S(2)}) collective-permute-start(bf16[2,32,512]{2,1,0:T(8,128)(2,1)S(1)} %get-tuple-element.30), channel_id=1, source_target_pairs={{0,8},{4,12},{8,0},{12,4},{1,9},{5,13},{9,1},{13,5},{2,10},{6,14},... | collective-permute-start | bytes 196616 | tf_op jit(solution)/shard_map/ppermute | solution.py:487
  26.9 1.0 %collective-permute-start.10 = (bf16[2,32,512]{2,1,0:T(8,128)(2,1)S(1)}, bf16[2,32,512]{2,1,0:T(8,128)(2,1)S(1)}, u32[]{:S(2)}, u32[]{:S(2)}) collective-permute-start(bf16[2,32,512]{2,1,0:T(8,128)(2,1)S(1)} %get-tuple-element.31), channel_id=1, source_target_pairs={{0,12},{4,0},{8,4},{12,8},{1,13},{5,1},{9,5},{13,9},{2,14},{6,2},{... | collective-permute-start | bytes 196616 | tf_op jit(solution)/shard_map/ppermute | solution.py:487
  27.9 0.2 shard_map.123.collect
  28.1 0.8 %maximum_bitcast_fusion = f32[1,256,512]{2,1,0:T(8,128)} fusion(f32[32,512]{1,0:T(8,128)S(1)} %get-tuple-element.33, f32[192,512]{1,0:T(8,128)S(1)} %get-tuple-element.27, f32[32,512]{1,0:T(8,128)S(1)} %get-tuple-element.32), kind=kLoop, calls=%fused_computation | loop fusion | flops 262144 | bytes 1048576 | tf_op jit(solution)/shard_map/broadcast_in_dim | solution.py:628
  28.9 1.5 %collective-permute-done.8.first = bf16[2,32,512]{2,1,0:T(8,128)(2,1)S(1)} collective-permute-done((bf16[2,32,512]{2,1,0:T(8,128)(2,1)S(1)}, bf16[2,32,512]{2,1,0:T(8,128)(2,1)S(1)}, u32[]{:S(2)}, u32[]{:S(2)}) %collective-permute-start.8) | collective-permute-done | bytes 65568 | tf_op jit(solution)/shard_map/ppermute | solution.py:487
  30.4 0.2 shard_map.124.begun
  30.6 1.2 %collective-permute-done.9.refs_0_ = bf16[2,32,512]{2,1,0:T(8,128)(2,1)S(1)} collective-permute-done((bf16[2,32,512]{2,1,0:T(8,128)(2,1)S(1)}, bf16[2,32,512]{2,1,0:T(8,128)(2,1)S(1)}, u32[]{:S(2)}, u32[]{:S(2)}) %collective-permute-start.9) | collective-permute-done | bytes 65568 | tf_op jit(solution)/shard_map/ppermute | solution.py:487
  31.8 1.0 %shard_map.125 = f32[256,512]{1,0:T(8,128)} custom-call(f32[256,512]{1,0:T(8,128)S(1)} %shard_map.124.begun, bf16[256,256]{1,0:T(8,128)(2,1)S(1)} %shard_map.123.collect, bf16[2,32,512]{2,1,0:T(8,128)(2,1)S(1)} %collective-permute-done.9.refs_0_, bf16[2,32,512]{2,1,0:T(8,128)(2,1)S(1)} %collective-permute-done.10.refs_1_), custom_call_target="tpu_custom_call" | custom-call | bytes 1048576 | tf_op jit(solution)/shard_map/pallas_call | solution.py:476
  (8 shorter events, 0.0 us)
Async XLA Ops:
  1.3 9.4 %collective-permute-start.4 = (s32[1,8]{1,0:T(1,128)S(1)}, s32[1,8]{1,0:T(1,128)S(1)}, u32[]{:S(2)}, u32[]{:S(2)}) collective-permute-start(s32[1,8]{1,0:T(1,128)S(1)} %bitcast_add_fusion.code.refs_0_), channel_id=1, source_target_pairs={{0,8},{4,12},{8,0},{12,4},{1,9},{5,13},{9,1},{13,5},{2,10},{6,14},... | collective-permute-start | bytes 104 | tf_op jit(solution)/shard_map/ppermute | solution.py:487
  5.3 3.5 %collective-permute-start.2 = (s32[1,8]{1,0:T(1,128)S(1)}, s32[1,8]{1,0:T(1,128)S(1)}, u32[]{:S(2)}, u32[]{:S(2)}) collective-permute-start(s32[1,8]{1,0:T(1,128)S(1)} %bitcast_add_fusion.code.refs_0_), channel_id=1, source_target_pairs={{0,12},{4,0},{8,4},{12,8},{1,13},{5,1},{9,5},{13,9},{2,14},{6,2},{... | collective-permute-start | bytes 104 | tf_op jit(solution)/shard_map/ppermute | solution.py:487
  6.7 6.3 %collective-permute-start = (s32[1,8]{1,0:T(1,128)S(1)}, s32[1,8]{1,0:T(1,128)S(1)}, u32[]{:S(2)}, u32[]{:S(2)}) collective-permute-start(s32[1,8]{1,0:T(1,128)S(1)} %bitcast_add_fusion.code.refs_0_), channel_id=1, source_target_pairs={{0,4},{4,8},{8,12},{12,0},{1,5},{5,9},{9,13},{13,1},{2,6},{6,10},{... | collective-permute-start | bytes 104 | tf_op jit(solution)/shard_map/ppermute | solution.py:487
  9.0 7.0 %collective-permute-start.3 = (bf16[2,32,512]{2,1,0:T(8,128)(2,1)S(1)}, bf16[2,32,512]{2,1,0:T(8,128)(2,1)S(1)}, u32[]{:S(2)}, u32[]{:S(2)}) collective-permute-start(bf16[2,32,512]{2,1,0:T(8,128)(2,1)S(1)} %shard_map.116), channel_id=1, source_target_pairs={{0,4},{4,8},{8,12},{12,0},{1,5},{5,9},{9,13},{13,1},{2,6},{6,10},{... | collective-permute-start | bytes 196616 | tf_op jit(solution)/shard_map/ppermute | solution.py:487
  10.8 6.1 %collective-permute-start.5 = (bf16[2,32,512]{2,1,0:T(8,128)(2,1)S(1)}, bf16[2,32,512]{2,1,0:T(8,128)(2,1)S(1)}, u32[]{:S(2)}, u32[]{:S(2)}) collective-permute-start(bf16[2,32,512]{2,1,0:T(8,128)(2,1)S(1)} %shard_map.117), channel_id=1, source_target_pairs={{0,8},{4,12},{8,0},{12,4},{1,9},{5,13},{9,1},{13,5},{2,10},{6,14},... | collective-permute-start | bytes 196616 | tf_op jit(solution)/shard_map/ppermute | solution.py:487
  13.2 4.4 %collective-permute-start.1 = (bf16[2,32,512]{2,1,0:T(8,128)(2,1)S(1)}, bf16[2,32,512]{2,1,0:T(8,128)(2,1)S(1)}, u32[]{:S(2)}, u32[]{:S(2)}) collective-permute-start(bf16[2,32,512]{2,1,0:T(8,128)(2,1)S(1)} %shard_map.114.after), channel_id=1, source_target_pairs={{0,12},{4,0},{8,4},{12,8},{1,13},{5,1},{9,5},{13,9},{2,14},{6,2},{... | collective-permute-start | bytes 196616 | tf_op jit(solution)/shard_map/ppermute | solution.py:487
  17.9 1.3 %collective-permute-start.6 = (bf16[256,128]{1,0:T(8,128)(2,1)S(1)}, bf16[256,128]{1,0:T(8,128)(2,1)S(1)}, u32[]{:S(2)}, u32[]{:S(2)}) collective-permute-start(bf16[256,128]{1,0:T(8,128)(2,1)S(1)} %shard_map.119), channel_id=1, source_target_pairs={{0,1},{1,0},{2,3},{3,2},{4,5},{5,4},{6,7},{7,6},{8,9},{9,8},{10,11... | collective-permute-start | bytes 196616 | tf_op jit(solution)/shard_map/ppermute | solution.py:562
  19.2 3.8 %collective-permute-start.7 = (bf16[16,640]{1,0:T(8,128)(2,1)S(1)}, bf16[16,640]{1,0:T(8,128)(2,1)S(1)}, u32[]{:S(2)}, u32[]{:S(2)}) collective-permute-start(bf16[16,640]{1,0:T(8,128)(2,1)S(1)} %shard_map.120), channel_id=1, source_target_pairs={{0,2},{2,0},{1,3},{3,1},{4,6},{6,4},{5,7},{7,5},{8,10},{10,8},{9,1... | collective-permute-start | bytes 61448 | tf_op jit(solution)/shard_map/ppermute | solution.py:574
  20.8 2.3 %copy-start = (bf16[96,64]{1,0:T(8,128)(2,1)S(1)}, bf16[96,64]{1,0:T(8,128)(2,1)}, u32[]{:S(2)}) copy-start(bf16[96,64]{1,0:T(8,128)(2,1)} %constant.10.clone.bands) | copy-start | bytes 36868
  24.0 6.4 %collective-permute-start.8 = (bf16[2,32,512]{2,1,0:T(8,128)(2,1)S(1)}, bf16[2,32,512]{2,1,0:T(8,128)(2,1)S(1)}, u32[]{:S(2)}, u32[]{:S(2)}) collective-permute-start(bf16[2,32,512]{2,1,0:T(8,128)(2,1)S(1)} %get-tuple-element.29), channel_id=1, source_target_pairs={{0,4},{4,8},{8,12},{12,0},{1,5},{5,9},{9,13},{13,1},{2,6},{6,10},{... | collective-permute-start | bytes 196616 | tf_op jit(solution)/shard_map/ppermute | solution.py:487
  24.7 7.1 %collective-permute-start.9 = (bf16[2,32,512]{2,1,0:T(8,128)(2,1)S(1)}, bf16[2,32,512]{2,1,0:T(8,128)(2,1)S(1)}, u32[]{:S(2)}, u32[]{:S(2)}) collective-permute-start(bf16[2,32,512]{2,1,0:T(8,128)(2,1)S(1)} %get-tuple-element.30), channel_id=1, source_target_pairs={{0,8},{4,12},{8,0},{12,4},{1,9},{5,13},{9,1},{13,5},{2,10},{6,14},... | collective-permute-start | bytes 196616 | tf_op jit(solution)/shard_map/ppermute | solution.py:487
  26.9 4.9 %collective-permute-start.10 = (bf16[2,32,512]{2,1,0:T(8,128)(2,1)S(1)}, bf16[2,32,512]{2,1,0:T(8,128)(2,1)S(1)}, u32[]{:S(2)}, u32[]{:S(2)}) collective-permute-start(bf16[2,32,512]{2,1,0:T(8,128)(2,1)S(1)} %get-tuple-element.31), channel_id=1, source_target_pairs={{0,12},{4,0},{8,4},{12,8},{1,13},{5,1},{9,5},{13,9},{2,14},{6,2},{... | collective-permute-start | bytes 196616 | tf_op jit(solution)/shard_map/ppermute | solution.py:487
